TPU v7x, 32 devices: a whole 2x2x4 slice. The times are simulated.
32 devices in a mesh: batch: 16 (over z, x, core), blk: 2 (over y).
Axes of the slice: x: 2, y: 2, z: 4, core: 2. Of those that a mesh axis runs over, the one named last changes fastest.
Arguments:
- hidden_in: bfloat16 [32, 2048, 768], P('batch', 'blk'), may hold values from -6 to 6
- lengths: int32 [32], P('batch'), may hold values from 256 to 2048, as said below
- cot_out: bfloat16 [32, 2048, 768], P('batch', 'blk'), may hold values from -6 to 6
- cot_cls: bfloat16 [32, 768], P('batch'), may hold values from -6 to 6
- w_query: bfloat16 [768, 768], P('batch', 'blk'), may hold values from -0.3125 to 0.3125
- w_key: bfloat16 [768, 768], P('batch', 'blk'), may hold values from -0.3125 to 0.3125
- w_value: bfloat16 [768, 768], P('batch', 'blk'), may hold values from -0.21875 to 0.21875
- w_out: bfloat16 [768, 768], P('batch', 'blk'), may hold values from -0.875 to 0.875
- w_inner: bfloat16 [768, 3072], P('batch', 'blk'), may hold values from -0.21875 to 0.21875
- w_outer: bfloat16 [3072, 768], P('batch', 'blk'), may hold values from -0.109375 to 0.109375
- b_query: bfloat16 [768], P('blk'), may hold values from -1 to 1
- b_value: bfloat16 [768], P('blk'), may hold values from -1 to 1
- b_out: bfloat16 [768], P('blk'), may hold values from -1 to 1
- norm1_gain: bfloat16 [768], P('blk'), may hold values from 0.5 to 1.5
- norm1_shift: bfloat16 [768], P('blk'), may hold values from -1 to 1
- b_inner: bfloat16 [3072], P('blk'), may hold values from -1 to 1
- b_outer: bfloat16 [768], P('blk'), may hold values from -1 to 1
- norm2_gain: bfloat16 [768], P('blk'), may hold values from 0.5 to 1.5
- norm2_shift: bfloat16 [768], P('blk'), may hold values from -1 to 1
Outputs:
- layer_out: bfloat16 [32, 2048, 768], P('batch', 'blk')
- cls_embed: bfloat16 [32, 768], P('batch', 'blk')
- grad_input: float32 [32, 2048, 768], P('batch', 'blk')
- grad_w_query: float32 [768, 768], P('batch', 'blk')
- grad_w_key: float32 [768, 768], P('batch', 'blk')
- grad_w_value: float32 [768, 768], P('batch', 'blk')
- grad_w_out: float32 [768, 768], P('batch', 'blk')
- grad_w_inner: float32 [768, 3072], P('batch', 'blk')
- grad_w_outer: float32 [3072, 768], P('batch', 'blk')
- grad_b_query: float32 [768], P('blk')
- grad_b_value: float32 [768], P('blk')
- grad_b_out: float32 [768], P('blk')
- grad_norm1_gain: float32 [768], P('blk')
- grad_norm1_shift: float32 [768], P('blk')
- grad_b_inner: float32 [3072], P('blk')
- grad_b_outer: float32 [768], P('blk')
- grad_norm2_gain: float32 [768], P('blk')
- grad_norm2_shift: float32 [768], P('blk')
Inputs may be any that keep to these rules, and one draw needn't show every extreme that they name: Passage p has lengths[p] live tokens, its first ones; the others are padding. In every group of 2 passages that share one index of batch, at least one passage is live at all 2048 positions.
All inputs are finite; a program needn't handle non-finite values.
Results may differ from a plain program's by a relative error of at most 0.024.
Values may be sent and summed in bfloat16 or wider, within the bound.
No kernel may reach another device: no remote copies, remote signals or barrier semaphores. Data moves between devices by JAX's collectives and lax.ppermute only.
A program may use at most 640 MiB of HBM per device.

v0:
```python
import jax
import jax.numpy as jnp
from jax import lax
from jax.sharding import PartitionSpec as P

HEADS = 12
HDIM = 64


def passed_along(block, axis, distance):
    devices = range(lax.axis_size(axis))
    route = [((i - distance) % len(devices), i) for i in devices]
    return lax.ppermute(block, axis, route)


def spread_2(shard, axis, root):
    mine = lax.axis_index(axis) == root
    return lax.psum(jnp.where(mine, shard, jnp.zeros_like(shard)), axis)


def layer_norm(values, gain, shift):
    middle = jnp.mean(values, axis=-1, keepdims=True)
    centered = values - middle
    spread = jnp.mean(centered * centered, axis=-1, keepdims=True)
    return centered * lax.rsqrt(spread + 1e-12) * gain + shift


def gelu_exact(values):
    return jax.nn.gelu(values, approximate=False)


def project(rows, weight):
    return jnp.dot(rows, weight, preferred_element_type=jnp.float32)


def project_back(grads, weight):
    return lax.dot_general(
        grads, weight, (((1,), (1,)), ((), ())), preferred_element_type=jnp.float32
    )


def weight_grad(rows, grads):
    return lax.dot_general(
        rows, grads, (((0,), (0,)), ((), ())), preferred_element_type=jnp.float32
    )


def column_sum(grads):
    return jnp.sum(grads.astype(jnp.float32), axis=0)


def on_device(
    hidden_in,
    lengths,
    cot_out,
    cot_cls,
    w_query,
    w_key,
    w_value,
    w_out,
    w_inner,
    w_outer,
    b_query,
    b_value,
    b_out,
    norm1_gain,
    norm1_shift,
    b_inner,
    b_outer,
    norm2_gain,
    norm2_shift,
):
    cycle_size = lax.axis_size("blk")
    cycle_pos = lax.axis_index("blk")
    (
        col_query,
        col_key,
        col_value,
        col_out,
        col_inner,
        col_outer,
        vec_query,
        vec_value,
        vec_out,
        vec_gain_one,
        vec_shift_one,
        vec_inner,
        vec_outer,
        vec_gain_two,
        vec_shift_two,
    ) = (
        lax.all_gather(w_query, "blk", axis=1, tiled=True),
        lax.all_gather(w_key, "blk", axis=1, tiled=True),
        lax.all_gather(w_value, "blk", axis=1, tiled=True),
        lax.all_gather(w_out, "blk", axis=1, tiled=True),
        lax.all_gather(w_inner, "blk", axis=1, tiled=True),
        lax.all_gather(w_outer, "blk", axis=1, tiled=True),
        lax.all_gather(b_query, "blk", axis=0, tiled=True),
        lax.all_gather(b_value, "blk", axis=0, tiled=True),
        lax.all_gather(b_out, "blk", axis=0, tiled=True),
        lax.all_gather(norm1_gain, "blk", axis=0, tiled=True),
        lax.all_gather(norm1_shift, "blk", axis=0, tiled=True),
        lax.all_gather(b_inner, "blk", axis=0, tiled=True),
        lax.all_gather(b_outer, "blk", axis=0, tiled=True),
        lax.all_gather(norm2_gain, "blk", axis=0, tiled=True),
        lax.all_gather(norm2_shift, "blk", axis=0, tiled=True),
    )
    mat_query, mat_key, mat_value, mat_out, mat_inner, mat_outer = (
        lax.all_gather(col_query, "batch", axis=0, tiled=True),
        lax.all_gather(col_key, "batch", axis=0, tiled=True),
        lax.all_gather(col_value, "batch", axis=0, tiled=True),
        lax.all_gather(col_out, "batch", axis=0, tiled=True),
        lax.all_gather(col_inner, "batch", axis=0, tiled=True),
        lax.all_gather(col_outer, "batch", axis=0, tiled=True),
    )
    bias_query = vec_query.astype(jnp.float32)
    bias_value = vec_value.astype(jnp.float32)
    bias_out = vec_out.astype(jnp.float32)
    gain_one = vec_gain_one.astype(jnp.float32)
    shift_one = vec_shift_one.astype(jnp.float32)
    bias_inner = vec_inner.astype(jnp.float32)
    bias_outer = vec_outer.astype(jnp.float32)
    gain_two = vec_gain_two.astype(jnp.float32)
    shift_two = vec_shift_two.astype(jnp.float32)
    groups, block_len, width = hidden_in.shape
    rows = groups * block_len
    head_shape = (groups, block_len, HEADS, HDIM)
    scale = HDIM ** (-0.5)
    hidden = hidden_in.reshape(rows, width)
    hidden_f = hidden.astype(jnp.float32)
    queries = (project(hidden, mat_query) + bias_query).astype(jnp.bfloat16).reshape(head_shape)
    keys = project(hidden, mat_key).astype(jnp.bfloat16).reshape(head_shape)
    values = (project(hidden, mat_value) + bias_value).astype(jnp.bfloat16).reshape(head_shape)
    offsets = jnp.arange(block_len, dtype=jnp.int32)

    def live_keys(step):
        source = (cycle_pos - step) % cycle_size
        return ((source * block_len + offsets)[None, :] < lengths[:, None])[:, None, None, :]

    def block_scores(key_block):
        return (
            jnp.einsum("sqhd,skhd->shqk", queries, key_block, preferred_element_type=jnp.float32)
            * scale
        )

    running_max = jnp.full((groups, HEADS, block_len), -1e30, jnp.float32)
    running_sum = jnp.zeros((groups, HEADS, block_len), jnp.float32)
    running_acc = jnp.zeros(head_shape, jnp.float32)
    visit_keys, visit_values = (keys, values)
    for step in range(cycle_size):
        if step > 0:
            visit_keys, visit_values = passed_along((visit_keys, visit_values), "blk", 1)
        live = live_keys(step)
        masked = jnp.where(live, block_scores(visit_keys), -1e30)
        new_max = jnp.maximum(running_max, jnp.max(masked, axis=-1))
        weights = jnp.where(live, jnp.exp(masked - new_max[..., None]), 0.0)
        factor = jnp.exp(running_max - new_max)
        running_sum = running_sum * factor + jnp.sum(weights, axis=-1)
        running_acc = running_acc * jnp.transpose(factor, (0, 2, 1))[..., None] + jnp.einsum(
            "shqk,skhd->sqhd",
            weights.astype(jnp.bfloat16),
            visit_values,
            preferred_element_type=jnp.float32,
        )
        running_max = new_max
    context = running_acc / jnp.transpose(running_sum, (0, 2, 1))[..., None]
    log_total = running_max + jnp.log(running_sum)
    context_low = context.reshape(rows, width).astype(jnp.bfloat16)
    attn_out = project(context_low, mat_out) + bias_out
    resid_one = hidden_f + attn_out
    normed = layer_norm(resid_one, gain_one, shift_one)
    normed_low = normed.astype(jnp.bfloat16)
    inner = project(normed_low, mat_inner) + bias_inner
    active_low = gelu_exact(inner).astype(jnp.bfloat16)
    outer = project(active_low, mat_outer) + bias_outer
    resid_two = normed + outer
    result = layer_norm(resid_two, gain_two, shift_two)
    layer_out = result.astype(jnp.bfloat16).reshape(groups, block_len, width)
    first_rows = layer_out[:, 0, :]
    everywhere = spread_2(first_rows, "blk", 0)
    share = width // cycle_size
    cls_part = lax.dynamic_slice_in_dim(everywhere, cycle_pos * share, share, 1)
    owner = (cycle_pos == 0).astype(jnp.float32)
    cot_rows = cot_out.astype(jnp.float32).at[:, 0, :].add(owner * cot_cls.astype(jnp.float32))
    cot_rows = cot_rows.reshape(rows, width)
    unused_two, norm_two_back = jax.vjp(layer_norm, resid_two, gain_two, shift_two)
    grad_resid_two, grad_gain_two, grad_shift_two = norm_two_back(cot_rows)
    grad_outer = grad_resid_two.astype(jnp.bfloat16)
    grad_bias_outer = column_sum(grad_outer)
    grad_mat_outer = weight_grad(active_low, grad_outer)
    grad_active = project_back(grad_outer, mat_outer)
    unused_gelu, gelu_back = jax.vjp(gelu_exact, inner)
    grad_inner = gelu_back(grad_active)[0].astype(jnp.bfloat16)
    grad_bias_inner = column_sum(grad_inner)
    grad_mat_inner = weight_grad(normed_low, grad_inner)
    grad_normed = grad_resid_two + project_back(grad_inner, mat_inner)
    unused_one, norm_one_back = jax.vjp(layer_norm, resid_one, gain_one, shift_one)
    grad_resid_one, grad_gain_one, grad_shift_one = norm_one_back(grad_normed)
    grad_attn = grad_resid_one.astype(jnp.bfloat16)
    grad_bias_out = column_sum(grad_attn)
    grad_mat_out = weight_grad(context_low, grad_attn)
    grad_context = project_back(grad_attn, mat_out).astype(jnp.bfloat16).reshape(head_shape)
    delta = jnp.einsum("sqhd,sqhd->shq", grad_context.astype(jnp.float32), context)
    grad_queries = jnp.zeros(head_shape, jnp.float32)
    carry_keys = jnp.zeros(head_shape, jnp.float32)
    carry_values = jnp.zeros(head_shape, jnp.float32)
    visit_keys, visit_values = (keys, values)
    for step in range(cycle_size):
        if step > 0:
            visit_keys, visit_values = passed_along((visit_keys, visit_values), "blk", 1)
        live = live_keys(step)
        probs_now = jnp.where(live, jnp.exp(block_scores(visit_keys) - log_total[..., None]), 0.0)
        grad_probs = jnp.einsum(
            "sqhd,skhd->shqk", grad_context, visit_values, preferred_element_type=jnp.float32
        )
        grad_scores = (probs_now * (grad_probs - delta[..., None])).astype(jnp.bfloat16)
        grad_queries = grad_queries + scale * jnp.einsum(
            "shqk,skhd->sqhd", grad_scores, visit_keys, preferred_element_type=jnp.float32
        )
        carry_keys = carry_keys + scale * jnp.einsum(
            "shqk,sqhd->skhd", grad_scores, queries, preferred_element_type=jnp.float32
        )
        carry_values = carry_values + jnp.einsum(
            "shqk,sqhd->skhd",
            probs_now.astype(jnp.bfloat16),
            grad_context,
            preferred_element_type=jnp.float32,
        )
        carry_keys, carry_values = (
            passed_along(carry_keys.astype(jnp.bfloat16), "blk", 1).astype(carry_keys.dtype),
            passed_along(carry_values.astype(jnp.bfloat16), "blk", 1).astype(carry_values.dtype),
        )
    grad_query_low = grad_queries.reshape(rows, width).astype(jnp.bfloat16)
    grad_key_low = carry_keys.reshape(rows, width).astype(jnp.bfloat16)
    grad_value_low = carry_values.reshape(rows, width).astype(jnp.bfloat16)
    grad_bias_query = column_sum(grad_query_low)
    grad_bias_value = column_sum(grad_value_low)
    grad_mat_query = weight_grad(hidden, grad_query_low)
    grad_mat_key = weight_grad(hidden, grad_key_low)
    grad_mat_value = weight_grad(hidden, grad_value_low)
    grad_hidden = (
        grad_resid_one
        + project_back(grad_query_low, mat_query)
        + project_back(grad_key_low, mat_key)
        + project_back(grad_value_low, mat_value)
    )
    grad_input = grad_hidden.reshape(groups, block_len, width)
    sum_query, sum_key, sum_value, sum_out, sum_inner, sum_outer = (
        lax.psum_scatter(
            grad_mat_query.astype(jnp.bfloat16), "batch", scatter_dimension=0, tiled=True
        ).astype(jnp.float32),
        lax.psum_scatter(
            grad_mat_key.astype(jnp.bfloat16), "batch", scatter_dimension=0, tiled=True
        ).astype(jnp.float32),
        lax.psum_scatter(
            grad_mat_value.astype(jnp.bfloat16), "batch", scatter_dimension=0, tiled=True
        ).astype(jnp.float32),
        lax.psum_scatter(
            grad_mat_out.astype(jnp.bfloat16), "batch", scatter_dimension=0, tiled=True
        ).astype(jnp.float32),
        lax.psum_scatter(
            grad_mat_inner.astype(jnp.bfloat16), "batch", scatter_dimension=0, tiled=True
        ).astype(jnp.float32),
        lax.psum_scatter(
            grad_mat_outer.astype(jnp.bfloat16), "batch", scatter_dimension=0, tiled=True
        ).astype(jnp.float32),
    )
    (
        total_query,
        total_value,
        total_out,
        total_gain_one,
        total_shift_one,
        total_inner,
        total_outer,
        total_gain_two,
        total_shift_two,
    ) = (
        lax.psum(grad_bias_query.astype(jnp.bfloat16), "batch").astype(jnp.float32),
        lax.psum(grad_bias_value.astype(jnp.bfloat16), "batch").astype(jnp.float32),
        lax.psum(grad_bias_out.astype(jnp.bfloat16), "batch").astype(jnp.float32),
        lax.psum(grad_gain_one.astype(jnp.bfloat16), "batch").astype(jnp.float32),
        lax.psum(grad_shift_one.astype(jnp.bfloat16), "batch").astype(jnp.float32),
        lax.psum(grad_bias_inner.astype(jnp.bfloat16), "batch").astype(jnp.float32),
        lax.psum(grad_bias_outer.astype(jnp.bfloat16), "batch").astype(jnp.float32),
        lax.psum(grad_gain_two.astype(jnp.bfloat16), "batch").astype(jnp.float32),
        lax.psum(grad_shift_two.astype(jnp.bfloat16), "batch").astype(jnp.float32),
    )
    (
        part_wq,
        part_wk,
        part_wv,
        part_wo,
        part_wi,
        part_wu,
        part_bq,
        part_bv,
        part_bo,
        part_g1,
        part_s1,
        part_bi,
        part_bu,
        part_g2,
        part_s2,
    ) = (
        lax.psum_scatter(
            sum_query.astype(jnp.bfloat16), "blk", scatter_dimension=1, tiled=True
        ).astype(jnp.float32),
        lax.psum_scatter(
            sum_key.astype(jnp.bfloat16), "blk", scatter_dimension=1, tiled=True
        ).astype(jnp.float32),
        lax.psum_scatter(
            sum_value.astype(jnp.bfloat16), "blk", scatter_dimension=1, tiled=True
        ).astype(jnp.float32),
        lax.psum_scatter(
            sum_out.astype(jnp.bfloat16), "blk", scatter_dimension=1, tiled=True
        ).astype(jnp.float32),
        lax.psum_scatter(
            sum_inner.astype(jnp.bfloat16), "blk", scatter_dimension=1, tiled=True
        ).astype(jnp.float32),
        lax.psum_scatter(
            sum_outer.astype(jnp.bfloat16), "blk", scatter_dimension=1, tiled=True
        ).astype(jnp.float32),
        lax.psum_scatter(
            total_query.astype(jnp.bfloat16), "blk", scatter_dimension=0, tiled=True
        ).astype(jnp.float32),
        lax.psum_scatter(
            total_value.astype(jnp.bfloat16), "blk", scatter_dimension=0, tiled=True
        ).astype(jnp.float32),
        lax.psum_scatter(
            total_out.astype(jnp.bfloat16), "blk", scatter_dimension=0, tiled=True
        ).astype(jnp.float32),
        lax.psum_scatter(
            total_gain_one.astype(jnp.bfloat16), "blk", scatter_dimension=0, tiled=True
        ).astype(jnp.float32),
        lax.psum_scatter(
            total_shift_one.astype(jnp.bfloat16), "blk", scatter_dimension=0, tiled=True
        ).astype(jnp.float32),
        lax.psum_scatter(
            total_inner.astype(jnp.bfloat16), "blk", scatter_dimension=0, tiled=True
        ).astype(jnp.float32),
        lax.psum_scatter(
            total_outer.astype(jnp.bfloat16), "blk", scatter_dimension=0, tiled=True
        ).astype(jnp.float32),
        lax.psum_scatter(
            total_gain_two.astype(jnp.bfloat16), "blk", scatter_dimension=0, tiled=True
        ).astype(jnp.float32),
        lax.psum_scatter(
            total_shift_two.astype(jnp.bfloat16), "blk", scatter_dimension=0, tiled=True
        ).astype(jnp.float32),
    )
    return (
        layer_out,
        cls_part,
        grad_input,
        part_wq,
        part_wk,
        part_wv,
        part_wo,
        part_wi,
        part_wu,
        part_bq,
        part_bv,
        part_bo,
        part_g1,
        part_s1,
        part_bi,
        part_bu,
        part_g2,
        part_s2,
    )


def solution(mesh):
    placed = (
        P("batch", "blk", None),
        P("batch"),
        P("batch", "blk", None),
        P("batch", None),
        P("batch", "blk"),
        P("batch", "blk"),
        P("batch", "blk"),
        P("batch", "blk"),
        P("batch", "blk"),
        P("batch", "blk"),
        P("blk"),
        P("blk"),
        P("blk"),
        P("blk"),
        P("blk"),
        P("blk"),
        P("blk"),
        P("blk"),
        P("blk"),
    )
    return jax.shard_map(
        on_device,
        mesh=mesh,
        in_specs=placed,
        out_specs=(
            P("batch", "blk", None),
            P("batch", "blk"),
            P("batch", "blk", None),
            P("batch", "blk"),
            P("batch", "blk"),
            P("batch", "blk"),
            P("batch", "blk"),
            P("batch", "blk"),
            P("batch", "blk"),
            P("blk"),
            P("blk"),
            P("blk"),
            P("blk"),
            P("blk"),
            P("blk"),
            P("blk"),
            P("blk"),
            P("blk"),
        ),
        check_vma=False,
    )
```

profile of v0, /device:TPU:0, one launch (start us, length us, event | category | flops | bytes accessed | tf_op | source)
XLA Modules:
  0.0 1272.2 jit_solution(6270724561001052892)
XLA Ops:
  7.2 7.2 all_gather.68
  30.3 7.3 all_gather.76
  158.9 36.6 %select_reduce_fusion.1 = (f32[2,12,1024]{2,1,0:T(8,128)S(1)}, f32[2,12,1024,1024]{2,3,1,0:T(8,128)}) fusion(pred[2,1024]{1,0:T(4,128)(4,1)S(1)} %get-tuple-element.125, bf16[2,1024,12,64]{1,0,3,2:T(2,128)(2,1)} %reshape.262, bf16[2,1024,12,64]{1,0,3,2:T(2,128)(2,1)S(1)} %reshape.261), kind=kOutput, calls=%fused_computation.7 | convolution fusion | flops 3296698368 | bytes 107055104 | tf_op jit(solution)/shard_map/sqhd,skhd->shqk/dot_general | solution.py:142
  195.5 32.8 %collective-permute-done = bf16[2,1024,12,64]{1,3,2,0:T(8,128)(2,1)} collective-permute-done((bf16[2,1024,12,64]{1,3,2,0:T(8,128)(2,1)}, bf16[2,1024,12,64]{1,3,2,0:T(8,128)(2,1)}, u32[]{:S(2)}, u32[]{:S(2)}) %collective-permute-start) | collective-permute-done | bytes 3145760 | tf_op jit(solution)/shard_map/ppermute | solution.py:13
  228.3 36.6 %select_reduce_fusion = (f32[2,12,1024]{2,1,0:T(8,128)S(1)}, f32[2,12,1024,1024]{2,3,1,0:T(8,128)}) fusion(pred[2,1024]{1,0:T(4,128)(4,1)S(1)} %get-tuple-element.124, bf16[2,1024,12,64]{1,3,2,0:T(8,128)(2,1)} %collective-permute-done, bf16[2,1024,12,64]{1,0,3,2:T(2,128)(2,1)S(1)} %reshape.261), kind=kOutput, calls=%fused_computation.6 | convolution fusion | flops 3296698368 | bytes 107055104 | tf_op jit(solution)/shard_map/sqhd,skhd->shqk/dot_general | solution.py:142
  264.9 62.4 %fusion.2 = (f32[2,12,1024]{2,1,0:T(8,128)S(1)}, f32[2,12,1024]{2,1,0:T(8,128)S(1)}) fusion(f32[2,12,1024,1024]{2,3,1,0:T(8,128)} %get-tuple-element.129, f32[2,12,1024]{2,1,0:T(8,128)S(1)} %get-tuple-element.123, pred[2,1024]{1,0:T(4,128)(4,1)S(1)} %get-tuple-element.125, f32[2,12,1024]{2,1,0:T(8,128)S(1)} %get-tuple-element.122, ...), kind=kLoop, calls=%fused_computation.10 | loop fusion | flops 251609088 | bytes 201723904 | tf_op jit(solution)/shard_map/reduce_sum | solution.py:158
  328.8 38.4 %fusion.12 = f32[2,12,64,1024]{3,2,1,0:T(8,128)} fusion(f32[2,12,1024,1024]{2,3,1,0:T(8,128)} %get-tuple-element.129, f32[2,12,1024]{2,1,0:T(8,128)S(1)} %get-tuple-element.123, pred[2,1024]{1,0:T(4,128)(4,1)S(1)} %get-tuple-element.125, bf16[2,1024,12,64]{1,0,3,2:T(2,128)(2,1)S(1)} %copy-done.7), kind=kOutput, calls=%fused_computation.17 | convolution fusion | flops 3347054592 | bytes 110200832 | tf_op jit(solution)/shard_map/shqk,skhd->sqhd/dot_general | solution.py:159
  367.3 39.9 %fusion.83 = (bf16[2,1024,12,64]{1,3,2,0:T(8,128)(2,1)S(1)}, f32[2,1024,12,64]{1,3,2,0:T(8,128)}) fusion(f32[2,1024,12]{1,2,0:T(8,128)S(1)} %copy-done.20, bf16[2,1024,12,64]{1,3,2,0:T(8,128)(2,1)} %collective-permute-done.1, f32[2,12,1024,1024]{2,3,1,0:T(8,128)} %get-tuple-element.127, f32[2,12,1024]{2,1,0:T(8,128)S(1)} %get-tuple-element.122, ...), kind=kOutput, calls=%fused_computation.155 | convolution fusion | flops 3354918912 | bytes 119932928 | tf_op jit(solution)/shard_map/shqk,skhd->sqhd/dot_general | solution.py:159
  422.3 70.5 %multiply_convert_fusion.2 = (bf16[2048,3072]{1,0:T(8,128)(2,1)}, f32[2048,3072]{1,0:T(8,128)}, f32[2048,3072]{1,0:T(8,128)}) fusion(f32[3072]{0:T(1024)S(1)} %bitcast.175, bf16[768,3072]{1,0:T(8,128)(2,1)} %all-gather.24.cloned.1.call-done, f32[2048,768]{1,0:T(8,128)} %copy-done.5, f32[768]{0:T(1024)S(1)} %copy-done.39, f32[768]{0:T(1024)S(1)} %copy-done.32, ...), kind=kOutput, calls=%fused_computation.25 | convolution fusion | flops 10086776832 | bytes 73959424 | tf_op jit(solution)/shard_map/dot_general | solution.py:33
  492.8 16.5 %fusion.85 = (f32[2048]{0:T(1024)S(1)}, f32[2048,768]{1,0:T(8,128)S(1)}) fusion(f32[768]{0:T(1024)S(1)} %copy-done.42, bf16[2048,3072]{1,0:T(8,128)(2,1)} %get-tuple-element.116, bf16[3072,768]{1,0:T(8,128)(2,1)} %all-gather.26.cloned.1.call-done, f32[768]{0:T(1024)S(1)} %copy-done.39, f32[768]{0:T(1024)S(1)} %copy-done.32, f32[2048]{0:T(1024)S(1)} %fusion.55, ...), kind=kOutput, calls=%fused_computation.157 | convolution fusion | flops 9674684416 | bytes 29918208 | tf_op jit(solution)/shard_map/dot_general | solution.py:33
  521.9 29.1 %fusion.87 = (bf16[3072]{0:T(1024)(128)(2,1)}, bf16[2048,3072]{1,0:T(8,128)(2,1)}) fusion(f32[2048,3072]{1,0:T(8,128)} %get-tuple-element.117, bf16[2048,768]{1,0:T(8,128)(2,1)S(1)} %get-tuple-element.109, bf16[3072,768]{1,0:T(8,128)(2,1)} %all-gather.26.cloned.1.call-done, f32[2048,3072]{1,0:T(8,128)} %get-tuple-element.134, f32[3072]{0:T(1024)S(1)} %bitcast.176), kind=kOutput, calls=%fused_computation.159 | convolution fusion | flops 9764336640 | bytes 70797312 | tf_op jit(solution)/shard_map/dot_general | solution.py:37
  551.0 19.3 %multiply_reduce_fusion.1 = (bf16[768]{0:T(1024)(128)(2,1)}, f32[2048]{0:T(1024)S(1)}, bf16[768]{0:T(1024)(128)(2,1)}, f32[2048,768]{1,0:T(8,128)S(1)}) fusion(f32[2048,768]{1,0:T(8,128)} %copy-done.5, f32[2048]{0:T(1024)S(1)} %fusion.55, f32[2048]{0:T(1024)S(1)} %broadcast_multiply_fusion.1, f32[768]{0:T(1024)S(1)} %copy-done.32, ...), kind=kOutput, calls=%fused_computation.53 | convolution fusion | flops 9679400960 | bytes 36214784 | tf_op jit(solution)/shard_map/dot_general | solution.py:37
  605.2 59.0 %multiply_convert_fusion.1 = bf16[2,12,1024,1024]{2,3,1,0:T(8,128)(2,1)} fusion(f32[2,12,1024,1024]{2,3,1,0:T(8,128)} %get-tuple-element.129, f32[2,12,1024]{2,1,0:T(8,128)S(1)} %multiply_reduce_fusion, f32[2,12,1024]{2,1,0:T(8,128)S(1)} %copy-done.18, pred[2,1024]{1,0:T(4,128)(4,1)S(1)} %copy-done.17, bf16[2,1024,12,64]{1,0,3,2:T(2,128)(2,1)} %reshape.267, ...), kind=kOutput, calls=%fused_computation.2 | convolution fusion | flops 3372220416 | bytes 157485056 | tf_op jit(solution)/shard_map/sqhd,skhd->shqk/dot_general | solution.py:213
  664.2 21.0 %fusion.72 = f32[2,12,64,1024]{3,2,1,0:T(8,128)} fusion(bf16[2,12,1024,1024]{2,3,1,0:T(8,128)(2,1)} %multiply_convert_fusion.1, bf16[2,1024,12,64]{1,0,3,2:T(2,128)(2,1)S(1)} %copy-done.4), kind=kOutput, calls=%fused_computation.147 | convolution fusion | flops 3221225472 | bytes 59768832 | tf_op jit(solution)/shard_map/shqk,skhd->sqhd/dot_general | solution.py:217
  685.3 57.8 %multiply_convert_fusion = bf16[2,12,1024,1024]{2,3,1,0:T(8,128)(2,1)} fusion(f32[2,12,1024,1024]{2,3,1,0:T(8,128)} %get-tuple-element.127, f32[2,12,1024]{2,1,0:T(8,128)S(1)} %multiply_reduce_fusion, f32[2,12,1024]{2,1,0:T(8,128)S(1)} %copy-done.18, pred[2,1024]{1,0:T(4,128)(4,1)S(1)} %copy-done.15, bf16[2,1024,12,64]{1,3,2,0:T(8,128)(2,1)} %collective-permute-done.1, ...), kind=kOutput, calls=%fused_computation | convolution fusion | flops 3372220416 | bytes 157485056 | tf_op jit(solution)/shard_map/sqhd,skhd->shqk/dot_general | solution.py:213
  743.1 21.3 %fusion.86 = (bf16[12,64]{1,0:T(8,128)(2,1)}, bf16[2,1024,12,64]{1,3,2,0:T(8,128)(2,1)S(1)}) fusion(f32[2,12,64,1024]{3,2,1,0:T(8,128)} %fusion.72, bf16[2,1024,12,64]{1,3,2,0:T(8,128)(2,1)} %collective-permute-done, bf16[2,12,1024,1024]{2,3,1,0:T(8,128)(2,1)} %multiply_convert_fusion), kind=kOutput, calls=%fused_computation.158 | convolution fusion | flops 3227516160 | bytes 62916096 | tf_op jit(solution)/shard_map/shqk,skhd->sqhd/dot_general | solution.py:217
  776.4 14.6 %convolution_convert_fusion = bf16[3072,768]{1,0:T(8,128)(2,1)} fusion(bf16[2048,3072]{1,0:T(8,128)(2,1)} %get-tuple-element.116, bf16[2048,768]{1,0:T(8,128)(2,1)S(1)} %copy-done.13), kind=kOutput, calls=%fused_computation.71 | convolution fusion | flops 9666035712 | bytes 20447232 | tf_op jit(solution)/shard_map/dot_general | solution.py:43
  791.0 37.0 %convert_bitcast_fusion = bf16[2,1024,12,64]{1,3,2,0:T(8,128)(2,1)} fusion(f32[2,12,1024,1024]{2,3,1,0:T(8,128)} %get-tuple-element.129, f32[2,12,1024]{2,1,0:T(8,128)S(1)} %copy-done.18, pred[2,1024]{1,0:T(4,128)(4,1)S(1)} %copy-done.17, bf16[2,1024,12,64]{1,0,3,2:T(2,128)(2,1)} %reshape.267), kind=kOutput, calls=%fused_computation.79 | convolution fusion | flops 3323461632 | bytes 107055104 | tf_op jit(solution)/shard_map/shqk,sqhd->skhd/dot_general | solution.py:223
  829.8 24.2 %fusion.31 = bf16[2,1024,12,64]{1,3,2,0:T(8,128)(2,1)} fusion(bf16[2,12,1024,1024]{2,3,1,0:T(8,128)(2,1)} %multiply_convert_fusion.1, bf16[2,1024,12,64]{1,0,3,2:T(2,128)(2,1)S(1)} %copy-done.1), kind=kOutput, calls=%fused_computation.76 | convolution fusion | flops 3224371200 | bytes 56623104 | tf_op jit(solution)/shard_map/shqk,sqhd->skhd/dot_general | solution.py:220
  854.1 18.5 %convolution_convert_fusion.1 = bf16[768,3072]{1,0:T(8,128)(2,1)} fusion(bf16[2048,3072]{1,0:T(8,128)(2,1)} %get-tuple-element.141, f32[2048,768]{1,0:T(8,128)} %copy-done.5, f32[768]{0:T(1024)S(1)} %copy-done.40, f32[768]{0:T(1024)S(1)} %copy-done.33, f32[2048]{0:T(1024)S(1)} %copy-done.29, f32[2048]{0:T(1024)S(1)} %copy-done.22), kind=kOutput, calls=%fused_computation.72 | convolution fusion | flops 9673900032 | bytes 23615488 | tf_op jit(solution)/shard_map/dot_general | solution.py:43
  872.7 26.8 %collective-permute-done.4 = bf16[2,1024,12,64]{1,3,2,0:T(8,128)(2,1)} collective-permute-done((bf16[2,1024,12,64]{1,3,2,0:T(8,128)(2,1)}, bf16[2,1024,12,64]{1,3,2,0:T(8,128)(2,1)}, u32[]{:S(2)}, u32[]{:S(2)}) %collective-permute-start.4) | collective-permute-done | bytes 3145760 | tf_op jit(solution)/shard_map/ppermute | solution.py:13
  899.5 38.6 %fusion.24 = bf16[2,1024,12,64]{1,3,2,0:T(8,128)(2,1)} fusion(bf16[2,1024,12,64]{1,3,2,0:T(8,128)(2,1)} %collective-permute-done.4, f32[2,12,1024,1024]{2,3,1,0:T(8,128)} %get-tuple-element.127, f32[2,12,1024]{2,1,0:T(8,128)S(1)} %copy-done.18, pred[2,1024]{1,0:T(4,128)(4,1)S(1)} %copy-done.15, bf16[2,1024,12,64]{1,0,3,2:T(2,128)(2,1)} %reshape.267), kind=kOutput, calls=%fused_computation.42 | convolution fusion | flops 3326607360 | bytes 110200832 | tf_op jit(solution)/shard_map/shqk,sqhd->skhd/dot_general | solution.py:223
  939.8 27.2 %collective-permute-done.2 = bf16[2,1024,12,64]{1,3,2,0:T(8,128)(2,1)} collective-permute-done((bf16[2,1024,12,64]{1,3,2,0:T(8,128)(2,1)}, bf16[2,1024,12,64]{1,3,2,0:T(8,128)(2,1)}, u32[]{:S(2)}, u32[]{:S(2)}) %collective-permute-start.2) | collective-permute-done | bytes 3145760 | tf_op jit(solution)/shard_map/ppermute | solution.py:13
  966.9 24.1 %fusion.25 = bf16[2,1024,12,64]{1,3,2,0:T(8,128)(2,1)} fusion(bf16[2,1024,12,64]{1,3,2,0:T(8,128)(2,1)} %collective-permute-done.2, bf16[2,12,1024,1024]{2,3,1,0:T(8,128)(2,1)} %multiply_convert_fusion, bf16[2,1024,12,64]{1,0,3,2:T(2,128)(2,1)S(1)} %copy-done.1), kind=kOutput, calls=%fused_computation.44 | convolution fusion | flops 3227516928 | bytes 59768832 | tf_op jit(solution)/shard_map/shqk,sqhd->skhd/dot_general | solution.py:220
  996.3 42.2 %collective-permute-done.5 = bf16[2,1024,12,64]{1,3,2,0:T(8,128)(2,1)} collective-permute-done((bf16[2,1024,12,64]{1,3,2,0:T(8,128)(2,1)}, bf16[2,1024,12,64]{1,3,2,0:T(8,128)(2,1)}, u32[]{:S(2)}, u32[]{:S(2)}) %collective-permute-start.5) | collective-permute-done | bytes 3145760 | tf_op jit(solution)/shard_map/ppermute | solution.py:13
  1051.1 47.8 %collective-permute-done.3 = bf16[2,1024,12,64]{1,3,2,0:T(8,128)(2,1)} collective-permute-done((bf16[2,1024,12,64]{1,3,2,0:T(8,128)(2,1)}, bf16[2,1024,12,64]{1,3,2,0:T(8,128)(2,1)}, u32[]{:S(2)}, u32[]{:S(2)}) %collective-permute-start.3) | collective-permute-done | bytes 3145760 | tf_op jit(solution)/shard_map/ppermute | solution.py:13
  1122.3 7.6 fusion.88
  1135.3 7.6 fusion.89
  1142.9 28.0 %reduce-scatter.39.cloned.1.call-done = bf16[48,768]{1,0:T(8,128)(2,1)} async-done(((bf16[768,768]{1,0:T(8,128)(2,1)}), bf16[48,768]{1,0:T(8,128)(2,1)}) %reduce-scatter.39.cloned.1.call-update) | async-done | bytes 73744
  1172.7 10.5 add_add_fusion.2
  1185.8 8.3 all-reduce.10
  1194.8 57.7 %all-reduce.9 = (bf16[384]{0:T(512)(128)(2,1)S(1)}, bf16[384]{0:T(512)(128)(2,1)S(1)}, bf16[384]{0:T(512)(128)(2,1)S(1)}, bf16[384]{0:T(512)(128)(2,1)S(1)}, bf1...) all-reduce(bf16[384]{0:T(512)(128)(2,1)S(1)} %dynamic-slice.9, ...), channel_id=1, replica_groups=mesh['batch'=16,'blk'=2] {'batch'}, use_global_device_ids=true, to_apply=%region_26.27 | all-reduce | flops 4608 | bytes 18432 | tf_op jit(solution)/shard_map/psum | solution.py:279
  (303 shorter events, 278.8 us)
Async XLA Ops:
  7.2 91.4 %copy-start.43 = (bf16[2,768]{1,0:T(2,128)(2,1)S(1)}, bf16[2,768]{1,0:T(2,128)(2,1)}, u32[]{:S(2)}) copy-start(bf16[2,768]{1,0:T(2,128)(2,1)} %param.24) | copy-start | bytes 9220
  7.2 96.7 %all-gather.20.cloned.1.call-start = ((), (), s32[]{:S(2)}) async-start(), calls=%async_computation.14 | async-start | bytes 1253376 | tf_op jit(solution)/shard_map/all_gather | solution.py:111
  14.5 102.1 %all-gather.16.cloned.1.call-start = ((), (), s32[]{:S(2)}) async-start(), calls=%async_computation.12 | async-start | bytes 1253376 | tf_op jit(solution)/shard_map/all_gather | solution.py:109
  19.5 115.4 %all-gather.18.cloned.1.call-start = ((), (), s32[]{:S(2)}) async-start(), calls=%async_computation.13 | async-start | bytes 1253376 | tf_op jit(solution)/shard_map/all_gather | solution.py:110
  25.2 386.3 %all-gather.22.cloned.1.call-start = ((), (), s32[]{:S(2)}) async-start(), calls=%async_computation.15 | async-start | bytes 1253376 | tf_op jit(solution)/shard_map/all_gather | solution.py:112
  30.3 392.0 %all-gather.24.cloned.1.call-start = ((), (), s32[]{:S(2)}) async-start(), calls=%async_computation.16 | async-start | bytes 5013504 | tf_op jit(solution)/shard_map/all_gather | solution.py:113
  37.6 455.1 %all-gather.26.cloned.1.call-start = ((), (), s32[]{:S(2)}) async-start(), calls=%async_computation.17 | async-start | bytes 5013504 | tf_op jit(solution)/shard_map/all_gather | solution.py:114
  43.9 948.9 %reduce-scatter.29.cloned.1.call-start = ((), (), s32[]{:S(2)}) async-start(), calls=%async_computation.21 | async-start | bytes 1253376 | tf_op jit(solution)/shard_map/reduce_scatter | solution.py:258
  103.9 225.0 %copy-start.16 = (pred[2,1024]{1,0:T(4,128)(4,1)}, pred[2,1024]{1,0:T(4,128)(4,1)S(1)}, u32[]{:S(2)}) copy-start(pred[2,1024]{1,0:T(4,128)(4,1)S(1)} %get-tuple-element.125) | copy-start | bytes 6148
  103.9 263.4 %copy-start.14 = (pred[2,1024]{1,0:T(4,128)(4,1)}, pred[2,1024]{1,0:T(4,128)(4,1)S(1)}, u32[]{:S(2)}) copy-start(pred[2,1024]{1,0:T(4,128)(4,1)S(1)} %get-tuple-element.124) | copy-start | bytes 6148
  129.2 99.1 %copy-start = (bf16[2,1024,12,64]{1,0,3,2:T(2,128)(2,1)}, bf16[2,1024,12,64]{1,0,3,2:T(2,128)(2,1)S(1)}, u32[]{:S(2)}) copy-start(bf16[2,1024,12,64]{1,0,3,2:T(2,128)(2,1)S(1)} %reshape.261) | copy-start | bytes 9437188
  156.9 71.4 %collective-permute-start = (bf16[2,1024,12,64]{1,3,2,0:T(8,128)(2,1)}, bf16[2,1024,12,64]{1,3,2,0:T(8,128)(2,1)}, u32[]{:S(2)}, u32[]{:S(2)}) collective-permute-start(bf16[2,1024,12,64]{1,3,2,0:T(8,128)(2,1)} %copy.108), channel_id=1, source_target_pairs={{1,0},{0,1},{3,2},{2,3},{5,4},{4,5},{7,6},{6,7},{9,8},{8,9},{11,10... | collective-permute-start | bytes 9437192 | tf_op jit(solution)/shard_map/ppermute | solution.py:13
  158.6 208.7 %collective-permute-start.1 = (bf16[2,1024,12,64]{1,3,2,0:T(8,128)(2,1)}, bf16[2,1024,12,64]{1,3,2,0:T(8,128)(2,1)}, u32[]{:S(2)}, u32[]{:S(2)}) collective-permute-start(bf16[2,1024,12,64]{1,3,2,0:T(8,128)(2,1)} %copy.110), channel_id=1, source_target_pairs={{1,0},{0,1},{3,2},{2,3},{5,4},{4,5},{7,6},{6,7},{9,8},{8,9},{11,10... | collective-permute-start | bytes 9437192 | tf_op jit(solution)/shard_map/ppermute | solution.py:13
  264.9 63.9 %copy-start.7 = (bf16[2,1024,12,64]{1,0,3,2:T(2,128)(2,1)S(1)}, bf16[2,1024,12,64]{1,0,3,2:T(2,128)(2,1)}, u32[]{:S(2)}) copy-start(bf16[2,1024,12,64]{1,0,3,2:T(2,128)(2,1)} %reshape.263) | copy-start | bytes 9437188
  418.2 152.2 %copy-start.21 = (f32[2048]{0:T(1024)}, f32[2048]{0:T(1024)S(1)}, u32[]{:S(2)}) copy-start(f32[2048]{0:T(1024)S(1)} %broadcast_multiply_fusion.1) | copy-start | bytes 24580
  422.2 148.2 %copy-start.28 = (f32[2048]{0:T(1024)}, f32[2048]{0:T(1024)S(1)}, u32[]{:S(2)}) copy-start(f32[2048]{0:T(1024)S(1)} %fusion.55) | copy-start | bytes 24580
  422.3 70.5 %copy-start.42 = (f32[768]{0:T(1024)S(1)}, f32[768]{0:T(1024)}, u32[]{:S(2)}) copy-start(f32[768]{0:T(1024)} %reshape.293) | copy-start | bytes 9220
  582.7 411.9 %reduce-scatter.37.cloned.1.call-start = ((), (), s32[]{:S(2)}) async-start(), calls=%async_computation.25 | async-start | bytes 1253376
  776.3 336.6 %reduce-scatter.35.cloned.1.call-start = ((), (), s32[]{:S(2)}) async-start(), calls=%async_computation.24 | async-start | bytes 5013504 | tf_op jit(solution)/shard_map/reduce_scatter | solution.py:264
  791.0 331.3 %reduce-scatter.31.cloned.1.call-start = ((), (), s32[]{:S(2)}) async-start(), calls=%async_computation.22 | async-start | bytes 5013504 | tf_op jit(solution)/shard_map/reduce_scatter | solution.py:261
  828.1 71.4 %collective-permute-start.4 = (bf16[2,1024,12,64]{1,3,2,0:T(8,128)(2,1)}, bf16[2,1024,12,64]{1,3,2,0:T(8,128)(2,1)}, u32[]{:S(2)}, u32[]{:S(2)}) collective-permute-start(bf16[2,1024,12,64]{1,3,2,0:T(8,128)(2,1)} %convert_bitcast_fusion), channel_id=1, source_target_pairs={{1,0},{0,1},{3,2},{2,3},{5,4},{4,5},{7,6},{6,7},{9,8},{8,9},{11,10... | collective-permute-start | bytes 9437192 | tf_op jit(solution)/shard_map/ppermute | solution.py:13
  854.1 112.9 %collective-permute-start.2 = (bf16[2,1024,12,64]{1,3,2,0:T(8,128)(2,1)}, bf16[2,1024,12,64]{1,3,2,0:T(8,128)(2,1)}, u32[]{:S(2)}, u32[]{:S(2)}) collective-permute-start(bf16[2,1024,12,64]{1,3,2,0:T(8,128)(2,1)} %fusion.31), channel_id=1, source_target_pairs={{1,0},{0,1},{3,2},{2,3},{5,4},{4,5},{7,6},{6,7},{9,8},{8,9},{11,10... | collective-permute-start | bytes 9437192 | tf_op jit(solution)/shard_map/ppermute | solution.py:13
  872.7 257.3 %reduce-scatter.43.cloned.1.call-start = ((), (), s32[]{:S(2)}) async-start(), calls=%async_computation.28 | async-start | bytes 294912
  938.1 100.4 %collective-permute-start.5 = (bf16[2,1024,12,64]{1,3,2,0:T(8,128)(2,1)}, bf16[2,1024,12,64]{1,3,2,0:T(8,128)(2,1)}, u32[]{:S(2)}, u32[]{:S(2)}) collective-permute-start(bf16[2,1024,12,64]{1,3,2,0:T(8,128)(2,1)} %fusion.24), channel_id=1, source_target_pairs={{1,0},{0,1},{3,2},{2,3},{5,4},{4,5},{7,6},{6,7},{9,8},{8,9},{11,10... | collective-permute-start | bytes 9437192 | tf_op jit(solution)/shard_map/ppermute | solution.py:13
  991.1 107.9 %collective-permute-start.3 = (bf16[2,1024,12,64]{1,3,2,0:T(8,128)(2,1)}, bf16[2,1024,12,64]{1,3,2,0:T(8,128)(2,1)}, u32[]{:S(2)}, u32[]{:S(2)}) collective-permute-start(bf16[2,1024,12,64]{1,3,2,0:T(8,128)(2,1)} %fusion.25), channel_id=1, source_target_pairs={{1,0},{0,1},{3,2},{2,3},{5,4},{4,5},{7,6},{6,7},{9,8},{8,9},{11,10... | collective-permute-start | bytes 9437192 | tf_op jit(solution)/shard_map/ppermute | solution.py:13
  994.5 137.2 %reduce-scatter.23.cloned.1.call-start = ((), (), s32[]{:S(2)}) async-start(), calls=%async_computation.18 | async-start | bytes 294912 | tf_op jit(solution)/shard_map/reduce_scatter | solution.py:306
  996.3 137.0 %reduce-scatter.41.cloned.1.call-start = ((), (), s32[]{:S(2)}) async-start(), calls=%async_computation.27 | async-start | bytes 1253376
  1050.8 120.1 %reduce-scatter.39.cloned.1.call-start = ((), (), s32[]{:S(2)}) async-start(), calls=%async_computation.26 | async-start | bytes 1253376
  1112.9 145.4 %reduce-scatter.45.cloned.1.call-start = ((), (), s32[]{:S(2)}) async-start(), calls=%async_computation.29 | async-start | bytes 589824
  1114.9 145.2 %reduce-scatter.33.cloned.1.call-start = ((), (), s32[]{:S(2)}) async-start(), calls=%async_computation.23 | async-start | bytes 442368 | tf_op jit(solution)/shard_map/reduce_scatter | solution.py:318
  1122.3 139.4 %reduce-scatter.27.cloned.1.call-start = ((), (), s32[]{:S(2)}) async-start(), calls=%async_computation.20 | async-start | bytes 294912 | tf_op jit(solution)/shard_map/reduce_scatter | solution.py:312
  1135.0 128.3 %reduce-scatter.25.cloned.1.call-start = ((), (), s32[]{:S(2)}) async-start(), calls=%async_computation.19 | async-start | bytes 294912 | tf_op jit(solution)/shard_map/reduce_scatter | solution.py:309
  (46 other events, 710.3 us)
Sparse Core Ops, SparseCore 0:
  14.6 38.6 all-gather.19
  55.6 37.2 all-gather.15
  95.2 37.2 all-gather.17
  134.7 37.3 all-gather.21
  174.2 52.1 all-gather.23
  228.5 51.7 all-gather.25
  582.8 59.2 reduce-scatter.28
  776.4 59.3 reduce-scatter.36
  839.7 74.5 reduce-scatter.34
  919.1 74.6 reduce-scatter.30
  996.5 12.2 reduce-scatter.42
  1011.5 13.1 reduce-scatter.22
  1051.0 59.3 reduce-scatter.40
  1113.8 57.0 reduce-scatter.38
  1173.0 12.0 reduce-scatter.44
  1187.3 12.0 reduce-scatter.32
  1201.5 10.9 reduce-scatter.26
  1214.6 10.9 reduce-scatter.24
where the time goes:
time: 1280 us; the launch traced here: 1270 us
  matrix products  672 us (52%)
  waiting for transfers between devices  205 us (16%)
  blocking collectives  141 us (11%)
  local copies, waits for them, and re-layouts  117 us (9%)
  other arithmetic  111 us (9%)
  between operations  16.9 us (1%)
    ppermute x6, waiting for transfers between devices, passed_along(): return lax.ppermute(block, axis, route)  177 us
    dot_general x2, matrix products, on_device(): jnp.einsum('sqhd,skhd->shqk', grad_context, visit_values, preferred_eleme...  117 us
    dot_general x6, matrix products, project(): return jnp.dot(rows, weight, preferred_element_type=jnp.float32)  110 us
    dot_general x6, matrix products, project_back(): lax.dot_general(grads, weight, (((1,), (1,)), ((), ())), preferred_elemen...  79.7 us
    dot_general x2, matrix products, on_device(): jnp.einsum('shqk,skhd->sqhd', weights.astype(jnp.bfloat16), visit_values,...  78.3 us
    dot_general x2, matrix products, on_device(): jnp.einsum('shqk,sqhd->skhd', probs_now.astype(jnp.bfloat16), grad_contex...  75.6 us
    dot_general x2, matrix products, block_scores(): jnp.einsum('sqhd,skhd->shqk', queries, key_block, preferred_element_type=...  73.2 us
    reduce_sum x1, other arithmetic, on_device(): running_sum = running_sum * factor + jnp.sum(weights, axis=-1)  62.4 us
  transfers between devices with their start and end apart: 24, of which 6 were waited for; matrix products, arithmetic and copies ran while one was open for 63% of the time, Pallas kernels for 0%

commit v1 on v0

v1 whole, which is shorter than its diff:
```python
import functools

import jax
import jax.numpy as jnp
from jax import lax
from jax.experimental import pallas as pl
from jax.experimental.pallas import tpu as pltpu
from jax.sharding import PartitionSpec as P

HEADS = 12
HDIM = 64
PAIR = 2 * HDIM
LOG2E = 1.4426950408889634
BF16 = jnp.bfloat16
F32 = jnp.float32


def live_rows(shape, axis, start, length, shift, span):
    row = start + lax.broadcasted_iota(jnp.int32, shape, axis)
    inner = lax.rem(row, span)
    turned = inner + shift
    turned = jnp.where(turned >= span, turned - span, turned)
    return row - inner + turned < length


def attend_kernel(
    info, q_ref, k_ref, v_ref, out_ref, p_ref, sum_ref, keys, vals, ques, bound, turned, *, chunk, span
):
    pos = pl.program_id(1)
    kv = k_ref.shape[0]
    width = p_ref.shape[2]
    factor = HDIM**-0.5 * LOG2E

    @pl.when(pos == 0)
    def prepare():
        live = live_rows((kv, PAIR), 0, 0, info[0], info[1], span)
        kept = jnp.where(live, k_ref[...], jnp.zeros((), BF16))
        keys[...] = kept
        across = live_rows((16, kv), 1, 0, info[0], info[1], span).astype(BF16)
        shown = jnp.where(live, v_ref[...], jnp.zeros((), BF16)).T
        turned_q = q_ref[...].T
        squares = kept.astype(F32)
        squares = (squares * squares).astype(BF16)
        half = lambda axis: lax.broadcasted_iota(jnp.int32, (PAIR, PAIR), axis) // HDIM
        sizes = jnp.dot(squares, (half(0) == half(1)).astype(BF16), preferred_element_type=F32)
        largest = jnp.max(sizes, axis=0, keepdims=True)
        for h in range(2):
            rows = slice(h * HDIM, (h + 1) * HDIM)
            mine = turned_q[rows, :]
            vals[h, 0:HDIM, :] = shown[rows, :]
            vals[h, HDIM:, :] = across
            blank = jnp.zeros_like(mine)
            ques[h] = jnp.concatenate([mine, blank] if h == 0 else [blank, mine], 0)
            sharp = mine.astype(F32)
            reach = jnp.sum(sharp * sharp, axis=0, keepdims=True)
            top = jnp.max(largest[:, rows], axis=1, keepdims=True)
            bound[h : h + 1, :] = jnp.sqrt(reach * top * 1.03) * factor

    cols = pl.ds(pl.multiple_of(pos * width, width), width)

    def weigh(h, peak):
        query = ques[h, :, cols]
        for at in range(0, kv, chunk):
            rows = slice(at, at + chunk)
            scores = jnp.dot(keys[rows, :], query, preferred_element_type=F32)
            p_ref[h, rows, :] = jnp.exp2(scores * factor - peak).astype(BF16)
        total = jnp.dot(vals[h], p_ref[h], preferred_element_type=F32)
        sums = total[HDIM : HDIM + 1, :]
        sum_ref[h] = sums
        turned[h * HDIM : (h + 1) * HDIM, :] = total[0:HDIM, :] / sums
        return jnp.min(sums)

    def exact_peak(h):
        query = ques[h, :, cols]

        def largest(at, peak):
            rows = pl.ds(pl.multiple_of(at * chunk, chunk), chunk)
            scores = jnp.dot(keys[rows, :], query, preferred_element_type=F32)
            live = live_rows((chunk, width), 0, at * chunk, info[0], info[1], span)
            return jnp.maximum(peak, jnp.max(jnp.where(live, scores, -1e30), axis=0, keepdims=True))

        return lax.fori_loop(0, kv // chunk, largest, jnp.full((1, width), -1e30, F32)) * factor

    lowest = [weigh(h, bound[h : h + 1, cols]) for h in range(2)]
    for h in range(2):
        @pl.when(jnp.logical_not(lowest[h] > 2.0**-70))
        def again(h=h):
            weigh(h, exact_peak(h))

    out_ref[...] = turned[...].T.astype(BF16)


def attend(info, q_from, k_from, v_from, span):
    (queries, q_at), (keys, k_at), (values, v_at) = q_from, k_from, v_from
    rows, kv = queries.shape[0], keys.shape[0]
    width = min(512, rows)
    pairs = HEADS // 2
    return pl.pallas_call(
        functools.partial(attend_kernel, chunk=min(256, kv), span=span),
        out_shape=(
            jax.ShapeDtypeStruct((rows, HEADS * HDIM), BF16),
            jax.ShapeDtypeStruct((HEADS, kv, rows), BF16),
            jax.ShapeDtypeStruct((HEADS, 1, rows), F32),
        ),
        grid_spec=pltpu.PrefetchScalarGridSpec(
            num_scalar_prefetch=1,
            grid=(pairs, rows // width),
            in_specs=[
                pl.BlockSpec((rows, PAIR), lambda j, c, s: (0, q_at + j)),
                pl.BlockSpec((kv, PAIR), lambda j, c, s: (0, k_at + j)),
                pl.BlockSpec((kv, PAIR), lambda j, c, s: (0, v_at + j)),
            ],
            out_specs=(
                pl.BlockSpec((width, PAIR), lambda j, c, s: (c, j)),
                pl.BlockSpec((2, kv, width), lambda j, c, s: (j, 0, c)),
                pl.BlockSpec((2, 1, width), lambda j, c, s: (j, 0, c)),
            ),
            scratch_shapes=[
                pltpu.VMEM((kv, PAIR), BF16),
                pltpu.VMEM((2, HDIM + 16, kv), BF16),
                pltpu.VMEM((2, PAIR, rows), BF16),
                pltpu.VMEM((2, rows), F32),
                pltpu.VMEM((PAIR, width), F32),
            ],
        ),
        compiler_params=pltpu.CompilerParams(vmem_limit_bytes=56 * 2**20),
        cost_estimate=pl.CostEstimate(
            flops=2 * 2 * HEADS * rows * kv * 256,
            bytes_accessed=2 * HEADS * rows * kv,
            transcendentals=HEADS * rows * kv,
        ),
        name="attend",
    )(info, queries, keys, values)


def attend_back_kernel(
    info,
    q_ref,
    k_ref,
    v_ref,
    g_ref,
    ctx_ref,
    sum_ref,
    p_ref,
    gq_ref,
    gk_ref,
    gv_ref,
    keys,
    grads,
    grads_up,
    delta,
    low,
    total,
    *,
    width,
    span,
):
    at = pl.program_id(1)
    kv, rows = k_ref.shape[0], q_ref.shape[0]
    block = p_ref.shape[1]
    scale = HDIM**-0.5

    @pl.when(at == 0)
    def prepare():
        live = live_rows((kv, PAIR), 0, 0, info[0], info[1], span)
        keys[...] = jnp.where(live, k_ref[...], jnp.zeros((), BF16)).T
        turned = g_ref[...].T.astype(F32)
        dots = turned * ctx_ref[...].T.astype(F32)
        parts = []
        for h in range(2):
            own = slice(h * HDIM, (h + 1) * HDIM)
            inverse = 1.0 / sum_ref[h]
            delta[h : h + 1, :] = jnp.sum(dots[own, :], axis=0, keepdims=True) * inverse
            parts.append((turned[own, :] * inverse).astype(BF16))
        blank = jnp.zeros((HDIM, rows), BF16)
        grads[0] = jnp.concatenate([parts[0], blank], 0)
        grads[1] = jnp.concatenate([blank, parts[1]], 0)
        grads_up[...] = jnp.concatenate(parts, 0).T
        total[...] = jnp.zeros_like(total)

    here = pl.ds(pl.multiple_of(at * block, block), block)
    values = v_ref[here, :]
    key_parts, value_parts = [], []
    for h in range(2):
        own = slice(h * HDIM, (h + 1) * HDIM)
        for start in range(0, rows, width):
            cols = slice(start, start + width)
            change = jnp.dot(values, grads[h, :, cols], preferred_element_type=F32)
            weight = p_ref[h, :, cols].astype(F32)
            low[h, :, cols] = (weight * (change - delta[h : h + 1, cols])).astype(BF16)
        value_parts.append(jnp.dot(p_ref[h], grads_up[...], preferred_element_type=F32))
        key_parts.append(jnp.dot(low[h], q_ref[...], preferred_element_type=F32))
        total[own, :] += jnp.dot(keys[own, here], low[h], preferred_element_type=F32)
    first = lax.broadcasted_iota(jnp.int32, (block, PAIR), 1) < HDIM
    live = live_rows((block, PAIR), 0, at * block, info[0], info[1], span)
    zero = jnp.zeros((), F32)
    gk_ref[...] = jnp.where(live, jnp.where(first, *key_parts) * scale, zero).astype(BF16)
    gv_ref[...] = jnp.where(live, jnp.where(first, *value_parts), zero).astype(BF16)

    @pl.when(at == kv // block - 1)
    def finish():
        gq_ref[...] = (total[...] * scale).T.astype(BF16)


def attend_back(info, q_from, k_from, v_from, grad, context, sums, probs, span):
    (queries, q_at), (keys, k_at), (values, v_at) = q_from, k_from, v_from
    rows, kv = queries.shape[0], keys.shape[0]
    block = min(512, kv)
    pairs = HEADS // 2
    wide = HEADS * HDIM
    return pl.pallas_call(
        functools.partial(attend_back_kernel, width=min(1024, rows), span=span),
        out_shape=(
            jax.ShapeDtypeStruct((rows, wide), BF16),
            jax.ShapeDtypeStruct((kv, wide), BF16),
            jax.ShapeDtypeStruct((kv, wide), BF16),
        ),
        grid_spec=pltpu.PrefetchScalarGridSpec(
            num_scalar_prefetch=1,
            grid=(pairs, kv // block),
            in_specs=[
                pl.BlockSpec((rows, PAIR), lambda j, c, s: (0, q_at + j)),
                pl.BlockSpec((kv, PAIR), lambda j, c, s: (0, k_at + j)),
                pl.BlockSpec((kv, PAIR), lambda j, c, s: (0, v_at + j)),
                pl.BlockSpec((rows, PAIR), lambda j, c, s: (0, j)),
                pl.BlockSpec((rows, PAIR), lambda j, c, s: (0, j)),
                pl.BlockSpec((2, 1, rows), lambda j, c, s: (j, 0, 0)),
                pl.BlockSpec((2, block, rows), lambda j, c, s: (j, c, 0)),
            ],
            out_specs=(
                pl.BlockSpec((rows, PAIR), lambda j, c, s: (0, j)),
                pl.BlockSpec((block, PAIR), lambda j, c, s: (c, j)),
                pl.BlockSpec((block, PAIR), lambda j, c, s: (c, j)),
            ),
            scratch_shapes=[
                pltpu.VMEM((PAIR, kv), BF16),
                pltpu.VMEM((2, PAIR, rows), BF16),
                pltpu.VMEM((rows, PAIR), BF16),
                pltpu.VMEM((2, rows), F32),
                pltpu.VMEM((2, block, rows), BF16),
                pltpu.VMEM((PAIR, rows), F32),
            ],
        ),
        compiler_params=pltpu.CompilerParams(vmem_limit_bytes=56 * 2**20),
        cost_estimate=pl.CostEstimate(
            flops=4 * 2 * HEADS * rows * kv * 256,
            bytes_accessed=2 * HEADS * rows * kv,
            transcendentals=0,
        ),
        name="attend_back",
    )(info, queries, keys, values, grad, context, sums, probs)


def rows_of(kept_ref, other_ref, step, split):
    return jnp.where(step < split, kept_ref[0], other_ref[...])


def project(rows, weight):
    return jnp.dot(rows, weight, preferred_element_type=F32)


def project_back(grads, weight):
    return lax.dot_general(grads, weight, (((1,), (1,)), ((), ())), preferred_element_type=F32)


def weight_grad(rows, grads):
    return lax.dot_general(rows, grads, (((0,), (0,)), ((), ())), preferred_element_type=F32)


def run_all(copies):
    for copy in copies:
        copy.start()
    return copies


def wait_all(copies):
    for copy in copies:
        copy.wait()


class Pieces:
    def __init__(self, shape, mesh_shape):
        self.m, self.n = mesh_shape
        self.r, self.c = shape

    def copies(self, packed, mats, sems, out):
        found = []
        r, c = self.r, self.c
        for j in range(self.m):
            for i in range(self.n):
                at = 0
                for t, mat in enumerate(mats):
                    tall = mat.shape[0] // (self.m * r)
                    wide = mat.shape[1] // (self.n * c)
                    for w in range(wide):
                        block = packed.at[j * self.n + i, pl.ds(at, tall * r), :]
                        place = mat.at[
                            pl.ds(j * tall * r, tall * r), pl.ds((i * wide + w) * c, c)
                        ]
                        at += tall * r
                        pair = (place, block) if out else (block, place)
                        found.append(pltpu.make_async_copy(*pair, sems.at[len(found)]))
        return found

    def by_mat(self, found, mats):
        counts = [mat.shape[1] // (self.n * self.c) for mat in mats]
        groups = [[] for _ in mats]
        at = 0
        for _ in range(self.m * self.n):
            for t, count in enumerate(counts):
                groups[t] += found[at : at + count]
                at += count
        return groups


def queries_kernel(info, kept_ref, other_ref, packed, bias_ref, out_ref, mat_q, mat_k, mat_v, sems, *, split, grid_of):
    step = pl.program_id(0)
    mats = [mat_q, mat_k, mat_v]

    @pl.when(step == 0)
    def load():
        wait_all(run_all(grid_of.copies(packed, mats, sems, False)))

    rows = rows_of(kept_ref, other_ref, step, split)
    width = mat_q.shape[1]
    for t, mat in enumerate(mats):
        cols = slice(t * width, (t + 1) * width)
        out_ref[:, cols] = (project(rows, mat[...]) + bias_ref[:, cols]).astype(BF16)


def split_specs(kept_at, tile, split, width):
    return [
        pl.BlockSpec((1, tile, width), lambda i, s: (s[kept_at], jnp.minimum(i, split - 1), 0)),
        pl.BlockSpec((tile, width), lambda i, s: (jnp.maximum(i - split, 0), 0)),
    ]


def whole_spec(shape):
    return pl.BlockSpec(shape, lambda i, s: (0,) * len(shape))


def queries_keys_values(info, kept, other, packed, bias, grid_of):
    block_len, width = other.shape
    tile = min(256, block_len)
    split = block_len // tile
    return pl.pallas_call(
        functools.partial(queries_kernel, split=split, grid_of=grid_of),
        out_shape=jax.ShapeDtypeStruct((2 * block_len, 3 * width), BF16),
        grid_spec=pltpu.PrefetchScalarGridSpec(
            num_scalar_prefetch=1,
            grid=(2 * split,),
            in_specs=split_specs(2, tile, split, width)
            + [pl.BlockSpec(memory_space=pl.ANY), whole_spec(bias.shape)],
            out_specs=pl.BlockSpec((tile, 3 * width), lambda i, s: (i, 0)),
            scratch_shapes=[pltpu.VMEM((width, width), BF16)] * 3
            + [pltpu.SemaphoreType.DMA((3 * grid_of.m * grid_of.n,))],
        ),
        compiler_params=pltpu.CompilerParams(vmem_limit_bytes=40 * 2**20),
        cost_estimate=pl.CostEstimate(
            flops=2 * 2 * block_len * width * 3 * width,
            bytes_accessed=2 * 2 * block_len * width * 4,
            transcendentals=0,
        ),
        name="queries",
    )(info, kept, other, packed, bias)


def normal(values):
    middle = jnp.mean(values, axis=-1, keepdims=True)
    centered = values - middle
    spread = jnp.mean(centered * centered, axis=-1, keepdims=True)
    inverse = lax.rsqrt(spread + 1e-12)
    return centered * inverse, inverse


def normal_back(grad, unit, inverse, gain):
    scaled = grad * gain
    mean = jnp.mean(scaled, axis=-1, keepdims=True)
    along = jnp.mean(scaled * unit, axis=-1, keepdims=True)
    return (scaled - mean - unit * along) * inverse


def gelu_pair(u):
    size = jnp.abs(u)
    below = 1.0 + (0.3275911 * 0.7071067811865476) * size
    t = pl.reciprocal(below, approx=True)
    t = t * (2.0 - below * t)
    bell = jnp.exp2((-0.5 * LOG2E) * u * u)
    poly = 0.5 * 1.061405429
    for factor in (-0.5 * 1.453152027, 0.5 * 1.421413741, -0.5 * 0.284496736, 0.5 * 0.254829592):
        poly = poly * t + factor
    tail = poly * t * bell
    phi = jnp.where(u >= 0.0, 1.0 - tail, tail)
    return u * phi, phi + (0.3989422804014327 * u) * bell


def add_rows(total, at, values):
    total[at : at + 1, 0 : values.shape[1]] += jnp.sum(values, axis=0, keepdims=True)


def middle_kernel(
    info,
    hid_kept,
    hid_other,
    cot_kept,
    cot_other,
    ctx_ref,
    cls_ref,
    packed,
    vec_ref,
    inner_bias,
    layer_ref,
    grad_ctx_ref,
    resid_ref,
    sums_ref,
    mat_out,
    mat_inner,
    mat_outer,
    acc_out,
    acc_inner,
    acc_outer,
    totals,
    active,
    slope,
    low,
    vec_low,
    sems,
    vec_sems,
    *,
    split,
    grid_of,
    chunk,
):
    step = pl.program_id(0)
    last = pl.num_programs(0) - 1
    mats = [mat_out, mat_inner, mat_outer]
    tile, width = ctx_ref.shape
    ff = mat_inner.shape[1]
    loads = grid_of.by_mat(grid_of.copies(packed, mats, sems, False), mats)

    @pl.when(step == 0)
    def start():
        for group in loads:
            run_all(group)
        for acc in (acc_out, acc_inner, acc_outer, totals):
            acc[...] = jnp.zeros_like(acc)
        wait_all(loads[0])

    bias_out, gain_one, shift_one, bias_outer, gain_two, shift_two = [
        vec_ref[t : t + 1, :] for t in range(6)
    ]
    hidden = rows_of(hid_kept, hid_other, step, split).astype(F32)
    context = ctx_ref[...]
    unit_one, inverse_one = normal(hidden + project(context, mat_out[...]) + bias_out)
    normed = unit_one * gain_one + shift_one
    normed_low = normed.astype(BF16)

    @pl.when(step == 0)
    def more():
        wait_all(loads[1])
        wait_all(loads[2])

    for at in range(0, ff, chunk):
        cols = slice(at, at + chunk)
        inner = project(normed_low, mat_inner[:, cols]) + inner_bias[:, cols]
        value, change = gelu_pair(inner)
        active[:, cols] = value.astype(BF16)
        slope[:, cols] = change.astype(BF16)
    unit_two, inverse_two = normal(normed + project(active[...], mat_outer[...]) + bias_outer)
    layer_ref[...] = (unit_two * gain_two + shift_two).astype(BF16)

    row = step * tile + lax.broadcasted_iota(jnp.int32, (tile, width), 0)
    grad_result = rows_of(cot_kept, cot_other, step, split).astype(F32)
    grad_result += jnp.where(row == info[4], cls_ref[...], 0.0)
    add_rows(totals, 4, grad_result * unit_two)
    add_rows(totals, 5, grad_result)
    grad_resid_two = normal_back(grad_result, unit_two, inverse_two, gain_two)
    grad_outer = grad_resid_two.astype(BF16)
    add_rows(totals, 3, grad_outer.astype(F32))
    for at in range(0, ff, chunk):
        cols = slice(at, at + chunk)
        grad_inner = project_back(grad_outer, mat_outer[cols, :]) * slope[:, cols].astype(F32)
        low[:, cols] = grad_inner.astype(BF16)
        totals[8:9, cols] += jnp.sum(grad_inner, axis=0, keepdims=True)
        acc_outer[cols, :] += weight_grad(active[:, cols], grad_outer)
    grad_normed = grad_resid_two + project_back(low[...], mat_inner[...])
    for at in range(0, ff, chunk):
        cols = slice(at, at + chunk)
        acc_inner[:, cols] += weight_grad(normed_low, low[:, cols])
    add_rows(totals, 1, grad_normed * unit_one)
    add_rows(totals, 2, grad_normed)
    grad_resid_one = normal_back(grad_normed, unit_one, inverse_one, gain_one)
    resid_ref[...] = grad_resid_one
    grad_attn = grad_resid_one.astype(BF16)
    add_rows(totals, 0, grad_attn.astype(F32))
    acc_out[...] += weight_grad(context, grad_attn)
    grad_ctx_ref[...] = project_back(grad_attn, mat_out[...]).astype(BF16)

    @pl.when(step == last)
    def finish():
        r, c, m, n = grid_of.r, grid_of.c, grid_of.m, grid_of.n
        stores = grid_of.by_mat(grid_of.copies(sums_ref, mats, sems, True), mats)
        for mat, acc, group in zip(mats, (acc_out, acc_inner, acc_outer), stores):
            mat[...] = acc[...].astype(BF16)
            run_all(group)
        vec_low[...] = jnp.zeros_like(vec_low)
        for i in range(n):
            for t in range(6):
                vec_low[i, t : t + 1, :] = totals[t : t + 1, i * c : (i + 1) * c]
            wide = ff // (n * c)
            for t in range(wide):
                at = (i * wide + t) * c
                vec_low[i, 6 + t : 7 + t, :] = totals[8:9, at : at + c]
        tails = []
        vec_bits = vec_low[...].astype(BF16)
        for i in range(n):
            active[16 * i : 16 * i + 16, 0:c] = vec_bits[i]
        for j in range(m):
            for i in range(n):
                tails.append(
                    pltpu.make_async_copy(
                        active.at[pl.ds(16 * i, 16), pl.ds(0, c)],
                        sums_ref.at[j * n + i, pl.ds(9 * r, 16), :],
                        vec_sems.at[j * n + i],
                    )
                )
        run_all(tails)
        for group in stores:
            wait_all(group)
        wait_all(tails)


def middle(info, hidden, cots, context, cls_row, packed, vectors, inner_bias, grid_of):
    block_len, width = hidden[1].shape
    ff = inner_bias.shape[1]
    tile = min(256, block_len)
    split = block_len // tile
    pieces = grid_of.m * grid_of.n
    row_spec = pl.BlockSpec((tile, width), lambda i, s: (i, 0))
    return pl.pallas_call(
        functools.partial(middle_kernel, split=split, grid_of=grid_of, chunk=768),
        out_shape=(
            jax.ShapeDtypeStruct((2 * block_len, width), BF16),
            jax.ShapeDtypeStruct((2 * block_len, width), BF16),
            jax.ShapeDtypeStruct((2 * block_len, width), F32),
            jax.ShapeDtypeStruct((pieces, 9 * grid_of.r + 16, grid_of.c), BF16),
        ),
        grid_spec=pltpu.PrefetchScalarGridSpec(
            num_scalar_prefetch=1,
            grid=(2 * split,),
            in_specs=split_specs(2, tile, split, width)
            + split_specs(3, tile, split, width)
            + [
                row_spec,
                whole_spec(cls_row.shape),
                pl.BlockSpec(memory_space=pl.ANY),
                whole_spec(vectors.shape),
                whole_spec(inner_bias.shape),
            ],
            out_specs=(row_spec, row_spec, row_spec, pl.BlockSpec(memory_space=pl.ANY)),
            scratch_shapes=[
                pltpu.VMEM((width, width), BF16),
                pltpu.VMEM((width, ff), BF16),
                pltpu.VMEM((ff, width), BF16),
                pltpu.VMEM((width, width), F32),
                pltpu.VMEM((width, ff), F32),
                pltpu.VMEM((ff, width), F32),
                pltpu.VMEM((16, ff), F32),
                pltpu.VMEM((tile, ff), BF16),
                pltpu.VMEM((tile, ff), BF16),
                pltpu.VMEM((tile, ff), BF16),
                pltpu.VMEM((grid_of.n, 16, grid_of.c), F32),
                pltpu.SemaphoreType.DMA((6 * pieces,)),
                pltpu.SemaphoreType.DMA((pieces,)),
            ],
        ),
        compiler_params=pltpu.CompilerParams(vmem_limit_bytes=60 * 2**20),
        cost_estimate=pl.CostEstimate(
            flops=2 * 2 * block_len * width * (width + 2 * ff) * 3,
            bytes_accessed=2 * block_len * width * 16 + 40 * width * width,
            transcendentals=2 * 2 * block_len * ff,
        ),
        name="middle",
    )(info, *hidden, *cots, context, cls_row, packed, vectors, inner_bias)


def tail_kernel(info, hid_kept, hid_other, gq_ref, gk_ref, gv_ref, resid_ref, packed, *rest, split, grid_of, full):
    step = pl.program_id(0)
    if full:
        grad_ref, sums_ref, mat_q, mat_k, mat_v, sems, acc, totals, vec_low, vec_sems = rest
    else:
        grad_ref, mat_q, mat_k, mat_v, sems = rest
    mats = [mat_q, mat_k, mat_v]
    grads = [gq_ref[...], gk_ref[...], gv_ref[...]]

    @pl.when(step == 0)
    def load():
        wait_all(run_all(grid_of.copies(packed, mats, sems, False)))

    def into_input():
        total = resid_ref[...]
        for grad, mat in zip(grads, mats):
            total += project_back(grad, mat[...])
        grad_ref[...] = total.astype(grad_ref.dtype)

    if not full:
        into_input()
        return

    pl.when(step < split)(into_input)

    @pl.when(step == 0)
    def clear():
        acc[...] = jnp.zeros_like(acc)
        totals[...] = jnp.zeros_like(totals)

    rows = rows_of(hid_kept, hid_other, step, split)
    for t, grad in enumerate(grads):
        acc[t] += weight_grad(rows, grad)
    add_rows(totals, 0, grads[0].astype(F32))
    add_rows(totals, 1, grads[2].astype(F32))

    @pl.when(step == pl.num_programs(0) - 1)
    def finish():
        r, c, m, n = grid_of.r, grid_of.c, grid_of.m, grid_of.n
        for t, mat in enumerate(mats):
            mat[...] = acc[t].astype(BF16)
        stores = run_all(grid_of.copies(sums_ref, mats, sems, True))
        vec_low[...] = jnp.zeros_like(vec_low)
        for i in range(n):
            part = jnp.concatenate([totals[0:2, i * c : (i + 1) * c], jnp.zeros((14, c), F32)], 0)
            vec_low[i] = part.astype(BF16)
        tails = []
        for j in range(m):
            for i in range(n):
                tails.append(
                    pltpu.make_async_copy(
                        vec_low.at[i],
                        sums_ref.at[j * n + i, pl.ds(3 * r, 16), :],
                        vec_sems.at[j * n + i],
                    )
                )
        run_all(tails)
        wait_all(stores)
        wait_all(tails)


def tail(info, hidden, grads, resid, packed, grid_of, full):
    block_len, width = hidden[1].shape
    tile = min(256, block_len)
    split = block_len // tile
    pieces = grid_of.m * grid_of.n
    steps = 2 * split if full else split
    at = (lambda i: i) if full else (lambda i: i + split)
    row_spec = pl.BlockSpec((tile, width), lambda i, s: (at(i), 0))
    out_spec = pl.BlockSpec((tile, width), lambda i, s: (jnp.minimum(i, split - 1), 0))
    out_shape = [jax.ShapeDtypeStruct((block_len, width), F32 if full else BF16)]
    out_specs = [out_spec]
    scratch = [pltpu.VMEM((width, width), BF16)] * 3 + [pltpu.SemaphoreType.DMA((3 * pieces,))]
    if full:
        out_shape.append(jax.ShapeDtypeStruct((pieces, 3 * grid_of.r + 16, grid_of.c), BF16))
        out_specs.append(pl.BlockSpec(memory_space=pl.ANY))
        scratch += [
            pltpu.VMEM((3, width, width), F32),
            pltpu.VMEM((8, width), F32),
            pltpu.VMEM((grid_of.n, 16, grid_of.c), BF16),
            pltpu.SemaphoreType.DMA((pieces,)),
        ]
    return pl.pallas_call(
        functools.partial(tail_kernel, split=split, grid_of=grid_of, full=full),
        out_shape=tuple(out_shape),
        grid_spec=pltpu.PrefetchScalarGridSpec(
            num_scalar_prefetch=1,
            grid=(steps,),
            in_specs=split_specs(2, tile, split, width)
            + [row_spec] * 4
            + [pl.BlockSpec(memory_space=pl.ANY)],
            out_specs=tuple(out_specs),
            scratch_shapes=scratch,
        ),
        compiler_params=pltpu.CompilerParams(vmem_limit_bytes=48 * 2**20),
        cost_estimate=pl.CostEstimate(
            flops=2 * block_len * width * 3 * width * (3 if full else 1),
            bytes_accessed=block_len * width * 16,
            transcendentals=0,
        ),
        name="tail_all" if full else "tail_other",
    )(info, *hidden, *grads, resid, packed)


def swap(block, axis, route):
    if all(a == b for a, b in route):
        return block
    return lax.ppermute(block, axis, route)


class Regroup:
    def __init__(self):
        self.n = lax.axis_size("blk")
        self.me = lax.axis_index("blk")
        self.per = self.n // 2
        self.passage = self.me // self.per
        self.part = lax.rem(self.me, 2)
        self.first = [(i, (i % 2) * self.per + i // 2) for i in range(self.n)]
        self.second = [(i, (1 - i % 2) * self.per + i // 2) for i in range(self.n)]
        self.stays = all(a == b for a, b in self.first)

    def gather(self, pair):
        other = lax.dynamic_index_in_dim(pair, 1 - self.part, 0, keepdims=False)
        other = swap(other, "blk", self.second)
        if self.stays:
            return (pair, other)
        kept = lax.dynamic_index_in_dim(pair, self.part, 0, keepdims=True)
        return (swap(kept, "blk", self.first), other)

    def kept_index(self):
        return self.part if self.stays else jnp.zeros_like(self.part)

    def back(self, kept, other):
        kept = swap(kept, "blk", [(b, a) for a, b in self.first])
        other = swap(other, "blk", [(b, a) for a, b in self.second])
        return kept, other

    def order(self, kept, other):
        return jnp.where(self.part == 0, jnp.stack([kept, other]), jnp.stack([other, kept]))


def pack(shards):
    c = min(s.shape[1] for s in shards)
    return jnp.concatenate(
        [s[:, at : at + c] for s in shards for at in range(0, s.shape[1], c)], axis=0
    )


def unpack(block, shapes):
    c = block.shape[-1]
    found, at = [], 0
    for rows, cols in shapes:
        parts = []
        for _ in range(cols // c):
            parts.append(block[..., at : at + rows, :])
            at += rows
        found.append(jnp.concatenate(parts, axis=-1) if len(parts) > 1 else parts[0])
    return found


class Weights:
    def __init__(self, shards):
        self.shapes = [s.shape for s in shards]
        self.m, self.n = lax.axis_size("batch"), lax.axis_size("blk")
        r, c = min(s[0] for s in self.shapes), min(s[1] for s in self.shapes)
        self.fits = r % 16 == 0 and c % 128 == 0
        packed = lax.all_gather(pack(shards), ("batch", "blk"), axis=0)
        if self.fits:
            self.grid_of = Pieces((r, c), (self.m, self.n))
            self.packed = packed
        else:
            self.grid_of = Pieces((r * self.m, c * self.n), (1, 1))
            whole = []
            for part in unpack(packed, self.shapes):
                rows, cols = part.shape[1:]
                part = part.reshape(self.m, self.n, rows, cols).transpose(0, 2, 1, 3)
                whole.append(part.reshape(self.m * rows, self.n * cols))
            self.packed = pack(whole)[None]

    def scatter(self, sums):
        extra = 16
        if not self.fits:
            rows = sums.shape[1] - extra
            wide = [(a * self.m, b * self.n) for a, b in self.shapes]
            parts = []
            for part in unpack(sums[0, :rows], wide):
                a, b = part.shape[0] // self.m, part.shape[1] // self.n
                part = part.reshape(self.m, a, self.n, b).transpose(0, 2, 1, 3)
                parts.append(part.reshape(self.m * self.n, a, b))
            c = min(s[1] for s in self.shapes)
            blocks = jnp.stack([pack([p[d] for p in parts]) for d in range(self.m * self.n)])
            vecs = sums[0, rows:].reshape(extra, self.n, c).transpose(1, 0, 2)
            vecs = jnp.broadcast_to(vecs[None], (self.m, self.n, extra, c))
            sums = jnp.concatenate([blocks, vecs.reshape(self.m * self.n, extra, c)], axis=1)
        height, c = sums.shape[1:]
        own = lax.psum_scatter(
            sums.reshape(-1, c), ("batch", "blk"), scatter_dimension=0, tiled=True
        )
        own = own.astype(F32)
        return [*unpack(own[: height - extra], self.shapes), own[height - extra :]]


def on_device(
    hidden_in,
    lengths,
    cot_out,
    cot_cls,
    w_query,
    w_key,
    w_value,
    w_out,
    w_inner,
    w_outer,
    b_query,
    b_value,
    b_out,
    norm1_gain,
    norm1_shift,
    b_inner,
    b_outer,
    norm2_gain,
    norm2_shift,
):
    plan = Regroup()
    groups, block_len, width = hidden_in.shape
    span = groups * block_len
    per = plan.per
    fleets = [[i * per + j for j in range(per)] for i in range(2)]
    first_row = plan.passage * block_len
    owner = lax.rem(plan.me, per) == 0

    length = lax.dynamic_index_in_dim(lengths, plan.passage, 0, keepdims=False)
    info = jnp.stack(
        [
            length,
            first_row,
            plan.kept_index(),
            plan.kept_index(),
            jnp.where(owner, first_row, -1),
        ]
    ).astype(jnp.int32)

    heads = Weights([w_query, w_key, w_value])
    dense = Weights([w_out, w_inner, w_outer])
    narrow = jnp.stack(
        [b_query, b_value, b_out, norm1_gain, norm1_shift, b_outer, norm2_gain, norm2_shift]
    )
    share = width // plan.n
    vec_shard = jnp.concatenate([narrow, b_inner.reshape(-1, share)], 0)
    vec_all = lax.all_gather(vec_shard, "blk", axis=0).astype(F32)
    narrow = vec_all[:, :8].transpose(1, 0, 2).reshape(8, width)
    bias_inner = vec_all[:, 8:].reshape(1, -1)
    bias_heads = jnp.concatenate([narrow[0:1], jnp.zeros_like(narrow[0:1]), narrow[1:2]], 1)

    hidden = plan.gather(hidden_in)
    cots = plan.gather(cot_out)
    qkv = queries_keys_values(info, *hidden, heads.packed, bias_heads, heads.grid_of)
    if per == 1:
        kv, key_at = qkv, width // PAIR
    else:
        kv = lax.all_gather(qkv[:, width:], "blk", axis=0, tiled=True, axis_index_groups=fleets)
        key_at = 0
    sources = ((qkv, 0), (kv, key_at), (kv, key_at + width // PAIR))
    context_low, probs, sums = attend(info, *sources, span)

    own_cls = lax.dynamic_index_in_dim(cot_cls, plan.passage, 0, keepdims=True).astype(F32)
    layer_out, grad_context, grad_resid, dense_sums = middle(
        info, hidden, cots, context_low, own_cls, dense.packed, narrow[2:], bias_inner, dense.grid_of
    )
    part_wo, part_wi, part_wu, dense_vecs = dense.scatter(dense_sums)
    part_bo, part_g1, part_s1, part_bu, part_g2, part_s2 = [dense_vecs[t] for t in range(6)]
    part_bi = dense_vecs[6 : 6 + b_inner.size // share].reshape(-1)

    top = lax.dynamic_slice_in_dim(layer_out, first_row, 1, 0)
    tops = lax.all_gather(top, "blk", axis=0, tiled=True)[::per]
    cls_part = lax.dynamic_slice_in_dim(tops, plan.me * share, share, 1)
    layer_rows = plan.order(*plan.back(layer_out[:block_len], layer_out[block_len:]))

    grad_q, grad_k, grad_v = attend_back(info, *sources, grad_context, context_low, sums, probs, span)
    if per > 1:
        grad_k, grad_v = [
            lax.psum_scatter(g, "blk", scatter_dimension=0, tiled=True, axis_index_groups=fleets)
            for g in (grad_k, grad_v)
        ]
    grads = (grad_q, grad_k, grad_v)
    (other,) = tail(info, hidden, grads, grad_resid, heads.packed, heads.grid_of, False)
    kept, head_sums = tail(info, hidden, grads, grad_resid, heads.packed, heads.grid_of, True)
    kept, other = plan.back(kept, other)
    grad_input = plan.order(kept, other.astype(F32))
    part_wq, part_wk, part_wv, head_vecs = heads.scatter(head_sums)
    part_bq, part_bv = head_vecs[0], head_vecs[1]
    return (
        layer_rows,
        cls_part,
        grad_input,
        part_wq,
        part_wk,
        part_wv,
        part_wo,
        part_wi,
        part_wu,
        part_bq,
        part_bv,
        part_bo,
        part_g1,
        part_s1,
        part_bi,
        part_bu,
        part_g2,
        part_s2,
    )


def solution(mesh):
    rows = P("batch", "blk", None)
    mats = (P("batch", "blk"),) * 6
    vecs = (P("blk"),) * 9
    return jax.shard_map(
        on_device,
        mesh=mesh,
        in_specs=(rows, P("batch"), rows, P("batch", None)) + mats + vecs,
        out_specs=(rows, P("batch", "blk"), rows) + mats + vecs,
        check_vma=False,
    )
```

time: 1280 us -> 843 us (0.66)
  matrix products: 672 us -> 0 us
  Pallas kernels: 0 us -> 352 us
  waiting for transfers between devices: 205 us -> 318 us
  other arithmetic: 111 us -> 12.9 us
  local copies, waits for them, and re-layouts: 117 us -> 26.2 us
  blocking collectives: 141 us -> 110 us
    dot_general x30 -> x0, matrix products: 672 us -> none  [the longest x2 117 us: on_device(): jnp.einsum('sqhd,skhd->shqk', grad_context, visit_values, preferred_eleme...]
    pallas_call x0 -> x6, Pallas kernels: none -> 352 us  [the longest x1 115 us: middle(): pl.pallas_call(functools.partial(middle_kernel, split=split, grid_of=grid...]
    reduce_scatter x7 -> x2, waiting for transfers between devices: 0.05 us -> 318 us  [scatter(): lax.psum_scatter(sums.reshape(-1, c), ('batch', 'blk'), scatter_dimension...]
    ppermute x6 -> x4, waiting for transfers between devices: 177 us -> 0.01 us  [swap(): return lax.ppermute(block, axis, route)]
    reduce_sum x10 -> x0, other arithmetic: 85.5 us -> none  [the longest x1 62.4 us: on_device(): running_sum = running_sum * factor + jnp.sum(weights, axis=-1)]
    psum x2 -> x0, blocking collectives: 66 us -> none  [the longest x1 57.7 us: on_device(): lax.psum(grad_bias_query.astype(jnp.bfloat16), 'batch').astype(jnp.float32)]
    unnamed x144 -> x43, local copies, waits for them, and re-layouts: 48.6 us -> 8.01 us
    all_gather x15 -> x2, blocking collectives: 75.1 us -> 110 us  [the longest x1 76.8 us: on_device(): vec_all = lax.all_gather(vec_shard, 'blk', axis=0).astype(F32)]
  transfers between devices with their start and end apart: 24 -> 8, of which waited for: 6 -> 2; matrix products, arithmetic and copies ran while one was open for 63% -> 3% of each run, Pallas kernels for 0% -> 12%
where the time goes in v1:
time: 843 us; the launch traced here: 838 us
  Pallas kernels  352 us (42%)
  waiting for transfers between devices  318 us (38%)
  blocking collectives  110 us (13%)
  local copies, waits for them, and re-layouts  26.2 us (3%)
  between operations  14.2 us (2%)
  other arithmetic  12.9 us (2%)
    reduce_scatter x2, waiting for transfers between devices, scatter(): lax.psum_scatter(sums.reshape(-1, c), ('batch', 'blk'), scatter_dimension...  318 us
    pallas_call x1, Pallas kernels, middle(): pl.pallas_call(functools.partial(middle_kernel, split=split, grid_of=grid...  115 us
    pallas_call x1, Pallas kernels, attend_back(): pl.pallas_call(functools.partial(attend_back_kernel, width=min(1024, rows...  112 us
    all_gather x1, blocking collectives, on_device(): vec_all = lax.all_gather(vec_shard, 'blk', axis=0).astype(F32)  76.8 us
    pallas_call x1, Pallas kernels, attend(): pl.pallas_call(functools.partial(attend_kernel, chunk=min(256, kv), span=...  75.9 us
    pallas_call x2, Pallas kernels, tail(): pl.pallas_call(functools.partial(tail_kernel, split=split, grid_of=grid_o...  35.4 us
    all_gather x1, blocking collectives, on_device(): tops = lax.all_gather(top, 'blk', axis=0, tiled=True)[::per]  33 us
  transfers between devices with their start and end apart: 8, of which 2 were waited for; matrix products, arithmetic and copies ran while one was open for 3% of the time, Pallas kernels for 12%

profile of v1, /device:TPU:0, one launch (start us, length us, event | category | flops | bytes accessed | tf_op | source)
XLA Modules:
  0.0 838.2 jit_solution(12221261403013751593)
XLA Ops:
  7.2 1.5 pad_maximum_fusion.1
  8.8 0.8 constant_dynamic-update-slice_fusion.1
  9.5 0.8 slice_dynamic-update-slice_fusion.3
  10.3 0.8 slice_dynamic-update-slice_fusion.2
  11.1 0.8 slice_dynamic-update-slice_fusion.1
  11.9 0.8 slice_dynamic-update-slice_fusion
  12.7 0.9 constant_dynamic-update-slice_fusion
  13.6 0.7 copy-done.6
  14.6 2.8 dynamic-slice_bitcast_fusion.1
  17.4 3.0 collective-permute-start
  20.4 2.7 dynamic-slice_bitcast_fusion
  23.3 76.8 %all-gather.3 = bf16[2,12,384]{2,1,0:T(8,128)(2,1)S(1)} all-gather(bf16[1,12,384]{2,1,0:T(8,128)(2,1)S(1)} %bitcast.34), channel_id=3, replica_groups=mesh['batch'=16,'blk'=2] {'blk'}, dimensions={0}, use_global_device_ids=true | all-gather | bytes 27648 | tf_op jit(solution)/shard_map/all_gather | solution.py:836
  103.3 2.0 copy-done.1
  105.3 13.5 %queries.1.q_ref.k_ref.v_ref = bf16[2048,2304]{1,0:T(8,128)(2,1)} custom-call(s32[5]{0:T(128)S(1)} %stack.69.info, bf16[2,1024,768]{2,1,0:T(8,128)(2,1)S(1)} %copy-done, bf16[1024,768]{1,0:T(8,128)(2,1)} %collective-permute-done.other_ref.hid_other, bf16[32,144,384]{2,1,0:T(8,128)(2,1)S(1)} %bitcast.30, f32[1,2304]{1,0:T(1,128)S(1)} %fusion.bias_ref), custom_call_target="tpu_custom_call" | custom-call | flops 7247757312 | bytes 12582912 | tf_op jit(solution)/shard_map/queries/pallas_call | solution.py:346
  118.7 75.9 %attend.1 = (bf16[2048,768]{1,0:T(8,128)(2,1)}, bf16[12,2048,2048]{2,1,0:T(8,128)(2,1)}, f32[12,1,2048]{2,1,0:T(1,128)}) custom-call(s32[5]{0:T(128)} %copy-done.2, bf16[2048,2304]{1,0:T(8,128)(2,1)} %queries.1.q_ref.k_ref.v_ref, bf16[2048,2304]{1,0:T(8,128)(2,1)} %queries.1.q_ref.k_ref.v_ref, bf16[2048,2304]{1,0:T(8,128)(2,1)} %queries.1.q_ref.k_ref.v_ref), custom_call_target="tpu_custom_call" | custom-call | flops 51539607552 | bytes 100663296 | tf_op jit(solution)/shard_map/attend/pallas_call | solution.py:98
  194.7 114.7 %middle.1 = (bf16[2048,768]{1,0:T(8,128)(2,1)}, bf16[2048,768]{1,0:T(8,128)(2,1)}, f32[2048,768]{1,0:T(8,128)}, bf16[32,448,384]{2,1,0:T(8,128)(2,1)}) custom-call(s32[5]{0:T(128)} %copy-done.2, bf16[2,1024,768]{2,1,0:T(8,128)(2,1)} %hid_kept.5, bf16[1024,768]{1,0:T(8,128)(2,1)} %collective-permute-done.other_ref.hid_other, bf16[2,1024,768]{2,1,0:T(8,128)(2,1)} %cot_kept.1, ...), custom_call_target="tpu_custom_call" | custom-call | flops 65229815808 | bytes 48758784 | tf_op jit(solution)/shard_map/middle/pallas_call | solution.py:540
  309.4 112.2 %attend_back.1 = (bf16[2048,768]{1,0:T(8,128)(2,1)}, bf16[2048,768]{1,0:T(8,128)(2,1)}, bf16[2048,768]{1,0:T(8,128)(2,1)}) custom-call(s32[5]{0:T(128)} %copy-done.2, bf16[2048,2304]{1,0:T(8,128)(2,1)} %queries.1.q_ref.k_ref.v_ref, bf16[2048,2304]{1,0:T(8,128)(2,1)} %queries.1.q_ref.k_ref.v_ref, bf16[2048,2304]{1,0:T(8,128)(2,1)} %queries.1.q_ref.k_ref.v_ref, ...), custom_call_target="tpu_custom_call" | custom-call | flops 103079215104 | bytes 100663296 | tf_op jit(solution)/shard_map/attend_back/pallas_call | solution.py:211
  421.6 23.7 %tail_all.1 = (f32[1024,768]{1,0:T(8,128)S(1)}, bf16[32,160,384]{2,1,0:T(8,128)(2,1)}) custom-call(s32[5]{0:T(128)S(1)} %copy-done.3, bf16[2,1024,768]{2,1,0:T(8,128)(2,1)} %hid_kept.5, bf16[1024,768]{1,0:T(8,128)(2,1)} %collective-permute-done.other_ref.hid_other, bf16[2048,768]{1,0:T(8,128)(2,1)} %get-tuple-element.35.gq_ref, ...), custom_call_target="tpu_custom_call" | custom-call | flops 10871635968 | bytes 12582912 | tf_op jit(solution)/shard_map/tail_all/pallas_call | solution.py:669
  445.9 11.7 %tail_other.1 = bf16[1024,768]{1,0:T(8,128)(2,1)} custom-call(s32[5]{0:T(128)S(1)} %copy-done.3, bf16[2,1024,768]{2,1,0:T(8,128)(2,1)} %hid_kept.5, bf16[1024,768]{1,0:T(8,128)(2,1)} %collective-permute-done.other_ref.hid_other, bf16[2048,768]{1,0:T(8,128)(2,1)} %get-tuple-element.35.gq_ref, bf16[2048,768]{1,0:T(8,128)(2,1)} %get-tuple-element.36.gk_ref, ...), custom_call_target="tpu_custom_call" | custom-call | flops 3623878656 | bytes 12582912 | tf_op jit(solution)/shard_map/tail_other/pallas_call | solution.py:669
  457.7 1.9 slice_bitcast_fusion
  459.6 2.0 collective-permute-start.2
  462.3 33.0 %all-gather.4 = bf16[2,1,768]{2,1,0:T(2,128)(2,1)S(1)} all-gather(bf16[1,1,768]{2,1,0:T(2,128)(2,1)S(1)} %dynamic-slice_bitcast_fusion.2), channel_id=1, replica_groups=mesh['batch'=16,'blk'=2] {'blk'}, dimensions={0}, use_global_device_ids=true | all-gather | bytes 4608 | tf_op jit(solution)/shard_map/all_gather | solution.py:861
  495.9 1.6 bitcast_convert_fusion
  497.5 2.9 maximum_select_fusion
  500.5 3.6 maximum_select_fusion.1
  504.0 172.6 %reduce-scatter.3.cloned.1.call-done = bf16[160,384]{1,0:T(8,128)(2,1)} async-done(((bf16[5120,384]{1,0:T(8,128)(2,1)}), bf16[160,384]{1,0:T(8,128)(2,1)}) %reduce-scatter.3.cloned.1.call-update) | async-done | bytes 122896 | tf_op jit(solution)/shard_map/reduce_scatter | solution.py:782
  676.6 0.9 convert_element_type.15
  678.1 1.5 fusion.2
  679.6 145.2 %reduce-scatter.5.cloned.1.call-done = bf16[448,384]{1,0:T(8,128)(2,1)} async-done(((bf16[14336,384]{1,0:T(8,128)(2,1)}), bf16[448,384]{1,0:T(8,128)(2,1)}) %reduce-scatter.5.cloned.1.call-update) | async-done | bytes 344080 | tf_op jit(solution)/shard_map/reduce_scatter | solution.py:782
  826.2 1.0 convert_element_type.16
  827.8 1.5 fusion.1
  830.1 1.6 slice.163
  (80 shorter events, 8.8 us)
Async XLA Ops:
  7.2 96.0 %all-gather.8.cloned.1.call-start = ((), (), s32[]{:S(2)}) async-start(), calls=%async_computation.4 | async-start | bytes 3649536 | tf_op jit(solution)/shard_map/all_gather | solution.py:753
  8.7 186.0 %all-gather.10.cloned.1.call-start = ((), (), s32[]{:S(2)}) async-start(), calls=%async_computation.5 | async-start | bytes 10948608 | tf_op jit(solution)/shard_map/all_gather | solution.py:753
  13.6 0.8 copy-start.6
  14.4 662.2 %reduce-scatter.3.cloned.1.call-start = ((), (), s32[]{:S(2)}) async-start(), calls=%async_computation.2 | async-start | bytes 4055040 | tf_op jit(solution)/shard_map/reduce_scatter | solution.py:782
  14.4 8.6 %copy-start.9 = (bf16[384]{0:T(512)(128)(2,1)S(1)}, bf16[384]{0:T(512)(128)(2,1)}, u32[]{:S(2)}) copy-start(bf16[384]{0:T(512)(128)(2,1)} %param.29) | copy-start | bytes 2308
  14.4 8.6 %copy-start.10 = (bf16[384]{0:T(512)(128)(2,1)S(1)}, bf16[384]{0:T(512)(128)(2,1)}, u32[]{:S(2)}) copy-start(bf16[384]{0:T(512)(128)(2,1)} %param.30) | copy-start | bytes 2308
  14.5 8.6 %copy-start.11 = (bf16[384]{0:T(512)(128)(2,1)S(1)}, bf16[384]{0:T(512)(128)(2,1)}, u32[]{:S(2)}) copy-start(bf16[384]{0:T(512)(128)(2,1)} %param.31) | copy-start | bytes 2308
  14.5 8.6 %copy-start.12 = (bf16[384]{0:T(512)(128)(2,1)S(1)}, bf16[384]{0:T(512)(128)(2,1)}, u32[]{:S(2)}) copy-start(bf16[384]{0:T(512)(128)(2,1)} %param.32) | copy-start | bytes 2308
  14.5 8.6 %copy-start.13 = (bf16[384]{0:T(512)(128)(2,1)S(1)}, bf16[384]{0:T(512)(128)(2,1)}, u32[]{:S(2)}) copy-start(bf16[384]{0:T(512)(128)(2,1)} %param.33) | copy-start | bytes 2308
  14.5 8.6 %copy-start.14 = (bf16[384]{0:T(512)(128)(2,1)S(1)}, bf16[384]{0:T(512)(128)(2,1)}, u32[]{:S(2)}) copy-start(bf16[384]{0:T(512)(128)(2,1)} %param.35) | copy-start | bytes 2308
  14.5 8.6 %copy-start.15 = (bf16[384]{0:T(512)(128)(2,1)S(1)}, bf16[384]{0:T(512)(128)(2,1)}, u32[]{:S(2)}) copy-start(bf16[384]{0:T(512)(128)(2,1)} %param.36) | copy-start | bytes 2308
  14.5 8.6 %copy-start.16 = (bf16[384]{0:T(512)(128)(2,1)S(1)}, bf16[384]{0:T(512)(128)(2,1)}, u32[]{:S(2)}) copy-start(bf16[384]{0:T(512)(128)(2,1)} %param.37) | copy-start | bytes 2308
  14.5 8.6 %copy-start.7 = (bf16[1536]{0:T(1024)(128)(2,1)S(1)}, bf16[1536]{0:T(1024)(128)(2,1)}, u32[]{:S(2)}) copy-start(bf16[1536]{0:T(1024)(128)(2,1)} %param.34) | copy-start | bytes 9220
  14.5 86.7 %copy-start.17 = (s32[2]{0:T(128)S(1)}, s32[2]{0:T(128)}, u32[]{:S(2)}) copy-start(s32[2]{0:T(128)} %param.20) | copy-start | bytes 28
  14.6 88.0 %copy-start.8 = (bf16[2,768]{1,0:T(2,128)(2,1)S(1)}, bf16[2,768]{1,0:T(2,128)(2,1)}, u32[]{:S(2)}) copy-start(bf16[2,768]{1,0:T(2,128)(2,1)} %param.22) | copy-start | bytes 9220
  14.6 88.7 %copy-start = (bf16[2,1024,768]{2,1,0:T(8,128)(2,1)S(1)}, bf16[2,1024,768]{2,1,0:T(8,128)(2,1)}, u32[]{:S(2)}) copy-start(bf16[2,1024,768]{2,1,0:T(8,128)(2,1)} %hid_kept.5) | copy-start | bytes 9437188
  17.4 85.8 %collective-permute-start = (bf16[1024,768]{1,0:T(8,128)(2,1)}, bf16[1024,768]{1,0:T(8,128)(2,1)}, u32[]{:S(2)}, u32[]{:S(2)}) collective-permute-start(bf16[1024,768]{1,0:T(8,128)(2,1)} %dynamic-slice_bitcast_fusion.1), channel_id=1, source_target_pairs={{0,1},{1,0},{2,3},{3,2},{4,5},{5,4},{6,7},{7,6},{8,9},{9,8},{10,11... | collective-permute-start | bytes 4718600 | tf_op jit(solution)/shard_map/ppermute | solution.py:694
  23.0 171.7 %collective-permute-start.1 = (bf16[1024,768]{1,0:T(8,128)(2,1)}, bf16[1024,768]{1,0:T(8,128)(2,1)}, u32[]{:S(2)}, u32[]{:S(2)}) collective-permute-start(bf16[1024,768]{1,0:T(8,128)(2,1)} %dynamic-slice_bitcast_fusion), channel_id=1, source_target_pairs={{0,1},{1,0},{2,3},{3,2},{4,5},{5,4},{6,7},{7,6},{8,9},{9,8},{10,11... | collective-permute-start | bytes 4718600 | tf_op jit(solution)/shard_map/ppermute | solution.py:694
  102.6 16.1 %copy-start.2 = (s32[5]{0:T(128)}, s32[5]{0:T(128)S(1)}, u32[]{:S(2)}) copy-start(s32[5]{0:T(128)S(1)} %stack.69.info) | copy-start | bytes 64
  103.3 2.0 copy-start.1
  309.4 112.2 %copy-start.3 = (s32[5]{0:T(128)S(1)}, s32[5]{0:T(128)}, u32[]{:S(2)}) copy-start(s32[5]{0:T(128)} %copy-done.2) | copy-start | bytes 64
  445.4 379.5 %reduce-scatter.5.cloned.1.call-start = ((), (), s32[]{:S(2)}) async-start(), calls=%async_computation.3 | async-start | bytes 11354112 | tf_op jit(solution)/shard_map/reduce_scatter | solution.py:782
  445.9 11.8 %copy-start.5 = (bf16[2048,768]{1,0:T(8,128)(2,1)S(1)}, bf16[2048,768]{1,0:T(8,128)(2,1)}, u32[]{:S(2)}) copy-start(bf16[2048,768]{1,0:T(8,128)(2,1)} %get-tuple-element.31) | copy-start | bytes 9437188
  457.6 38.2 %collective-permute-start.3 = (bf16[1024,768]{1,0:T(8,128)(2,1)}, bf16[1024,768]{1,0:T(8,128)(2,1)}, u32[]{:S(2)}, u32[]{:S(2)}) collective-permute-start(bf16[1024,768]{1,0:T(8,128)(2,1)} %tail_other.1), channel_id=1, source_target_pairs={{1,0},{0,1},{3,2},{2,3},{5,4},{4,5},{7,6},{6,7},{9,8},{8,9},{11,10... | collective-permute-start | bytes 4718600 | tf_op jit(solution)/shard_map/ppermute | solution.py:694
  459.6 40.8 %collective-permute-start.2 = (bf16[1024,768]{1,0:T(8,128)(2,1)}, bf16[1024,768]{1,0:T(8,128)(2,1)}, u32[]{:S(2)}, u32[]{:S(2)}) collective-permute-start(bf16[1024,768]{1,0:T(8,128)(2,1)} %get-tuple-element.51), channel_id=1, source_target_pairs={{1,0},{0,1},{3,2},{2,3},{5,4},{4,5},{7,6},{6,7},{9,8},{8,9},{11,10... | collective-permute-start | bytes 4718600 | tf_op jit(solution)/shard_map/ppermute | solution.py:694
  497.5 2.9 copy-start.4
Sparse Core Ops, SparseCore 0:
  11.5 69.1 all-gather.7
  83.7 88.0 all-gather.9
  445.5 231.0 reduce-scatter.2
  682.4 142.3 reduce-scatter.4

commit v2 on v1

v2 whole, which is shorter than its diff:
```python
import functools

import jax
import jax.numpy as jnp
from jax import lax
from jax.experimental import pallas as pl
from jax.experimental.pallas import tpu as pltpu
from jax.sharding import PartitionSpec as P

HEADS = 12
HDIM = 64
PAIR = 2 * HDIM
LOG2E = 1.4426950408889634
BF16 = jnp.bfloat16
F32 = jnp.float32


def live_rows(shape, axis, start, length, shift, span):
    rows = shape[axis]
    step = min(rows, span)
    parts = []
    for at in range(0, rows, step):
        first = start + at
        base = (first // span) * span
        sizes = list(shape)
        sizes[axis] = step
        turned = lax.broadcasted_iota(jnp.int32, tuple(sizes), axis) + (first - base + shift)
        turned = jnp.where(turned >= span, turned - span, turned)
        parts.append(turned < length - base)
    return parts[0] if len(parts) == 1 else jnp.concatenate(parts, axis)


def chunk_of(rows):
    return min(1024, rows // 2)


def segments(rows, size):
    for at in range(0, rows, size):
        for h in range(2):
            yield h, slice(at, at + size), slice(2 * at + h * size, 2 * at + (h + 1) * size)


def beside(part, h):
    blank = jnp.zeros_like(part)
    return jnp.concatenate([part, blank] if h == 0 else [blank, part], 0)


def head_rows(h):
    return slice(h * HDIM, (h + 1) * HDIM)


def attend_kernel(
    info, q_ref, k_ref, v_ref, out_ref, p_ref, sum_ref, keys, vals, ques, bound, turned, *, chunk, across, span
):
    pos = pl.program_id(1)
    kv = k_ref.shape[0]
    size, width = out_ref.shape[0], p_ref.shape[2]
    factor = HDIM**-0.5 * LOG2E

    @pl.when(pos == 0)
    def prepare():
        live = live_rows((kv, PAIR), 0, 0, info[0], info[1], span)
        kept = jnp.where(live, k_ref[...], jnp.zeros((), BF16))
        keys[...] = kept
        vals[0:PAIR, :] = jnp.where(live, v_ref[...], jnp.zeros((), BF16)).T
        vals[PAIR:, :] = live_rows((16, kv), 1, 0, info[0], info[1], span).astype(BF16)
        turned_q = q_ref[...].T
        squares = kept.astype(F32)
        squares = (squares * squares).astype(BF16)
        half = lambda axis: lax.broadcasted_iota(jnp.int32, (PAIR, PAIR), axis) // HDIM
        sizes = jnp.dot(squares, (half(0) == half(1)).astype(BF16), preferred_element_type=F32)
        largest = jnp.max(sizes, axis=0, keepdims=True)
        tops = [jnp.max(largest[:, head_rows(h)], axis=1, keepdims=True) for h in range(2)]
        for h, queries, cols in segments(q_ref.shape[0], size):
            mine = turned_q[head_rows(h), queries]
            ques[:, cols] = beside(mine, h)
            sharp = mine.astype(F32)
            reach = jnp.sum(sharp * sharp, axis=0, keepdims=True)
            bound[:, cols] = jnp.sqrt(reach * tops[h] * 1.03) * factor

    cols = pl.ds(pl.multiple_of(pos * width, width), width)

    def weigh(peak):
        for start in range(0, width, across):
            own = slice(start, start + across)
            query = ques[:, pl.ds(pl.multiple_of(pos * width + start, across), across)]
            for at in range(0, kv, chunk):
                rows = slice(at, at + chunk)
                scores = jnp.dot(keys[rows, :], query, preferred_element_type=F32)
                p_ref[0, rows, own] = jnp.exp2(scores * factor - peak[:, own]).astype(BF16)
        total = jnp.dot(vals[...], p_ref[0], preferred_element_type=F32)
        sums = total[PAIR : PAIR + 1, :]
        sum_ref[0] = sums
        for h in range(2):
            own = slice(h * size, (h + 1) * size)
            turned[head_rows(h), :] = total[head_rows(h), own] / sums[:, own]
        return jnp.min(sums)

    def exact_peak():
        query = ques[:, cols]

        def largest(at, peak):
            rows = pl.ds(pl.multiple_of(at * chunk, chunk), chunk)
            scores = jnp.dot(keys[rows, :], query, preferred_element_type=F32)
            live = live_rows((chunk, width), 0, at * chunk, info[0], info[1], span)
            return jnp.maximum(peak, jnp.max(jnp.where(live, scores, -1e30), axis=0, keepdims=True))

        return lax.fori_loop(0, kv // chunk, largest, jnp.full((1, width), -1e30, F32)) * factor

    lowest = weigh(bound[:, cols])

    @pl.when(jnp.logical_not(lowest > 2.0**-70))
    def again():
        weigh(exact_peak())

    out_ref[...] = turned[...].T.astype(BF16)


def attend(info, q_from, k_from, v_from, span):
    (queries, q_at), (keys, k_at), (values, v_at) = q_from, k_from, v_from
    rows, kv = queries.shape[0], keys.shape[0]
    size = chunk_of(rows)
    pairs = HEADS // 2
    return pl.pallas_call(
        functools.partial(
            attend_kernel, chunk=min(256, kv), across=min(256, 2 * size), span=span
        ),
        out_shape=(
            jax.ShapeDtypeStruct((rows, HEADS * HDIM), BF16),
            jax.ShapeDtypeStruct((pairs, kv, 2 * rows), BF16),
            jax.ShapeDtypeStruct((pairs, 1, 2 * rows), F32),
        ),
        grid_spec=pltpu.PrefetchScalarGridSpec(
            num_scalar_prefetch=1,
            grid=(pairs, rows // size),
            in_specs=[
                pl.BlockSpec((rows, PAIR), lambda j, c, s: (0, q_at + j)),
                pl.BlockSpec((kv, PAIR), lambda j, c, s: (0, k_at + j)),
                pl.BlockSpec((kv, PAIR), lambda j, c, s: (0, v_at + j)),
            ],
            out_specs=(
                pl.BlockSpec((size, PAIR), lambda j, c, s: (c, j)),
                pl.BlockSpec((1, kv, 2 * size), lambda j, c, s: (j, 0, c)),
                pl.BlockSpec((1, 1, 2 * size), lambda j, c, s: (j, 0, c)),
            ),
            scratch_shapes=[
                pltpu.VMEM((kv, PAIR), BF16),
                pltpu.VMEM((PAIR + 16, kv), BF16),
                pltpu.VMEM((PAIR, 2 * rows), BF16),
                pltpu.VMEM((1, 2 * rows), F32),
                pltpu.VMEM((PAIR, size), F32),
            ],
        ),
        compiler_params=pltpu.CompilerParams(vmem_limit_bytes=60 * 2**20),
        name="attend",
    )(info, queries, keys, values)


def attend_back_kernel(
    info,
    units,
    q_ref,
    k_ref,
    v_ref,
    g_ref,
    ctx_ref,
    sum_ref,
    p_ref,
    *rest,
    chunk,
    size,
    span,
    more,
    extra,
):
    before, rest = (rest[:3], rest[3:]) if more else (None, rest)
    rest = rest[extra:]
    gq_ref, gk_ref, gv_ref, keys, grads, grads_up, ques_up, delta, low, total, key_sum, value_sum = rest
    step = pl.program_id(1)
    kv, rows = k_ref.shape[0], q_ref.shape[0]
    block, part = p_ref.shape[1:]
    scale = HDIM**-0.5

    @pl.when(step == 0)
    def prepare():
        live = live_rows((kv, PAIR), 0, 0, info[0], info[1], span)
        keys[...] = jnp.where(live, k_ref[...], jnp.zeros((), BF16)).T
        turned = g_ref[...].T.astype(F32)
        dots = turned * ctx_ref[...].T.astype(F32)
        for h, queries, cols in segments(rows, size):
            inverse = 1.0 / sum_ref[0, :, cols]
            own = head_rows(h)
            delta[:, cols] = jnp.sum(dots[own, queries], axis=0, keepdims=True) * inverse
            shared = beside((turned[own, queries] * inverse).astype(BF16), h)
            grads[:, cols] = shared
            grads_up[cols, :] = shared.T
            lane = lax.broadcasted_iota(jnp.int32, (queries.stop - queries.start, PAIR), 1)
            ques_up[cols, :] = jnp.where(lane // HDIM == h, q_ref[queries, :], jnp.zeros((), BF16))
        for held in (total, key_sum, value_sum):
            held[...] = jnp.zeros_like(held)

    here = pl.ds(pl.multiple_of(units[0, step] * block, block), block)
    there = pl.multiple_of(units[1, step] * part, part)
    cols = pl.ds(there, part)
    values = v_ref[here, :]
    for start in range(0, part, chunk):
        own = slice(start, start + chunk)
        from_all = pl.ds(there + start, chunk)
        change = jnp.dot(values, grads[:, from_all], preferred_element_type=F32)
        low[:, own] = (p_ref[0, :, own].astype(F32) * (change - delta[:, from_all])).astype(BF16)
    value_sum[here, :] += jnp.dot(p_ref[0], grads_up[cols, :], preferred_element_type=F32)
    key_sum[here, :] += jnp.dot(low[...], ques_up[cols, :], preferred_element_type=F32)
    total[:, cols] += jnp.dot(keys[:, here], low[...], preferred_element_type=F32)

    @pl.when(step == pl.num_programs(1) - 1)
    def finish():
        live = live_rows((kv, PAIR), 0, 0, info[0], info[1], span)
        zero = jnp.zeros((), F32)
        found = [jnp.where(live, key_sum[...] * scale, zero), jnp.where(live, value_sum[...], zero)]
        for t, (ref, value) in enumerate(zip((gk_ref, gv_ref), found)):
            if more:
                value += before[t + 1][...].astype(F32)
            ref[...] = value.astype(BF16)
        parts = [[], []]
        for h, queries, cols in segments(rows, size):
            parts[h].append(total[head_rows(h), cols])
        value = (jnp.concatenate([jnp.concatenate(p, 1) for p in parts], 0) * scale).T
        if more:
            value += before[0][...].astype(F32)
        gq_ref[...] = value.astype(BF16)


def attend_back(info, q_from, k_from, v_from, grad, context, sums, probs, span, units, before, events=()):
    (queries, q_at), (keys, k_at), (values, v_at) = q_from, k_from, v_from
    rows, kv = queries.shape[0], keys.shape[0]
    pairs = HEADS // 2
    wide = HEADS * HDIM
    more = before is not None
    block, part, size = min(1024, kv), rows, chunk_of(rows)
    cut = 2 if more else 1
    rows, kv = rows // cut, kv // cut
    out_rows = [rows, kv, kv]
    units = jnp.array(list(zip(*units)), jnp.int32)
    col = lambda height, at=0: pl.BlockSpec((height, PAIR), lambda j, c, s, u: (0, at + j))
    return pl.pallas_call(
        functools.partial(
            attend_back_kernel,
            chunk=min(512, part),
            size=size,
            span=span,
            more=more,
            extra=len(events),
        ),
        out_shape=tuple(jax.ShapeDtypeStruct((height, wide), BF16) for height in out_rows),
        grid_spec=pltpu.PrefetchScalarGridSpec(
            num_scalar_prefetch=2,
            grid=(pairs, units.shape[1]),
            in_specs=[
                col(rows, q_at),
                col(kv, k_at),
                col(kv, v_at),
                col(rows),
                col(rows),
                pl.BlockSpec((1, 1, 2 * rows), lambda j, c, s, u: (j, 0, 0)),
                pl.BlockSpec((1, block, part), lambda j, c, s, u: (j, u[0, c], u[1, c])),
            ]
            + ([col(height) for height in out_rows] if more else [])
            + any_specs(events),
            out_specs=tuple(col(height) for height in out_rows),
            scratch_shapes=[
                pltpu.VMEM((PAIR, kv), BF16),
                pltpu.VMEM((PAIR, 2 * rows), BF16),
                pltpu.VMEM((2 * rows, PAIR), BF16),
                pltpu.VMEM((2 * rows, PAIR), BF16),
                pltpu.VMEM((1, 2 * rows), F32),
                pltpu.VMEM((block, part), BF16),
                pltpu.VMEM((PAIR, 2 * rows), F32),
                pltpu.VMEM((kv, PAIR), F32),
                pltpu.VMEM((kv, PAIR), F32),
            ],
        ),
        compiler_params=pltpu.CompilerParams(vmem_limit_bytes=60 * 2**20),
        name="attend_back_last" if more else "attend_back",
    )(info, units, queries, keys, values, grad, context, sums, probs, *(before or ()), *events)


def rows_of(kept_ref, other_ref, step, split):
    return jnp.where(step < split, kept_ref[0], other_ref[...])


def project(rows, weight):
    return jnp.dot(rows, weight, preferred_element_type=F32)


def project_back(grads, weight):
    return lax.dot_general(grads, weight, (((1,), (1,)), ((), ())), preferred_element_type=F32)


def weight_grad(rows, grads):
    return lax.dot_general(rows, grads, (((0,), (0,)), ((), ())), preferred_element_type=F32)


def run_all(copies):
    for copy in copies:
        copy.start()
    return copies


def wait_all(copies):
    for copy in copies:
        copy.wait()


class Pieces:
    def __init__(self, shape, mesh_shape, bundles):
        self.r, self.c = shape
        self.m, self.n = mesh_shape
        self.bundles = bundles
        self.slots = self.m * self.n

    def place(self, masks, slot, info):
        if masks is None:
            return slot // self.n, lax.rem(slot, self.n)
        return info[5] ^ (masks[slot] // self.n), info[6] ^ (masks[slot] % self.n)

    def copies(self, refs, mats, sems, info, out):
        found = [[] for _ in mats]
        r, c = self.r, self.c
        count = 0
        for (masks, members), ref in zip(self.bundles, refs):
            for slot in range(self.slots if masks is None else len(masks)):
                j, i = self.place(masks, slot, info)
                at = 0
                for t in members:
                    mat = mats[t]
                    tall = mat.shape[0] // (self.m * r)
                    wide = mat.shape[1] // (self.n * c)
                    for w in range(wide):
                        if isinstance(ref, (tuple, list)):
                            each = self.slots // len(ref)
                            block = ref[slot // each].at[slot % each, pl.ds(at, tall * r), :]
                        else:
                            block = ref.at[slot, pl.ds(at, tall * r), :]
                        down = pl.multiple_of(j * (tall * r), tall * r)
                        side = pl.multiple_of((i * wide + w) * c, c)
                        place = mat.at[pl.ds(down, tall * r), pl.ds(side, c)]
                        at += tall * r
                        pair = (place, block) if out else (block, place)
                        found[t].append(pltpu.make_async_copy(*pair, sems.at[count]))
                        count += 1
        return found

    def count(self):
        return 9 * self.slots


def any_specs(arrays):
    return [pl.BlockSpec(memory_space=pl.ANY)] * len(arrays)


def queries_kernel(info, kept_ref, other_ref, bias_ref, *rest, split, grid_of):
    count = len(grid_of.bundles)
    packed, (out_ref, mat_q, mat_k, mat_v, sems) = rest[:count], rest[count:]
    step = pl.program_id(0)
    mats = [mat_q, mat_k, mat_v]

    @pl.when(step == 0)
    def load():
        loads = grid_of.copies(packed, mats, sems, info, False)
        for group in loads:
            run_all(group)
        for group in loads:
            wait_all(group)

    rows = rows_of(kept_ref, other_ref, step, split)
    width = mat_q.shape[1]
    for t, mat in enumerate(mats):
        cols = slice(t * width, (t + 1) * width)
        out_ref[:, cols] = (project(rows, mat[...]) + bias_ref[:, cols]).astype(BF16)


def split_specs(kept_at, tile, split, width):
    return [
        pl.BlockSpec((1, tile, width), lambda i, s: (s[kept_at], jnp.minimum(i, split - 1), 0)),
        pl.BlockSpec((tile, width), lambda i, s: (jnp.maximum(i - split, 0), 0)),
    ]


def whole_spec(shape):
    return pl.BlockSpec(shape, lambda i, s: (0,) * len(shape))


def queries_keys_values(info, kept, other, weights, bias):
    block_len, width = other.shape
    tile = min(512, block_len)
    split = block_len // tile
    mat = jax.ShapeDtypeStruct((width, width), BF16)
    return pl.pallas_call(
        functools.partial(queries_kernel, split=split, grid_of=weights.grid_of),
        out_shape=(jax.ShapeDtypeStruct((2 * block_len, 3 * width), BF16), mat, mat, mat),
        grid_spec=pltpu.PrefetchScalarGridSpec(
            num_scalar_prefetch=1,
            grid=(2 * split,),
            in_specs=split_specs(2, tile, split, width)
            + [whole_spec(bias.shape)]
            + any_specs(weights.packed),
            out_specs=(pl.BlockSpec((tile, 3 * width), lambda i, s: (i, 0)),)
            + (whole_spec(mat.shape),) * 3,
            scratch_shapes=[pltpu.SemaphoreType.DMA((weights.grid_of.count(),))],
        ),
        compiler_params=pltpu.CompilerParams(vmem_limit_bytes=60 * 2**20),
        name="queries",
    )(info, kept, other, bias, *weights.packed)


def normal(values):
    middle = jnp.mean(values, axis=-1, keepdims=True)
    centered = values - middle
    spread = jnp.mean(centered * centered, axis=-1, keepdims=True)
    inverse = lax.rsqrt(spread + 1e-12)
    return centered * inverse, inverse


def normal_back(grad, unit, inverse, gain):
    scaled = grad * gain
    mean = jnp.mean(scaled, axis=-1, keepdims=True)
    along = jnp.mean(scaled * unit, axis=-1, keepdims=True)
    return (scaled - mean - unit * along) * inverse


def gelu_pair(u):
    phi = 0.5 + 0.5 * lax.erf(0.7071067811865476 * u)
    bell = jnp.exp2((-0.5 * LOG2E) * (u * u))
    return u * phi, phi + (0.3989422804014327 * u) * bell


def add_rows(total, at, values):
    total[at : at + 1, 0 : values.shape[1]] += jnp.sum(values, axis=0, keepdims=True)


def middle_kernel(
    info,
    hid_kept,
    hid_other,
    cot_kept,
    cot_other,
    ctx_ref,
    cls_ref,
    vec_ref,
    inner_bias,
    packed,
    layer_kept,
    layer_other,
    top_ref,
    grad_ctx_ref,
    resid_ref,
    sums_ref,
    mat_out,
    mat_inner,
    mat_outer,
    acc_out,
    acc_inner,
    acc_outer,
    totals,
    active,
    slope,
    low,
    vec_low,
    sems,
    vec_sems,
    *,
    split,
    grid_of,
    chunk,
):
    step = pl.program_id(0)
    last = pl.num_programs(0) - 1
    mats = [mat_out, mat_inner, mat_outer]
    tile, width = ctx_ref.shape
    ff = mat_inner.shape[1]
    loads = grid_of.copies([packed], mats, sems, info, False)

    @pl.when(step == 0)
    def start():
        for group in loads:
            run_all(group)
        for acc in (acc_out, acc_inner, acc_outer, totals):
            acc[...] = jnp.zeros_like(acc)
        wait_all(loads[0])

    bias_out, gain_one, shift_one, bias_outer, gain_two, shift_two = [
        vec_ref[t : t + 1, :] for t in range(6)
    ]
    hidden = rows_of(hid_kept, hid_other, step, split).astype(F32)
    context = ctx_ref[...]
    unit_one, inverse_one = normal(hidden + project(context, mat_out[...]) + bias_out)
    normed = unit_one * gain_one + shift_one
    normed_low = normed.astype(BF16)

    @pl.when(step == 0)
    def more():
        wait_all(loads[1])
        wait_all(loads[2])

    for at in range(0, ff, chunk):
        cols = slice(at, at + chunk)
        inner = project(normed_low, mat_inner[:, cols]) + inner_bias[:, cols]
        value, change = gelu_pair(inner)
        active[:, cols] = value.astype(BF16)
        slope[:, cols] = change.astype(BF16)
    unit_two, inverse_two = normal(normed + project(active[...], mat_outer[...]) + bias_outer)
    layer = (unit_two * gain_two + shift_two).astype(BF16)

    @pl.when(step < split)
    def kept():
        layer_kept[0] = layer

    @pl.when(step >= split)
    def other():
        layer_other[...] = layer

    @pl.when(step * tile == info[1])
    def top():
        top_ref[...] = layer[0:16, :]


    row = step * tile + lax.broadcasted_iota(jnp.int32, (tile, width), 0)
    grad_result = rows_of(cot_kept, cot_other, step, split).astype(F32)
    grad_result += jnp.where(row == info[4], cls_ref[...], 0.0)
    add_rows(totals, 4, grad_result * unit_two)
    add_rows(totals, 5, grad_result)
    grad_resid_two = normal_back(grad_result, unit_two, inverse_two, gain_two)
    grad_outer = grad_resid_two.astype(BF16)
    add_rows(totals, 3, grad_outer.astype(F32))
    for at in range(0, ff, chunk):
        cols = slice(at, at + chunk)
        grad_inner = project_back(grad_outer, mat_outer[cols, :]) * slope[:, cols].astype(F32)
        low[:, cols] = grad_inner.astype(BF16)
        totals[8:9, cols] += jnp.sum(grad_inner, axis=0, keepdims=True)
        acc_outer[cols, :] += weight_grad(active[:, cols], grad_outer)
    grad_normed = grad_resid_two + project_back(low[...], mat_inner[...])
    for at in range(0, ff, chunk):
        cols = slice(at, at + chunk)
        acc_inner[:, cols] += weight_grad(normed_low, low[:, cols])
    add_rows(totals, 1, grad_normed * unit_one)
    add_rows(totals, 2, grad_normed)
    grad_resid_one = normal_back(grad_normed, unit_one, inverse_one, gain_one)
    resid_ref[...] = grad_resid_one
    grad_attn = grad_resid_one.astype(BF16)
    add_rows(totals, 0, grad_attn.astype(F32))
    acc_out[...] += weight_grad(context, grad_attn)
    grad_ctx_ref[...] = project_back(grad_attn, mat_out[...]).astype(BF16)

    @pl.when(step == last)
    def finish():
        r, c, m, n = grid_of.r, grid_of.c, grid_of.m, grid_of.n
        stores = grid_of.copies([sums_ref], mats, sems, info, True)
        for mat, acc, group in zip(mats, (acc_out, acc_inner, acc_outer), stores):
            mat[...] = acc[...].astype(BF16)
            run_all(group)
        vec_low[...] = jnp.zeros_like(vec_low)
        for i in range(n):
            for t in range(6):
                vec_low[i, t : t + 1, :] = totals[t : t + 1, i * c : (i + 1) * c]
            wide = ff // (n * c)
            for t in range(wide):
                at = (i * wide + t) * c
                vec_low[i, 6 + t : 7 + t, :] = totals[8:9, at : at + c]
        tails = []
        vec_bits = vec_low[...].astype(BF16)
        for i in range(n):
            active[16 * i : 16 * i + 16, 0:c] = vec_bits[i]
        for j in range(m):
            for i in range(n):
                tails.append(
                    pltpu.make_async_copy(
                        active.at[pl.ds(16 * i, 16), pl.ds(0, c)],
                        sums_ref.at[j * n + i, pl.ds(9 * r, 16), :],
                        vec_sems.at[j * n + i],
                    )
                )
        run_all(tails)
        for group in stores:
            wait_all(group)
        wait_all(tails)


def kept_spec(tile, split, width):
    return pl.BlockSpec((1, tile, width), lambda i, s: (s[2], jnp.minimum(i, split - 1), 0))


def other_spec(tile, split, width):
    return pl.BlockSpec((tile, width), lambda i, s: (jnp.maximum(i - split, 0), 0))


def middle(info, hidden, cots, context, cls_row, weights, vectors, inner_bias):
    block_len, width = hidden[1].shape
    grid_of = weights.grid_of
    ff = inner_bias.shape[1]
    tile = min(256, block_len)
    split = block_len // tile
    row_spec = pl.BlockSpec((tile, width), lambda i, s: (i, 0))
    return pl.pallas_call(
        functools.partial(middle_kernel, split=split, grid_of=grid_of, chunk=768),
        out_shape=(
            jax.ShapeDtypeStruct(hidden[0].shape, BF16),
            jax.ShapeDtypeStruct((block_len, width), BF16),
            jax.ShapeDtypeStruct((16, width), BF16),
            jax.ShapeDtypeStruct((2 * block_len, width), BF16),
            jax.ShapeDtypeStruct((2 * block_len, width), F32),
            jax.ShapeDtypeStruct((grid_of.slots, 9 * grid_of.r + 16, grid_of.c), BF16),
        ),
        grid_spec=pltpu.PrefetchScalarGridSpec(
            num_scalar_prefetch=1,
            grid=(2 * split,),
            in_specs=split_specs(2, tile, split, width)
            + split_specs(2, tile, split, width)
            + [
                row_spec,
                whole_spec(cls_row.shape),
                whole_spec(vectors.shape),
                whole_spec(inner_bias.shape),
                pl.BlockSpec(memory_space=pl.ANY),
            ],
            out_specs=(
                kept_spec(tile, split, width),
                other_spec(tile, split, width),
                whole_spec((16, width)),
                row_spec,
                row_spec,
                pl.BlockSpec(memory_space=pl.ANY),
            ),
            scratch_shapes=[
                pltpu.VMEM((width, width), BF16),
                pltpu.VMEM((width, ff), BF16),
                pltpu.VMEM((ff, width), BF16),
                pltpu.VMEM((width, width), F32),
                pltpu.VMEM((width, ff), F32),
                pltpu.VMEM((ff, width), F32),
                pltpu.VMEM((16, ff), F32),
                pltpu.VMEM((tile, ff), BF16),
                pltpu.VMEM((tile, ff), BF16),
                pltpu.VMEM((tile, ff), BF16),
                pltpu.VMEM((grid_of.n, 16, grid_of.c), F32),
                pltpu.SemaphoreType.DMA((grid_of.count(),)),
                pltpu.SemaphoreType.DMA((grid_of.slots,)),
            ],
        ),
        compiler_params=pltpu.CompilerParams(vmem_limit_bytes=60 * 2**20),
        name="middle",
    )(info, *hidden, *cots, context, cls_row, vectors, inner_bias, *weights.packed)


def input_grad_kernel(info, gq_ref, gk_ref, gv_ref, resid_ref, mat_q, mat_k, mat_v, grad_ref, *, kept):
    total = resid_ref[...]
    for ref, mat in zip((gq_ref, gk_ref, gv_ref), (mat_q, mat_k, mat_v)):
        total += project_back(ref[...], mat[...])
    if kept:
        grad_ref[0] = total.astype(grad_ref.dtype)
    else:
        grad_ref[...] = total.astype(grad_ref.dtype)


def input_grad(info, grads, resid, mats, out_shape, dtype, kept):
    rows, width = resid.shape
    block_len = rows // 2
    tile = min(512, block_len)
    split = block_len // tile
    off = 0 if kept else split
    spec = pl.BlockSpec((tile, width), lambda i, s: (i + off, 0))
    place = kept_spec(tile, split, width) if kept else other_spec(tile, 0, width)
    return pl.pallas_call(
        functools.partial(input_grad_kernel, kept=kept),
        out_shape=jax.ShapeDtypeStruct(out_shape, dtype),
        grid_spec=pltpu.PrefetchScalarGridSpec(
            num_scalar_prefetch=1,
            grid=(split,),
            in_specs=[spec] * 4 + [whole_spec(mat.shape) for mat in mats],
            out_specs=place,
        ),
        compiler_params=pltpu.CompilerParams(vmem_limit_bytes=60 * 2**20),
        name="input_grad_kept" if kept else "input_grad_other",
    )(info, *grads, resid, *mats)


def head_grads_kernel(info, hid_kept, hid_other, *rest, split, grid_of, outs, extra):
    kept, other, rest = rest[:3], rest[3:6], rest[6 + extra :]
    sums, (acc, mat_q, mat_k, mat_v, totals, vec_low, sems, vec_sems) = rest[:outs], rest[outs:]
    mats = [mat_q, mat_k, mat_v]
    step = pl.program_id(0)

    @pl.when(step == 0)
    def clear():
        acc[...] = jnp.zeros_like(acc)
        totals[...] = jnp.zeros_like(totals)

    rows = rows_of(hid_kept, hid_other, step, split)
    grads = [jnp.where(step < split, a[...], b[...]) for a, b in zip(kept, other)]
    for t, grad in enumerate(grads):
        acc[t] += weight_grad(rows, grad)
    add_rows(totals, 0, grads[0].astype(F32))
    add_rows(totals, 1, grads[2].astype(F32))

    @pl.when(step == pl.num_programs(0) - 1)
    def finish():
        r, c, n = grid_of.r, grid_of.c, grid_of.n
        ((masks, _),) = grid_of.bundles
        stores = grid_of.copies([list(sums)], mats, sems, info, True)
        for t, mat in enumerate(mats):
            mat[...] = acc[t].astype(BF16)
            run_all(stores[t])
        for i in range(n):
            part = jnp.concatenate([totals[0:2, i * c : (i + 1) * c], jnp.zeros((14, c), F32)], 0)
            vec_low[i] = part.astype(BF16)
        tails = []
        each = grid_of.slots // outs
        for slot in range(grid_of.slots):
            j, i = grid_of.place(masks, slot, info)
            place = sums[slot // each].at[slot % each, pl.ds(3 * r, 16), :]
            tails.append(pltpu.make_async_copy(vec_low.at[i], place, vec_sems.at[slot]))
        run_all(tails)
        for group in stores:
            wait_all(group)
        wait_all(tails)


def head_grads(info, hidden, kept, other, grid_of, outs, events=()):
    block_len, width = hidden[1].shape
    tile = min(512, block_len)
    split = block_len // tile
    last = other[0].shape[0] // tile - split
    kept_rows = pl.BlockSpec((tile, width), lambda i, s: (jnp.minimum(i, split - 1), 0))
    other_rows = pl.BlockSpec((tile, width), lambda i, s: (jnp.maximum(i, split), 0))
    block = (grid_of.slots // outs, 3 * grid_of.r + 16, grid_of.c)
    return pl.pallas_call(
        functools.partial(
            head_grads_kernel, split=split, grid_of=grid_of, outs=outs, extra=len(events)
        ),
        out_shape=(jax.ShapeDtypeStruct(block, BF16),) * outs,
        grid_spec=pltpu.PrefetchScalarGridSpec(
            num_scalar_prefetch=1,
            grid=(2 * split,),
            in_specs=split_specs(2, tile, split, width) + [kept_rows] * 3 + [other_rows] * 3 + any_specs(events),
            out_specs=(pl.BlockSpec(memory_space=pl.ANY),) * outs,
            scratch_shapes=[pltpu.VMEM((3, width, width), F32)]
            + [pltpu.VMEM((width, width), BF16)] * 3
            + [
                pltpu.VMEM((8, width), F32),
                pltpu.VMEM((grid_of.n, 16, grid_of.c), BF16),
                pltpu.SemaphoreType.DMA((grid_of.count(),)),
                pltpu.SemaphoreType.DMA((grid_of.slots,)),
            ],
        ),
        compiler_params=pltpu.CompilerParams(vmem_limit_bytes=60 * 2**20),
        name="head_grads",
    )(info, *hidden, *kept, *other, *events)


def pick_kernel(info, pair_ref, *rest):
    rest[-1][...] = pair_ref[0]


def pick_other(info, pair, events):
    _, block_len, width = pair.shape
    tile = min(512, block_len)
    return pl.pallas_call(
        pick_kernel,
        out_shape=jax.ShapeDtypeStruct((block_len, width), pair.dtype),
        grid_spec=pltpu.PrefetchScalarGridSpec(
            num_scalar_prefetch=1,
            grid=(block_len // tile,),
            in_specs=[pl.BlockSpec((1, tile, width), lambda i, s: (1 - s[2], i, 0))]
            + any_specs(events),
            out_specs=pl.BlockSpec((tile, width), lambda i, s: (i, 0)),
        ),
        compiler_params=pltpu.CompilerParams(vmem_limit_bytes=60 * 2**20),
        name="pick_other",
    )(info, pair, *events)


def pack_kernel(*refs, count):
    out = refs[-1]
    c = out.shape[1]
    at = 0
    for ref in refs[:count]:
        rows, cols = ref.shape
        for start in range(0, cols, c):
            out[at : at + rows, :] = ref[:, start : start + c]
            at += rows


def pack_after(shards, events):
    c = min(s.shape[1] for s in shards)
    rows = sum(s.size for s in shards) // c
    return pl.pallas_call(
        functools.partial(pack_kernel, count=len(shards)),
        out_shape=jax.ShapeDtypeStruct((rows, c), BF16),
        in_specs=[pl.BlockSpec(memory_space=pltpu.VMEM)] * len(shards) + any_specs(events),
        compiler_params=pltpu.CompilerParams(vmem_limit_bytes=60 * 2**20),
        name="pack",
    )(*shards, *events)


def stack_kernel(*refs, count, outs):
    at = 0
    for out in refs[-outs:]:
        rows = out.shape[1]
        for k, ref in enumerate(refs[:count]):
            out[k] = ref[at : at + rows, :]
        at += rows


def stack_rows(blocks, cuts, events):
    c = blocks[0].shape[1]
    return pl.pallas_call(
        functools.partial(stack_kernel, count=len(blocks), outs=len(cuts)),
        out_shape=tuple(jax.ShapeDtypeStruct((len(blocks), rows, c), BF16) for rows in cuts),
        in_specs=[pl.BlockSpec(memory_space=pltpu.VMEM)] * len(blocks) + any_specs(events),
        compiler_params=pltpu.CompilerParams(vmem_limit_bytes=60 * 2**20),
        name="stack_rows",
    )(*blocks, *events)


def add_kernel(*refs, count, extra):
    parts, outs = refs[:count], refs[count + extra :]
    each = outs[0].shape[0]
    for k, out in enumerate(outs):
        here = slice(k * each, (k + 1) * each)
        out[...] = sum(part[here].astype(F32) for part in parts).astype(BF16)


def add_blocks(parts, groups, events):
    shape = (parts[0].shape[0] // groups,) + parts[0].shape[1:]
    return pl.pallas_call(
        functools.partial(add_kernel, count=len(parts), extra=len(events)),
        out_shape=(jax.ShapeDtypeStruct(shape, BF16),) * groups,
        in_specs=[pl.BlockSpec(memory_space=pltpu.VMEM)] * len(parts) + any_specs(events),
        compiler_params=pltpu.CompilerParams(vmem_limit_bytes=60 * 2**20),
        name="add_blocks",
    )(*parts, *events)


def place_kernel(info, base_ref, other_ref, out_ref):
    out_ref[0] = other_ref[...].astype(out_ref.dtype)


def place_other(info, base, other):
    block_len, width = other.shape
    tile = min(512, block_len)
    return pl.pallas_call(
        place_kernel,
        out_shape=jax.ShapeDtypeStruct(base.shape, base.dtype),
        grid_spec=pltpu.PrefetchScalarGridSpec(
            num_scalar_prefetch=1,
            grid=(block_len // tile,),
            in_specs=[
                pl.BlockSpec(memory_space=pl.ANY),
                pl.BlockSpec((tile, width), lambda i, s: (i, 0)),
            ],
            out_specs=pl.BlockSpec((1, tile, width), lambda i, s: (1 - s[2], i, 0)),
        ),
        input_output_aliases={1: 0},
        compiler_params=pltpu.CompilerParams(vmem_limit_bytes=60 * 2**20),
        name="place_other",
    )(info, base, other)


def swap(block, axis, route):
    if all(a == b for a, b in route):
        return block
    return lax.ppermute(block, axis, route)


class Regroup:
    def __init__(self):
        self.n = lax.axis_size("blk")
        self.me = lax.axis_index("blk")
        self.per = self.n // 2
        self.passage = self.me // self.per
        self.part = lax.rem(self.me, 2)
        self.first = [(i, (i % 2) * self.per + i // 2) for i in range(self.n)]
        self.second = [(i, (1 - i % 2) * self.per + i // 2) for i in range(self.n)]
        self.stays = all(a == b for a, b in self.first)

    def pick(self, info, pair, events=()):
        if self.stays:
            return pick_other(info, pair, events)
        return lax.dynamic_index_in_dim(pair, 1 - self.part, 0, keepdims=False)

    def gather(self, pair, picked):
        other = swap(picked, "blk", self.second)
        if self.stays:
            return (pair, other)
        kept = lax.dynamic_index_in_dim(pair, self.part, 0, keepdims=True)
        return (swap(kept, "blk", self.first), other)

    def kept_index(self):
        return self.part if self.stays else jnp.zeros_like(self.part)

    def all_blocks(self, block):
        if self.n != 2:
            return lax.all_gather(block, "blk", axis=0)
        other = lax.ppermute(block, "blk", [(0, 1), (1, 0)])
        return jnp.where(self.me == 0, jnp.stack([block, other]), jnp.stack([other, block]))

    def send_back(self, other):
        return swap(other, "blk", [(b, a) for a, b in self.second])

    def join(self, info, kept, other):
        if self.stays:
            return place_other(info, kept, other)
        kept = swap(kept[0], "blk", [(b, a) for a, b in self.first])
        other = other.astype(kept.dtype)
        return jnp.where(self.part == 0, jnp.stack([kept, other]), jnp.stack([other, kept]))


def pack(shards):
    c = min(s.shape[1] for s in shards)
    return jnp.concatenate(
        [s[:, at : at + c] for s in shards for at in range(0, s.shape[1], c)], axis=0
    )


def unpack(block, shapes):
    c = block.shape[-1]
    found, at = [], 0
    for rows, cols in shapes:
        parts = []
        for _ in range(cols // c):
            parts.append(block[..., at : at + rows, :])
            at += rows
        found.append(jnp.concatenate(parts, axis=-1) if len(parts) > 1 else parts[0])
    return found


def exchanged(block, mask):
    both = ("batch", "blk")
    places = range(lax.axis_size("batch") * lax.axis_size("blk"))
    return lax.ppermute(block, both, [(i, i ^ mask) for i in places])


def xor_gather(block, stages):
    found, masks = block[None], [0]
    for stage in stages:
        parts = [found] + [exchanged(found, mask) for mask in stage]
        masks = masks + [held ^ mask for mask in stage for held in masks]
        found = jnp.concatenate(parts, 0)
    return found, masks


def xor_masks(stages):
    masks = [0]
    for stage in stages:
        masks = [held ^ mask for held in masks for mask in [0] + stage]
    return masks


def xor_sum(groups, stages, meanwhile):
    for at, stage in enumerate(stages):
        parts = [groups[0]] + [exchanged(g, mask) for mask, g in zip(stage, groups[1:])]
        if at == len(stages) - 1:
            return [part[0] for part in parts]
        events = meanwhile if at == len(stages) - 2 else ()
        groups = add_blocks(parts, len(stages[at + 1]) + 1, events)


class Weights:
    def __init__(self, shards, by_pairs, events=()):
        self.shapes = [s.shape for s in shards]
        self.m, self.n = lax.axis_size("batch"), lax.axis_size("blk")
        m, n = self.m, self.n
        r, c = min(s[0] for s in self.shapes), min(s[1] for s in self.shapes)
        self.fits = r % 16 == 0 and c % 128 == 0
        powers = m & (m - 1) == 0 and n & (n - 1) == 0 and m >= 8
        self.by_pairs = by_pairs and self.fits and powers
        every = list(range(len(shards)))
        if self.by_pairs:
            y, core, x = list(range(1, n)), [n], [2 * n]
            z = list(range(4 * n, m * n, 4 * n))
            near = pack_after(shards, ())
            near = [near] + [exchanged(near, mask) for mask in y]
            cut = sum(s.size for s in shards[:-1]) // c
            cuts = [cut, near[0].shape[0] - cut]
            near = stack_rows(near, cuts, events(near))
            self.packed, bundles, self.half = [], [], []
            for rows, members, order in (
                (near[0], every[:-1], [z, x]),
                (near[1], every[-1:], [x, z]),
            ):
                part, masks = xor_gather(rows, order[:1])
                self.half.append(part)
                part, more = xor_gather(part, order[1:])
                masks = [a ^ b for a in more for b in masks]
                for mask in [0] + core:
                    block = exchanged(part, mask) if mask else part
                    self.packed.append(block.reshape(-1, *rows.shape[1:]))
                    bundles.append(([a ^ b ^ mask for a in masks for b in [0] + y], members))
            self.grid_of = Pieces((r, c), (m, n), bundles)
            self.stages = [core, [a ^ b for a in [0] + x for b in [0] + y][1:], z]
            self.sums_of = Pieces((r, c), (m, n), [(xor_masks(self.stages), every)])
            return
        if callable(events):
            events = ()
        packed = pack_after(shards, events) if self.fits else pack(shards)
        packed = lax.all_gather(packed, ("batch", "blk"), axis=0)
        if self.fits:
            self.grid_of = Pieces((r, c), (m, n), [(None, every)])
            self.packed = [packed]
        else:
            self.grid_of = Pieces((r * m, c * n), (1, 1), [(None, every)])
            whole = []
            for part in unpack(packed, self.shapes):
                rows, cols = part.shape[1:]
                part = part.reshape(m, n, rows, cols).transpose(0, 2, 1, 3)
                whole.append(part.reshape(m * rows, n * cols))
            self.packed = [pack(whole)[None]]
        self.sums_of = self.grid_of

    def halfway(self):
        return tuple(self.half) if self.by_pairs else ()

    def scatter(self, sums, meanwhile=()):
        extra = 16
        if self.by_pairs:
            return finish_sums(xor_sum(sums, self.stages, meanwhile), self.shapes)
        (sums,) = sums
        if not self.fits:
            rows = sums.shape[1] - extra
            wide = [(a * self.m, b * self.n) for a, b in self.shapes]
            parts = []
            for part in unpack(sums[0, :rows], wide):
                a, b = part.shape[0] // self.m, part.shape[1] // self.n
                part = part.reshape(self.m, a, self.n, b).transpose(0, 2, 1, 3)
                parts.append(part.reshape(self.m * self.n, a, b))
            c = min(s[1] for s in self.shapes)
            blocks = jnp.stack([pack([p[d] for p in parts]) for d in range(self.m * self.n)])
            vecs = sums[0, rows:].reshape(extra, self.n, c).transpose(1, 0, 2)
            vecs = jnp.broadcast_to(vecs[None], (self.m, self.n, extra, c))
            sums = jnp.concatenate([blocks, vecs.reshape(self.m * self.n, extra, c)], axis=1)
        height, c = sums.shape[1:]
        own = lax.psum_scatter(
            sums.reshape(-1, c), ("batch", "blk"), scatter_dimension=0, tiled=True
        )
        return finish_sums([own], self.shapes)


def finish_kernel(*refs, count):
    parts, outs = refs[:count], refs[count:]
    at = 0
    for out in outs:
        rows, cols = out.shape
        c = parts[0].shape[1]
        for start in range(0, cols, c):
            here = slice(at, at + rows)
            out[:, start : start + c] = sum(part[here, :].astype(F32) for part in parts)
            at += rows


def finish_sums(parts, shapes):
    height, c = parts[0].shape
    used = sum(a * b for a, b in shapes) // c
    shapes = list(shapes) + [(height - used, c)]
    if used % 16:
        total = sum(part.astype(F32) for part in parts)
        return [*unpack(total[:used], shapes[:-1]), total[used:]]
    return pl.pallas_call(
        functools.partial(finish_kernel, count=len(parts)),
        out_shape=tuple(jax.ShapeDtypeStruct(shape, F32) for shape in shapes),
        compiler_params=pltpu.CompilerParams(vmem_limit_bytes=60 * 2**20),
        name="finish_sums",
    )(*parts)


def on_device(
    hidden_in,
    lengths,
    cot_out,
    cot_cls,
    w_query,
    w_key,
    w_value,
    w_out,
    w_inner,
    w_outer,
    b_query,
    b_value,
    b_out,
    norm1_gain,
    norm1_shift,
    b_inner,
    b_outer,
    norm2_gain,
    norm2_shift,
):
    plan = Regroup()
    groups, block_len, width = hidden_in.shape
    span = groups * block_len
    per = plan.per
    fleets = [[i * per + j for j in range(per)] for i in range(2)]
    first_row = plan.passage * block_len
    owner = lax.rem(plan.me, per) == 0

    length = lax.dynamic_index_in_dim(lengths, plan.passage, 0, keepdims=False)
    info = jnp.stack(
        [
            length,
            first_row,
            plan.kept_index(),
            plan.kept_index(),
            jnp.where(owner, first_row, -1),
            lax.axis_index("batch"),
            plan.me,
        ]
    ).astype(jnp.int32)

    share = width // plan.n
    narrow = jnp.stack(
        [b_query, b_value, b_out, norm1_gain, norm1_shift, b_outer, norm2_gain, norm2_shift]
    )
    vec_all = plan.all_blocks(jnp.concatenate([narrow, b_inner.reshape(-1, share)], 0)).astype(F32)
    narrow = vec_all[:, :8].transpose(1, 0, 2).reshape(8, width)
    bias_inner = vec_all[:, 8:].reshape(1, -1)
    bias_heads = jnp.concatenate([narrow[0:1], jnp.zeros_like(narrow[0:1]), narrow[1:2]], 1)

    picked = []

    def pick_hidden(near):
        picked.append(plan.pick(info, hidden_in, near))
        return picked

    heads = Weights([w_query, w_key, w_value], True, pick_hidden)
    hidden = plan.gather(hidden_in, picked[0] if picked else plan.pick(info, hidden_in))
    dense = Weights([w_out, w_inner, w_outer], False, heads.halfway())
    qkv, *mats = queries_keys_values(info, *hidden, heads, bias_heads)
    cots = plan.gather(cot_out, plan.pick(info, cot_out, (qkv,)))
    if per == 1:
        kv, key_at = qkv, width // PAIR
    else:
        kv = lax.all_gather(qkv[:, width:], "blk", axis=0, tiled=True, axis_index_groups=fleets)
        key_at = 0
    sources = ((qkv, 0), (kv, key_at), (kv, key_at + width // PAIR))
    context_low, probs, sums = attend(info, *sources, span)

    own_cls = lax.dynamic_index_in_dim(cot_cls, plan.passage, 0, keepdims=True).astype(F32)
    layer_kept, layer_other, top, grad_context, grad_resid, dense_sums = middle(
        info, hidden, cots, context_low, own_cls, dense, narrow[2:], bias_inner
    )
    part_wo, part_wi, part_wu, dense_vecs = dense.scatter([dense_sums])
    part_bo, part_g1, part_s1, part_bu, part_g2, part_s2 = [dense_vecs[t] for t in range(6)]
    part_bi = dense_vecs[6 : 6 + b_inner.size // share].reshape(-1)
    layer_rows = plan.join(info, layer_kept, plan.send_back(layer_other))
    tops = plan.all_blocks(top)[::per, 0, :]
    cls_part = lax.dynamic_slice_in_dim(tops, plan.me * share, share, 1)

    back = functools.partial(
        attend_back, info, *sources, grad_context, context_low, sums, probs, span
    )
    give = functools.partial(input_grad, info, resid=grad_resid, mats=mats)
    if per == 1:
        most = back([(1, 1), (1, 0), (0, 1)], None)
        other = give(most, out_shape=(block_len, width), dtype=BF16, kept=False)
        rest = back([(0, 0)], most, (other, layer_rows))
        other = plan.send_back(other)
    else:
        blocks = span * per // min(1024, span * per)
        grad_q, *grad_kv = back([(k, q) for k in range(blocks) for q in range(2)], None)
        most = [grad_q] + [
            lax.psum_scatter(g, "blk", scatter_dimension=0, tiled=True, axis_index_groups=fleets)
            for g in grad_kv
        ]
        other = plan.send_back(give(most, out_shape=(block_len, width), dtype=BF16, kept=False))
        rest = most
    head_sums = head_grads(
        info, hidden, rest, most, heads.sums_of, 2 if heads.by_pairs else 1, (other,)
    )
    kept = give(rest, out_shape=hidden[0].shape, dtype=F32, kept=True)
    grad_input = plan.join(info, kept, other)
    part_wq, part_wk, part_wv, head_vecs = heads.scatter(head_sums, (grad_input,))
    part_bq, part_bv = head_vecs[0], head_vecs[1]
    return (
        layer_rows,
        cls_part,
        grad_input,
        part_wq,
        part_wk,
        part_wv,
        part_wo,
        part_wi,
        part_wu,
        part_bq,
        part_bv,
        part_bo,
        part_g1,
        part_s1,
        part_bi,
        part_bu,
        part_g2,
        part_s2,
    )


def solution(mesh):
    rows = P("batch", "blk", None)
    mats = (P("batch", "blk"),) * 6
    vecs = (P("blk"),) * 9
    return jax.shard_map(
        on_device,
        mesh=mesh,
        in_specs=(rows, P("batch"), rows, P("batch", None)) + mats + vecs,
        out_specs=(rows, P("batch", "blk"), rows) + mats + vecs,
        check_vma=False,
    )
```

time: 843 us -> 591 us (0.70)
  waiting for transfers between devices: 318 us -> 73 us
  blocking collectives: 110 us -> 0 us
  starting transfers between devices: 5.21 us -> 98 us
  Pallas kernels: 352 us -> 375 us
  local copies, waits for them, and re-layouts: 26.2 us -> 17.6 us
    reduce_scatter x2 -> x1, waiting for transfers between devices: 318 us -> 0.01 us  [scatter(): lax.psum_scatter(sums.reshape(-1, c), ('batch', 'blk'), scatter_dimension...]
    all_gather x2 -> x0, blocking collectives: 110 us -> none  [the longest x1 76.8 us: on_device(): vec_all = lax.all_gather(vec_shard, 'blk', axis=0).astype(F32)]
    ppermute x0 -> x20, starting transfers between devices: none -> 91.4 us  [the longest x18 87.9 us: exchanged(): return lax.ppermute(block, both, [(i, i ^ mask) for i in places])]
    ppermute x0 -> x20, waiting for transfers between devices: none -> 73 us  [the longest x18 53.2 us: exchanged(): return lax.ppermute(block, both, [(i, i ^ mask) for i in places])]
    pallas_call x5 -> x18, Pallas kernels: 237 us -> 271 us  [the longest x2 126 us: attend_back(): pl.pallas_call(functools.partial(attend_back_kernel, chunk=min(512, part)...]
    pallas_call x1, Pallas kernels: 115 us -> 104 us  [middle(): pl.pallas_call(functools.partial(middle_kernel, split=split, grid_of=grid...]
  transfers between devices with their start and end apart: 8 -> 26, of which waited for: 2 -> 11; matrix products, arithmetic and copies ran while one was open for 3% -> 2% of each run, Pallas kernels for 12% -> 45%
where the time goes in v2:
time: 591 us; the launch traced here: 586 us
  Pallas kernels  375 us (63%)
  starting transfers between devices  98 us (17%)
  waiting for transfers between devices  73 us (12%)
  local copies, waits for them, and re-layouts  17.6 us (3%)
  between operations  14.6 us (2%)
  other arithmetic  8.19 us (1%)
    pallas_call x2, Pallas kernels, attend_back(): pl.pallas_call(functools.partial(attend_back_kernel, chunk=min(512, part)...  126 us
    pallas_call x1, Pallas kernels, middle(): pl.pallas_call(functools.partial(middle_kernel, split=split, grid_of=grid...  104 us
    ppermute x18, starting transfers between devices, exchanged(): return lax.ppermute(block, both, [(i, i ^ mask) for i in places])  87.9 us
    pallas_call x1, Pallas kernels, attend(): pl.pallas_call(functools.partial(attend_kernel, chunk=min(256, kv), acros...  64.5 us
    ppermute x18, waiting for transfers between devices, exchanged(): return lax.ppermute(block, both, [(i, i ^ mask) for i in places])  53.2 us
    ppermute x2, waiting for transfers between devices, all_blocks(): other = lax.ppermute(block, 'blk', [(0, 1), (1, 0)])  19.7 us
    pallas_call x2, Pallas kernels, input_grad(): pl.pallas_call(functools.partial(input_grad_kernel, kept=kept), out_shape...  18.9 us
    pallas_call x1, Pallas kernels, head_grads(): pl.pallas_call(functools.partial(head_grads_kernel, split=split, grid_of=...  17.5 us
  transfers between devices with their start and end apart: 26, of which 11 were waited for; matrix products, arithmetic and copies ran while one was open for 2% of the time, Pallas kernels for 45%

profile of v2, /device:TPU:0, one launch (start us, length us, event | category | flops | bytes accessed | tf_op | source)
XLA Modules:
  0.0 586.2 jit_solution(10556929913225401719)
XLA Ops:
  8.7 3.0 collective-permute-start
  15.6 3.0 pick_other.2.refs_2_
  21.9 3.6 collective-permute-start.5
  27.9 2.8 collective-permute-done.5
  30.7 6.3 %collective-permute-done.4 = bf16[1,2,96,384]{3,2,1,0:T(8,128)(2,1)S(1)} collective-permute-done((bf16[1,2,96,384]{3,2,1,0:T(8,128)(2,1)}, bf16[1,2,96,384]{3,2,1,0:T(8,128)(2,1)S(1)}, u32[]{:S(2)}, u32[]{:S(2)}) %collective-permute-start.4) | collective-permute-done | bytes 147488 | tf_op jit(solution)/shard_map/ppermute | solution.py:939
  37.1 2.1 pad_maximum_fusion.1
  43.2 14.9 %collective-permute-done.6 = bf16[1,4,2,96,384]{4,3,2,1,0:T(8,128)(2,1)S(1)} collective-permute-done((bf16[1,4,2,96,384]{4,3,2,1,0:T(8,128)(2,1)}, bf16[1,4,2,96,384]{4,3,2,1,0:T(8,128)(2,1)S(1)}, u32[]{:S(2)}, u32[]{:S(2)}) %collective-permute-start.6) | collective-permute-done | bytes 589856 | tf_op jit(solution)/shard_map/ppermute | solution.py:939
  58.1 2.2 pad_maximum_fusion
  63.2 19.7 %collective-permute-done.2 = bf16[12,384]{1,0:T(8,128)(2,1)S(1)} collective-permute-done((bf16[12,384]{1,0:T(8,128)(2,1)S(1)}, bf16[12,384]{1,0:T(8,128)(2,1)S(1)}, u32[]{:S(2)}, u32[]{:S(2)}) %collective-permute-start.2) | collective-permute-done | bytes 9248 | tf_op jit(solution)/shard_map/ppermute | solution.py:903
  83.0 8.5 %collective-permute-done.9 = bf16[1,2,2,48,384]{4,3,2,1,0:T(8,128)(2,1)} collective-permute-done((bf16[1,2,2,48,384]{4,3,2,1,0:T(8,128)(2,1)S(1)}, bf16[1,2,2,48,384]{4,3,2,1,0:T(8,128)(2,1)}, u32[]{:S(2)}, u32[]{:S(2)}) %collective-permute-start.9) | collective-permute-done | bytes 147488 | tf_op jit(solution)/shard_map/ppermute | solution.py:939
  96.2 16.4 %queries.1 = (bf16[2048,2304]{1,0:T(8,128)(2,1)}, bf16[768,768]{1,0:T(8,128)(2,1)}, bf16[768,768]{1,0:T(8,128)(2,1)}, bf16[768,768]{1,0:T(8,128)(2,1)}) custom-call(s32[7]{0:T(128)} %stack.74.info, bf16[2,1024,768]{2,1,0:T(8,128)(2,1)} %hid_kept.3, bf16[1024,768]{1,0:T(8,128)(2,1)} %copy-done, f32[1,2304]{1,0:T(1,128)} %fusion.1.bias_ref, ...), custom_call_target="tpu_custom_call" | custom-call | tf_op jit(solution)/shard_map/queries/pallas_call | solution.py:398
  112.6 3.1 pick_other.3
  115.8 2.9 collective-permute-start.13
  120.5 64.5 %attend.1 = (bf16[2048,768]{1,0:T(8,128)(2,1)}, bf16[6,2048,4096]{2,1,0:T(8,128)(2,1)}, f32[6,1,4096]{2,1,0:T(1,128)}) custom-call(s32[7]{0:T(128)} %stack.74.info, bf16[2048,2304]{1,0:T(8,128)(2,1)} %get-tuple-element.59.rest_0_.q_ref.k_ref.v_ref, bf16[2048,2304]{1,0:T(8,128)(2,1)} %get-tuple-element.59.rest_0_.q_ref.k_ref.v_ref, ...), custom_call_target="tpu_custom_call" | custom-call | tf_op jit(solution)/shard_map/attend/pallas_call | solution.py:124
  186.1 103.9 %middle.1 = (bf16[2,1024,768]{2,1,0:T(8,128)(2,1)}, bf16[1024,768]{1,0:T(8,128)(2,1)}, bf16[16,768]{1,0:T(8,128)(2,1)}, bf16[2048,768]{1,0:T(8,128)(2,1)}, f32[2...) custom-call(s32[7]{0:T(128)} %stack.74.info, bf16[2,1024,768]{2,1,0:T(8,128)(2,1)} %hid_kept.3, bf16[1024,768]{1,0:T(8,128)(2,1)} %copy-done, ...), custom_call_target="tpu_custom_call" | custom-call | tf_op jit(solution)/shard_map/middle/pallas_call | solution.py:603
  290.1 91.6 %attend_back.1 = (bf16[2048,768]{1,0:T(8,128)(2,1)}, bf16[2048,768]{1,0:T(8,128)(2,1)}, bf16[2048,768]{1,0:T(8,128)(2,1)}) custom-call(s32[7]{0:T(128)} %stack.74.info, s32[2,3]{1,0:T(2,128)} %constant.49.clone.units, bf16[2048,2304]{1,0:T(8,128)(2,1)} %get-tuple-element.59.rest_0_.q_ref.k_ref.v_ref, ...), custom_call_target="tpu_custom_call" | custom-call | tf_op jit(solution)/shard_map/attend_back/pallas_call | solution.py:245
  381.7 9.5 %input_grad_other.1.rest_3_ = bf16[1024,768]{1,0:T(8,128)(2,1)} custom-call(s32[7]{0:T(128)} %stack.74.info, bf16[2048,768]{1,0:T(8,128)(2,1)} %get-tuple-element.67.gq_ref.rest_0_.rest_3_, bf16[2048,768]{1,0:T(8,128)(2,1)} %get-tuple-element.68.gk_ref.rest_1_.rest_4_, bf16[2048,768]{1,0:T(8,128)(2,1)} %get-tuple-element.69.gv_ref.rest_2_.rest_5_, ...), custom_call_target="tpu_custom_call" | custom-call | tf_op jit(solution)/shard_map/input_grad_other/pallas_call | solution.py:672
  391.2 2.0 collective-permute-start.16
  394.4 3.1 place_other.2.rest_4_
  398.0 34.5 %attend_back_last.1 = (bf16[1024,768]{1,0:T(8,128)(2,1)}, bf16[1024,768]{1,0:T(8,128)(2,1)}, bf16[1024,768]{1,0:T(8,128)(2,1)}) custom-call(s32[7]{0:T(128)} %stack.74.info, s32[2,1]{1,0:T(2,128)} %call_exported.0.units, bf16[2048,2304]{1,0:T(8,128)(2,1)} %get-tuple-element.59.rest_0_.q_ref.k_ref.v_ref, ...), custom_call_target="tpu_custom_call" | custom-call | tf_op jit(solution)/shard_map/attend_back_last/pallas_call | solution.py:245
  433.7 17.5 %head_grads.1 = (bf16[16,160,384]{2,1,0:T(8,128)(2,1)}, bf16[16,160,384]{2,1,0:T(8,128)(2,1)}) custom-call(s32[7]{0:T(128)} %stack.74.info, bf16[2,1024,768]{2,1,0:T(8,128)(2,1)} %hid_kept.3, bf16[1024,768]{1,0:T(8,128)(2,1)} %copy-done, bf16[1024,768]{1,0:T(8,128)(2,1)} %get-tuple-element.74.gq_ref.rest_0_, ...), custom_call_target="tpu_custom_call" | custom-call | tf_op jit(solution)/shard_map/head_grads/pallas_call | solution.py:735
  451.2 47.1 %collective-permute-start.17 = (bf16[16,160,384]{2,1,0:T(8,128)(2,1)}, bf16[16,160,384]{2,1,0:T(8,128)(2,1)S(1)}, u32[]{:S(2)}, u32[]{:S(2)}) collective-permute-start(bf16[16,160,384]{2,1,0:T(8,128)(2,1)} %get-tuple-element.78), channel_id=1, source_target_pairs={{0,2},{1,3},{2,0},{3,1},{4,6},{5,7},{6,4},{7,5},{8,10},{9,11},{10,... | collective-permute-start | bytes 5898248 | tf_op jit(solution)/shard_map/ppermute | solution.py:939
  498.3 3.8 collective-permute-done.17.refs_1_
  503.4 3.8 add_blocks.2
  507.1 2.0 collective-permute-start.18
  512.6 9.4 %input_grad_kept.1.base_ref = f32[2,1024,768]{2,1,0:T(8,128)} custom-call(s32[7]{0:T(128)} %stack.74.info, bf16[1024,768]{1,0:T(8,128)(2,1)} %get-tuple-element.74.gq_ref.rest_0_, bf16[1024,768]{1,0:T(8,128)(2,1)} %get-tuple-element.75.gk_ref.rest_1_, bf16[1024,768]{1,0:T(8,128)(2,1)} %get-tuple-element.76.gv_ref.rest_2_, ...), custom_call_target="tpu_custom_call" | custom-call | tf_op jit(solution)/shard_map/input_grad_kept/pallas_call | solution.py:672
  522.0 3.6 place_other.3.refs_4_
  525.6 7.2 %collective-permute-done.20.refs_3_ = bf16[4,160,384]{2,1,0:T(8,128)(2,1)S(1)} collective-permute-done((bf16[4,160,384]{2,1,0:T(8,128)(2,1)}, bf16[4,160,384]{2,1,0:T(8,128)(2,1)S(1)}, u32[]{:S(2)}, u32[]{:S(2)}) %collective-permute-start.20) | collective-permute-done | bytes 491552 | tf_op jit(solution)/shard_map/ppermute | solution.py:939
  533.6 2.4 add_blocks.3
  536.0 24.1 %collective-permute-start.21 = (bf16[1,160,384]{2,1,0:T(8,128)(2,1)}, bf16[1,160,384]{2,1,0:T(8,128)(2,1)S(1)}, u32[]{:S(2)}, u32[]{:S(2)}) collective-permute-start(bf16[1,160,384]{2,1,0:T(8,128)(2,1)} %get-tuple-element.84), channel_id=1, source_target_pairs={{0,8},{1,9},{2,10},{3,11},{4,12},{5,13},{6,14},{7,15},{8,0},{9,1},... | collective-permute-start | bytes 368648 | tf_op jit(solution)/shard_map/ppermute | solution.py:939
  560.0 2.4 collective-permute-start.23
  564.1 6.4 %collective-permute-done.22 = bf16[1,160,384]{2,1,0:T(8,128)(2,1)S(1)} collective-permute-done((bf16[1,160,384]{2,1,0:T(8,128)(2,1)}, bf16[1,160,384]{2,1,0:T(8,128)(2,1)S(1)}, u32[]{:S(2)}, u32[]{:S(2)}) %collective-permute-start.22) | collective-permute-done | bytes 122912 | tf_op jit(solution)/shard_map/ppermute | solution.py:939
  (126 shorter events, 44.4 us)
Async XLA Ops:
  7.2 177.8 %all-gather.3.cloned.1.call-start = ((), (), s32[]{:S(2)}) async-start(), calls=%async_computation.2 | async-start | bytes 10948608 | tf_op jit(solution)/shard_map/all_gather | solution.py:1005
  8.7 6.2 %collective-permute-start = (bf16[144,384]{1,0:T(8,128)(2,1)}, bf16[144,384]{1,0:T(8,128)(2,1)S(1)}, u32[]{:S(2)}, u32[]{:S(2)}) collective-permute-start(bf16[144,384]{1,0:T(8,128)(2,1)} %pack.2.rest_0_.refs_0_), channel_id=1, source_target_pairs={{0,1},{1,0},{2,3},{3,2},{4,5},{5,4},{6,7},{7,6},{8,9},{9,8},{10,11... | collective-permute-start | bytes 331784 | tf_op jit(solution)/shard_map/ppermute | solution.py:939
  20.2 6.1 %collective-permute-start.8 = (bf16[1,2,48,384]{3,2,1,0:T(8,128)(2,1)}, bf16[1,2,48,384]{3,2,1,0:T(8,128)(2,1)S(1)}, u32[]{:S(2)}, u32[]{:S(2)}) collective-permute-start(bf16[1,2,48,384]{3,2,1,0:T(8,128)(2,1)} %bitcast.45), channel_id=1, source_target_pairs={{0,4},{1,5},{2,6},{3,7},{4,0},{5,1},{6,2},{7,3},{8,12},{9,13},{10,... | collective-permute-start | bytes 221192 | tf_op jit(solution)/shard_map/ppermute | solution.py:939
  21.9 8.8 %collective-permute-start.5 = (bf16[1,2,96,384]{3,2,1,0:T(8,128)(2,1)}, bf16[1,2,96,384]{3,2,1,0:T(8,128)(2,1)S(1)}, u32[]{:S(2)}, u32[]{:S(2)}) collective-permute-start(bf16[1,2,96,384]{3,2,1,0:T(8,128)(2,1)} %bitcast.36), channel_id=1, source_target_pairs={{0,24},{1,25},{2,26},{3,27},{4,28},{5,29},{6,30},{7,31},{8,16},{9,... | collective-permute-start | bytes 442376 | tf_op jit(solution)/shard_map/ppermute | solution.py:939
  25.5 11.5 %collective-permute-start.4 = (bf16[1,2,96,384]{3,2,1,0:T(8,128)(2,1)}, bf16[1,2,96,384]{3,2,1,0:T(8,128)(2,1)S(1)}, u32[]{:S(2)}, u32[]{:S(2)}) collective-permute-start(bf16[1,2,96,384]{3,2,1,0:T(8,128)(2,1)} %bitcast.37), channel_id=1, source_target_pairs={{0,16},{1,17},{2,18},{3,19},{4,20},{5,21},{6,22},{7,23},{8,24},{9,... | collective-permute-start | bytes 442376 | tf_op jit(solution)/shard_map/ppermute | solution.py:939
  25.5 11.5 %collective-permute-start.3 = (bf16[1,2,96,384]{3,2,1,0:T(8,128)(2,1)}, bf16[1,2,96,384]{3,2,1,0:T(8,128)(2,1)S(1)}, u32[]{:S(2)}, u32[]{:S(2)}) collective-permute-start(bf16[1,2,96,384]{3,2,1,0:T(8,128)(2,1)} %bitcast.38), channel_id=1, source_target_pairs={{0,8},{1,9},{2,10},{3,11},{4,12},{5,13},{6,14},{7,15},{8,0},{9,1},... | collective-permute-start | bytes 442376 | tf_op jit(solution)/shard_map/ppermute | solution.py:939
  39.1 21.2 %copy-start.21 = (bf16[384]{0:T(512)(128)(2,1)S(1)}, bf16[384]{0:T(512)(128)(2,1)}, u32[]{:S(2)}) copy-start(bf16[384]{0:T(512)(128)(2,1)} %param.34) | copy-start | bytes 2308
  39.1 21.2 %copy-start.22 = (bf16[384]{0:T(512)(128)(2,1)S(1)}, bf16[384]{0:T(512)(128)(2,1)}, u32[]{:S(2)}) copy-start(bf16[384]{0:T(512)(128)(2,1)} %param.35) | copy-start | bytes 2308
  39.2 21.2 %copy-start.23 = (bf16[384]{0:T(512)(128)(2,1)S(1)}, bf16[384]{0:T(512)(128)(2,1)}, u32[]{:S(2)}) copy-start(bf16[384]{0:T(512)(128)(2,1)} %param.37) | copy-start | bytes 2308
  39.2 21.3 %copy-start.24 = (bf16[384]{0:T(512)(128)(2,1)S(1)}, bf16[384]{0:T(512)(128)(2,1)}, u32[]{:S(2)}) copy-start(bf16[384]{0:T(512)(128)(2,1)} %param.38) | copy-start | bytes 2308
  39.2 21.3 %copy-start.25 = (bf16[384]{0:T(512)(128)(2,1)S(1)}, bf16[384]{0:T(512)(128)(2,1)}, u32[]{:S(2)}) copy-start(bf16[384]{0:T(512)(128)(2,1)} %param.39) | copy-start | bytes 2308
  39.2 21.3 %copy-start.16 = (bf16[1536]{0:T(1024)(128)(2,1)S(1)}, bf16[1536]{0:T(1024)(128)(2,1)}, u32[]{:S(2)}) copy-start(bf16[1536]{0:T(1024)(128)(2,1)} %param.36) | copy-start | bytes 9220
  41.1 533.4 %reduce-scatter.2.cloned.1.call-start = ((), (), s32[]{:S(2)}) async-start(), calls=%async_computation.1 | async-start | bytes 11354112 | tf_op jit(solution)/shard_map/reduce_scatter | solution.py:1041
  41.1 17.0 %collective-permute-start.6 = (bf16[1,4,2,96,384]{4,3,2,1,0:T(8,128)(2,1)}, bf16[1,4,2,96,384]{4,3,2,1,0:T(8,128)(2,1)S(1)}, u32[]{:S(2)}, u32[]{:S(2)}) collective-permute-start(bf16[1,4,2,96,384]{4,3,2,1,0:T(8,128)(2,1)} %get-tuple-element.105), channel_id=1, source_target_pairs={{0,4},{1,5},{2,6},{3,7},{4,0},{5,1},{6,2},{7,3},{8,12},{9,13},{10,... | collective-permute-start | bytes 1769480 | tf_op jit(solution)/shard_map/ppermute | solution.py:939
  41.7 53.0 %collective-permute-start.1 = (bf16[1024,768]{1,0:T(8,128)(2,1)S(1)}, bf16[1024,768]{1,0:T(8,128)(2,1)S(1)}, u32[]{:S(2)}, u32[]{:S(2)}) collective-permute-start(bf16[1024,768]{1,0:T(8,128)(2,1)S(1)} %copy-done.1), channel_id=1, source_target_pairs={{0,1},{1,0},{2,3},{3,2},{4,5},{5,4},{6,7},{7,6},{8,9},{9,8},{10,11... | collective-permute-start | bytes 4718600 | tf_op jit(solution)/shard_map/ppermute | solution.py:871
  60.3 34.4 %collective-permute-start.7 = (bf16[2,4,2,96,384]{4,3,2,1,0:T(8,128)(2,1)}, bf16[2,4,2,96,384]{4,3,2,1,0:T(8,128)(2,1)}, u32[]{:S(2)}, u32[]{:S(2)}) collective-permute-start(bf16[2,4,2,96,384]{4,3,2,1,0:T(8,128)(2,1)} %pad_maximum_fusion), channel_id=1, source_target_pairs={{0,2},{1,3},{2,0},{3,1},{4,6},{5,7},{6,4},{7,5},{8,10},{9,11},{10,... | collective-permute-start | bytes 3538952 | tf_op jit(solution)/shard_map/ppermute | solution.py:939
  60.6 22.4 %collective-permute-start.2 = (bf16[12,384]{1,0:T(8,128)(2,1)S(1)}, bf16[12,384]{1,0:T(8,128)(2,1)S(1)}, u32[]{:S(2)}, u32[]{:S(2)}) collective-permute-start(bf16[12,384]{1,0:T(8,128)(2,1)S(1)} %concatenate.18), channel_id=1, source_target_pairs={{0,1},{1,0},{2,3},{3,2},{4,5},{5,4},{6,7},{7,6},{8,9},{9,8},{10,11... | collective-permute-start | bytes 27656 | tf_op jit(solution)/shard_map/ppermute | solution.py:903
  62.1 20.9 %collective-permute-start.11 = (bf16[1,2,2,48,384]{4,3,2,1,0:T(8,128)(2,1)S(1)}, bf16[1,2,2,48,384]{4,3,2,1,0:T(8,128)(2,1)S(1)}, u32[]{:S(2)}, u32[]{:S(2)}) collective-permute-start(bf16[1,2,2,48,384]{4,3,2,1,0:T(8,128)(2,1)S(1)} %get-tuple-element.107), channel_id=1, source_target_pairs={{0,24},{1,25},{2,26},{3,27},{4,28},{5,29},{6,30},{7,31},{8,16},{9,... | collective-permute-start | bytes 442376 | tf_op jit(solution)/shard_map/ppermute | solution.py:939
  63.2 19.8 %collective-permute-start.10 = (bf16[1,2,2,48,384]{4,3,2,1,0:T(8,128)(2,1)S(1)}, bf16[1,2,2,48,384]{4,3,2,1,0:T(8,128)(2,1)}, u32[]{:S(2)}, u32[]{:S(2)}) collective-permute-start(bf16[1,2,2,48,384]{4,3,2,1,0:T(8,128)(2,1)S(1)} %get-tuple-element.107), channel_id=1, source_target_pairs={{0,16},{1,17},{2,18},{3,19},{4,20},{5,21},{6,22},{7,23},{8,24},{9,... | collective-permute-start | bytes 442376 | tf_op jit(solution)/shard_map/ppermute | solution.py:939
  83.0 8.6 %collective-permute-start.9 = (bf16[1,2,2,48,384]{4,3,2,1,0:T(8,128)(2,1)S(1)}, bf16[1,2,2,48,384]{4,3,2,1,0:T(8,128)(2,1)}, u32[]{:S(2)}, u32[]{:S(2)}) collective-permute-start(bf16[1,2,2,48,384]{4,3,2,1,0:T(8,128)(2,1)S(1)} %get-tuple-element.107), channel_id=1, source_target_pairs={{0,8},{1,9},{2,10},{3,11},{4,12},{5,13},{6,14},{7,15},{8,0},{9,1},... | collective-permute-start | bytes 442376 | tf_op jit(solution)/shard_map/ppermute | solution.py:939
  92.7 2.1 collective-permute-start.12
  115.8 69.2 %collective-permute-start.13 = (bf16[1024,768]{1,0:T(8,128)(2,1)}, bf16[1024,768]{1,0:T(8,128)(2,1)S(1)}, u32[]{:S(2)}, u32[]{:S(2)}) collective-permute-start(bf16[1024,768]{1,0:T(8,128)(2,1)} %pick_other.3), channel_id=1, source_target_pairs={{0,1},{1,0},{2,3},{3,2},{4,5},{5,4},{6,7},{7,6},{8,9},{9,8},{10,11... | collective-permute-start | bytes 4718600 | tf_op jit(solution)/shard_map/ppermute | solution.py:871
  290.1 103.2 %collective-permute-start.14 = (bf16[1024,768]{1,0:T(8,128)(2,1)}, bf16[1024,768]{1,0:T(8,128)(2,1)S(1)}, u32[]{:S(2)}, u32[]{:S(2)}) collective-permute-start(bf16[1024,768]{1,0:T(8,128)(2,1)} %get-tuple-element.62), channel_id=1, source_target_pairs={{1,0},{0,1},{3,2},{2,3},{5,4},{4,5},{7,6},{6,7},{9,8},{8,9},{11,10... | collective-permute-start | bytes 4718600 | tf_op jit(solution)/shard_map/ppermute | solution.py:871
  391.2 41.3 %collective-permute-start.16 = (bf16[1024,768]{1,0:T(8,128)(2,1)}, bf16[1024,768]{1,0:T(8,128)(2,1)S(1)}, u32[]{:S(2)}, u32[]{:S(2)}) collective-permute-start(bf16[1024,768]{1,0:T(8,128)(2,1)} %input_grad_other.1.rest_3_), channel_id=1, source_target_pairs={{1,0},{0,1},{3,2},{2,3},{5,4},{4,5},{7,6},{6,7},{9,8},{8,9},{11,10... | collective-permute-start | bytes 4718600 | tf_op jit(solution)/shard_map/ppermute | solution.py:871
  451.2 50.9 %collective-permute-start.17 = (bf16[16,160,384]{2,1,0:T(8,128)(2,1)}, bf16[16,160,384]{2,1,0:T(8,128)(2,1)S(1)}, u32[]{:S(2)}, u32[]{:S(2)}) collective-permute-start(bf16[16,160,384]{2,1,0:T(8,128)(2,1)} %get-tuple-element.78), channel_id=1, source_target_pairs={{0,2},{1,3},{2,0},{3,1},{4,6},{5,7},{6,4},{7,5},{8,10},{9,11},{10,... | collective-permute-start | bytes 5898248 | tf_op jit(solution)/shard_map/ppermute | solution.py:939
  507.1 18.5 %collective-permute-start.18 = (bf16[4,160,384]{2,1,0:T(8,128)(2,1)}, bf16[4,160,384]{2,1,0:T(8,128)(2,1)S(1)}, u32[]{:S(2)}, u32[]{:S(2)}) collective-permute-start(bf16[4,160,384]{2,1,0:T(8,128)(2,1)} %get-tuple-element.80), channel_id=1, source_target_pairs={{0,1},{1,0},{2,3},{3,2},{4,5},{5,4},{6,7},{7,6},{8,9},{9,8},{10,11... | collective-permute-start | bytes 1474568 | tf_op jit(solution)/shard_map/ppermute | solution.py:939
  509.1 16.5 %collective-permute-start.19 = (bf16[4,160,384]{2,1,0:T(8,128)(2,1)}, bf16[4,160,384]{2,1,0:T(8,128)(2,1)S(1)}, u32[]{:S(2)}, u32[]{:S(2)}) collective-permute-start(bf16[4,160,384]{2,1,0:T(8,128)(2,1)} %get-tuple-element.81), channel_id=1, source_target_pairs={{0,4},{1,5},{2,6},{3,7},{4,0},{5,1},{6,2},{7,3},{8,12},{9,13},{10,... | collective-permute-start | bytes 1474568 | tf_op jit(solution)/shard_map/ppermute | solution.py:939
  509.1 23.7 %collective-permute-start.20 = (bf16[4,160,384]{2,1,0:T(8,128)(2,1)}, bf16[4,160,384]{2,1,0:T(8,128)(2,1)S(1)}, u32[]{:S(2)}, u32[]{:S(2)}) collective-permute-start(bf16[4,160,384]{2,1,0:T(8,128)(2,1)} %get-tuple-element.82), channel_id=1, source_target_pairs={{0,5},{1,4},{2,7},{3,6},{4,1},{5,0},{6,3},{7,2},{8,13},{9,12},{10,... | collective-permute-start | bytes 1474568 | tf_op jit(solution)/shard_map/ppermute | solution.py:939
  510.7 51.8 %collective-permute-start.15 = (bf16[16,768]{1,0:T(8,128)(2,1)S(1)}, bf16[16,768]{1,0:T(8,128)(2,1)S(1)}, u32[]{:S(2)}, u32[]{:S(2)}) collective-permute-start(bf16[16,768]{1,0:T(8,128)(2,1)S(1)} %copy-done.15), channel_id=1, source_target_pairs={{0,1},{1,0},{2,3},{3,2},{4,5},{5,4},{6,7},{7,6},{8,9},{9,8},{10,11... | collective-permute-start | bytes 73736 | tf_op jit(solution)/shard_map/ppermute | solution.py:903
  536.0 28.2 %collective-permute-start.21 = (bf16[1,160,384]{2,1,0:T(8,128)(2,1)}, bf16[1,160,384]{2,1,0:T(8,128)(2,1)S(1)}, u32[]{:S(2)}, u32[]{:S(2)}) collective-permute-start(bf16[1,160,384]{2,1,0:T(8,128)(2,1)} %get-tuple-element.84), channel_id=1, source_target_pairs={{0,8},{1,9},{2,10},{3,11},{4,12},{5,13},{6,14},{7,15},{8,0},{9,1},... | collective-permute-start | bytes 368648 | tf_op jit(solution)/shard_map/ppermute | solution.py:939
  560.0 10.5 %collective-permute-start.22 = (bf16[1,160,384]{2,1,0:T(8,128)(2,1)}, bf16[1,160,384]{2,1,0:T(8,128)(2,1)S(1)}, u32[]{:S(2)}, u32[]{:S(2)}) collective-permute-start(bf16[1,160,384]{2,1,0:T(8,128)(2,1)} %get-tuple-element.85), channel_id=1, source_target_pairs={{0,16},{1,17},{2,18},{3,19},{4,20},{5,21},{6,22},{7,23},{8,24},{9,... | collective-permute-start | bytes 368648 | tf_op jit(solution)/shard_map/ppermute | solution.py:939
  560.0 10.5 %collective-permute-start.23 = (bf16[1,160,384]{2,1,0:T(8,128)(2,1)}, bf16[1,160,384]{2,1,0:T(8,128)(2,1)S(1)}, u32[]{:S(2)}, u32[]{:S(2)}) collective-permute-start(bf16[1,160,384]{2,1,0:T(8,128)(2,1)} %get-tuple-element.86), channel_id=1, source_target_pairs={{0,24},{1,25},{2,26},{3,27},{4,28},{5,29},{6,30},{7,31},{8,16},{9,... | collective-permute-start | bytes 368648 | tf_op jit(solution)/shard_map/ppermute | solution.py:939
  (20 other events, 129.5 us)
Sparse Core Ops, SparseCore 0:
  41.2 102.7 all-gather.2
  290.2 229.6 reduce-scatter.1

commit v3 on v2

--- a/solution.py
+++ b/solution.py
@@ -50,8 +50,9 @@
 
 
 def attend_kernel(
-    info, q_ref, k_ref, v_ref, out_ref, p_ref, sum_ref, keys, vals, ques, bound, turned, *, chunk, across, span
+    info, q_ref, k_ref, v_ref, *rest, chunk, across, span, extra
 ):
+    out_ref, p_ref, sum_ref, keys, vals, ques, bound, turned = rest[extra:]
     pos = pl.program_id(1)
     kv = k_ref.shape[0]
     size, width = out_ref.shape[0], p_ref.shape[2]
@@ -116,14 +117,19 @@
     out_ref[...] = turned[...].T.astype(BF16)
 
 
-def attend(info, q_from, k_from, v_from, span):
-    (queries, q_at), (keys, k_at), (values, v_at) = q_from, k_from, v_from
+def attend(info, sources, span, first, count, before):
+    (queries, q_at), (keys, k_at), (values, v_at) = sources
     rows, kv = queries.shape[0], keys.shape[0]
     size = chunk_of(rows)
     pairs = HEADS // 2
+    before = before or ()
     return pl.pallas_call(
         functools.partial(
-            attend_kernel, chunk=min(256, kv), across=min(256, 2 * size), span=span
+            attend_kernel,
+            chunk=min(256, kv),
+            across=min(256, 2 * size),
+            span=span,
+            extra=len(before),
         ),
         out_shape=(
             jax.ShapeDtypeStruct((rows, HEADS * HDIM), BF16),
@@ -132,16 +138,17 @@
         ),
         grid_spec=pltpu.PrefetchScalarGridSpec(
             num_scalar_prefetch=1,
-            grid=(pairs, rows // size),
+            grid=(count, rows // size),
             in_specs=[
-                pl.BlockSpec((rows, PAIR), lambda j, c, s: (0, q_at + j)),
-                pl.BlockSpec((kv, PAIR), lambda j, c, s: (0, k_at + j)),
-                pl.BlockSpec((kv, PAIR), lambda j, c, s: (0, v_at + j)),
-            ],
+                pl.BlockSpec((rows, PAIR), lambda j, c, s: (0, q_at(first + j))),
+                pl.BlockSpec((kv, PAIR), lambda j, c, s: (0, k_at(first + j))),
+                pl.BlockSpec((kv, PAIR), lambda j, c, s: (0, v_at(first + j))),
+            ]
+            + any_specs(before),
             out_specs=(
-                pl.BlockSpec((size, PAIR), lambda j, c, s: (c, j)),
-                pl.BlockSpec((1, kv, 2 * size), lambda j, c, s: (j, 0, c)),
-                pl.BlockSpec((1, 1, 2 * size), lambda j, c, s: (j, 0, c)),
+                pl.BlockSpec((size, PAIR), lambda j, c, s: (c, first + j)),
+                pl.BlockSpec((1, kv, 2 * size), lambda j, c, s: (first + j, 0, c)),
+                pl.BlockSpec((1, 1, 2 * size), lambda j, c, s: (first + j, 0, c)),
             ),
             scratch_shapes=[
                 pltpu.VMEM((kv, PAIR), BF16),
@@ -151,9 +158,10 @@
                 pltpu.VMEM((PAIR, size), F32),
             ],
         ),
+        input_output_aliases={4 + t: t for t in range(len(before))},
         compiler_params=pltpu.CompilerParams(vmem_limit_bytes=60 * 2**20),
         name="attend",
-    )(info, queries, keys, values)
+    )(info, queries, keys, values, *before)
 
 
 def attend_back_kernel(
@@ -230,8 +238,8 @@
         gq_ref[...] = value.astype(BF16)
 
 
-def attend_back(info, q_from, k_from, v_from, grad, context, sums, probs, span, units, before, events=()):
-    (queries, q_at), (keys, k_at), (values, v_at) = q_from, k_from, v_from
+def attend_back(info, sources, grad, context, sums, probs, span, units, before, events=()):
+    (queries, q_at), (keys, k_at), (values, v_at) = sources
     rows, kv = queries.shape[0], keys.shape[0]
     pairs = HEADS // 2
     wide = HEADS * HDIM
@@ -241,7 +249,9 @@
     rows, kv = rows // cut, kv // cut
     out_rows = [rows, kv, kv]
     units = jnp.array(list(zip(*units)), jnp.int32)
-    col = lambda height, at=0: pl.BlockSpec((height, PAIR), lambda j, c, s, u: (0, at + j))
+    col = lambda height, at=lambda j: j: pl.BlockSpec(
+        (height, PAIR), lambda j, c, s, u: (0, at(j))
+    )
     return pl.pallas_call(
         functools.partial(
             attend_back_kernel,
@@ -312,7 +322,8 @@
 
 
 class Pieces:
-    def __init__(self, shape, mesh_shape, bundles):
+    def __init__(self, shape, mesh_shape, bundles, turned=()):
+        self.turned = turned
         self.r, self.c = shape
         self.m, self.n = mesh_shape
         self.bundles = bundles
@@ -321,7 +332,7 @@
     def place(self, masks, slot, info):
         if masks is None:
             return slot // self.n, lax.rem(slot, self.n)
-        return info[5] ^ (masks[slot] // self.n), info[6] ^ (masks[slot] % self.n)
+        return info[5] ^ (masks[slot] // self.n), masks[slot] % self.n
 
     def copies(self, refs, mats, sems, info, out):
         found = [[] for _ in mats]
@@ -334,15 +345,16 @@
                 for t in members:
                     mat = mats[t]
                     tall = mat.shape[0] // (self.m * r)
-                    wide = mat.shape[1] // (self.n * c)
+                    wide = max(mat.shape[1] // (self.n * c), 1)
                     for w in range(wide):
                         if isinstance(ref, (tuple, list)):
                             each = self.slots // len(ref)
                             block = ref[slot // each].at[slot % each, pl.ds(at, tall * r), :]
                         else:
                             block = ref.at[slot, pl.ds(at, tall * r), :]
-                        down = pl.multiple_of(j * (tall * r), tall * r)
-                        side = pl.multiple_of((i * wide + w) * c, c)
+                        row = j ^ (info[6] * (self.m // 2)) if t in self.turned else j
+                        down = pl.multiple_of(row * (tall * r), tall * r)
+                        side = (i * wide + w) * c if mat.shape[1] > c else 0
                         place = mat.at[pl.ds(down, tall * r), pl.ds(side, c)]
                         at += tall * r
                         pair = (place, block) if out else (block, place)
@@ -358,9 +370,9 @@
     return [pl.BlockSpec(memory_space=pl.ANY)] * len(arrays)
 
 
-def queries_kernel(info, kept_ref, other_ref, bias_ref, *rest, split, grid_of):
+def queries_kernel(info, kept_ref, other_ref, bias_ref, *rest, split, grid_of, extra):
     count = len(grid_of.bundles)
-    packed, (out_ref, mat_q, mat_k, mat_v, sems) = rest[:count], rest[count:]
+    packed, (out_ref, mat_q, mat_k, mat_v, sems) = rest[:count], rest[count + extra :]
     step = pl.program_id(0)
     mats = [mat_q, mat_k, mat_v]
 
@@ -390,27 +402,32 @@
     return pl.BlockSpec(shape, lambda i, s: (0,) * len(shape))
 
 
-def queries_keys_values(info, kept, other, weights, bias):
+def queries_keys_values(info, kept, other, packed, grid_of, bias, group, before):
     block_len, width = other.shape
     tile = min(512, block_len)
     split = block_len // tile
+    wide = bias.shape[1]
+    before = before or ()
     mat = jax.ShapeDtypeStruct((width, width), BF16)
+    inputs = [kept, other, bias, *packed]
     return pl.pallas_call(
-        functools.partial(queries_kernel, split=split, grid_of=weights.grid_of),
+        functools.partial(queries_kernel, split=split, grid_of=grid_of, extra=len(before)),
         out_shape=(jax.ShapeDtypeStruct((2 * block_len, 3 * width), BF16), mat, mat, mat),
         grid_spec=pltpu.PrefetchScalarGridSpec(
             num_scalar_prefetch=1,
             grid=(2 * split,),
             in_specs=split_specs(2, tile, split, width)
             + [whole_spec(bias.shape)]
-            + any_specs(weights.packed),
-            out_specs=(pl.BlockSpec((tile, 3 * width), lambda i, s: (i, 0)),)
-            + (whole_spec(mat.shape),) * 3,
-            scratch_shapes=[pltpu.SemaphoreType.DMA((weights.grid_of.count(),))],
+            + any_specs(packed)
+            + any_specs(before),
+            out_specs=(pl.BlockSpec((tile, wide), lambda i, s: (i, group)),)
+            + (pl.BlockSpec((width, wide // 3), lambda i, s: (0, group)),) * 3,
+            scratch_shapes=[pltpu.SemaphoreType.DMA((grid_of.count(),))],
         ),
+        input_output_aliases={1 + len(inputs) + t: t for t in range(len(before))},
         compiler_params=pltpu.CompilerParams(vmem_limit_bytes=60 * 2**20),
         name="queries",
-    )(info, kept, other, bias, *weights.packed)
+    )(info, *inputs, *before)
 
 
 def normal(values):
@@ -651,7 +668,8 @@
     )(info, *hidden, *cots, context, cls_row, vectors, inner_bias, *weights.packed)
 
 
-def input_grad_kernel(info, gq_ref, gk_ref, gv_ref, resid_ref, mat_q, mat_k, mat_v, grad_ref, *, kept):
+def input_grad_kernel(info, gq_ref, gk_ref, gv_ref, resid_ref, mat_q, mat_k, mat_v, *rest, kept):
+    grad_ref = rest[-1]
     total = resid_ref[...]
     for ref, mat in zip((gq_ref, gk_ref, gv_ref), (mat_q, mat_k, mat_v)):
         total += project_back(ref[...], mat[...])
@@ -661,7 +679,7 @@
         grad_ref[...] = total.astype(grad_ref.dtype)
 
 
-def input_grad(info, grads, resid, mats, out_shape, dtype, kept):
+def input_grad(info, grads, resid, mats, out_shape, dtype, kept, events=()):
     rows, width = resid.shape
     block_len = rows // 2
     tile = min(512, block_len)
@@ -675,12 +693,12 @@
         grid_spec=pltpu.PrefetchScalarGridSpec(
             num_scalar_prefetch=1,
             grid=(split,),
-            in_specs=[spec] * 4 + [whole_spec(mat.shape) for mat in mats],
+            in_specs=[spec] * 4 + [whole_spec(mat.shape) for mat in mats] + any_specs(events),
             out_specs=place,
         ),
         compiler_params=pltpu.CompilerParams(vmem_limit_bytes=60 * 2**20),
         name="input_grad_kept" if kept else "input_grad_other",
-    )(info, *grads, resid, *mats)
+    )(info, *grads, resid, *mats, *events)
 
 
 def head_grads_kernel(info, hid_kept, hid_other, *rest, split, grid_of, outs, extra):
@@ -762,7 +780,7 @@
 
 def pick_other(info, pair, events):
     _, block_len, width = pair.shape
-    tile = min(512, block_len)
+    tile = min(256, block_len)
     return pl.pallas_call(
         pick_kernel,
         out_shape=jax.ShapeDtypeStruct((block_len, width), pair.dtype),
@@ -799,26 +817,6 @@
         compiler_params=pltpu.CompilerParams(vmem_limit_bytes=60 * 2**20),
         name="pack",
     )(*shards, *events)
-
-
-def stack_kernel(*refs, count, outs):
-    at = 0
-    for out in refs[-outs:]:
-        rows = out.shape[1]
-        for k, ref in enumerate(refs[:count]):
-            out[k] = ref[at : at + rows, :]
-        at += rows
-
-
-def stack_rows(blocks, cuts, events):
-    c = blocks[0].shape[1]
-    return pl.pallas_call(
-        functools.partial(stack_kernel, count=len(blocks), outs=len(cuts)),
-        out_shape=tuple(jax.ShapeDtypeStruct((len(blocks), rows, c), BF16) for rows in cuts),
-        in_specs=[pl.BlockSpec(memory_space=pltpu.VMEM)] * len(blocks) + any_specs(events),
-        compiler_params=pltpu.CompilerParams(vmem_limit_bytes=60 * 2**20),
-        name="stack_rows",
-    )(*blocks, *events)
 
 
 def add_kernel(*refs, count, extra):
@@ -883,7 +881,7 @@
         self.stays = all(a == b for a, b in self.first)
 
     def pick(self, info, pair, events=()):
-        if self.stays:
+        if self.stays and events:
             return pick_other(info, pair, events)
         return lax.dynamic_index_in_dim(pair, 1 - self.part, 0, keepdims=False)
 
@@ -971,40 +969,31 @@
         m, n = self.m, self.n
         r, c = min(s[0] for s in self.shapes), min(s[1] for s in self.shapes)
         self.fits = r % 16 == 0 and c % 128 == 0
-        powers = m & (m - 1) == 0 and n & (n - 1) == 0 and m >= 8
+        powers = m & (m - 1) == 0 and n == 2 and m >= 8
         self.by_pairs = by_pairs and self.fits and powers
+        self.local = powers and self.fits
         every = list(range(len(shards)))
         if self.by_pairs:
             y, core, x = list(range(1, n)), [n], [2 * n]
             z = list(range(4 * n, m * n, 4 * n))
-            near = pack_after(shards, ())
-            near = [near] + [exchanged(near, mask) for mask in y]
-            cut = sum(s.size for s in shards[:-1]) // c
-            cuts = [cut, near[0].shape[0] - cut]
-            near = stack_rows(near, cuts, events(near))
-            self.packed, bundles, self.half = [], [], []
-            for rows, members, order in (
-                (near[0], every[:-1], [z, x]),
-                (near[1], every[-1:], [x, z]),
-            ):
-                part, masks = xor_gather(rows, order[:1])
-                self.half.append(part)
-                part, more = xor_gather(part, order[1:])
-                masks = [a ^ b for a in more for b in masks]
-                for mask in [0] + core:
-                    block = exchanged(part, mask) if mask else part
-                    self.packed.append(block.reshape(-1, *rows.shape[1:]))
-                    bundles.append(([a ^ b ^ mask for a in masks for b in [0] + y], members))
-            self.grid_of = Pieces((r, c), (m, n), bundles)
+            own = pack_after(shards, ())
+            found, masks = xor_gather(own, [z, x])
+            self.packed, self.grids = [], []
+            for far in (0, 1):
+                if far:
+                    found = exchanged(found, y[0])
+                    masks = [mask ^ y[0] for mask in masks]
+                self.packed.append([found, exchanged(found, core[0])])
+                bundles = [(masks, every), ([mask ^ core[0] for mask in masks], every)]
+                self.grids.append(Pieces((r, c), (m, n), bundles))
             self.stages = [core, [a ^ b for a in [0] + x for b in [0] + y][1:], z]
             self.sums_of = Pieces((r, c), (m, n), [(xor_masks(self.stages), every)])
             return
-        if callable(events):
-            events = ()
         packed = pack_after(shards, events) if self.fits else pack(shards)
         packed = lax.all_gather(packed, ("batch", "blk"), axis=0)
         if self.fits:
-            self.grid_of = Pieces((r, c), (m, n), [(None, every)])
+            turned = (0,) if self.local else ()
+            self.grid_of = Pieces((r, c), (m, n), [(None, every)], turned)
             self.packed = [packed]
         else:
             self.grid_of = Pieces((r * m, c * n), (1, 1), [(None, every)])
@@ -1015,9 +1004,6 @@
                 whole.append(part.reshape(m * rows, n * cols))
             self.packed = [pack(whole)[None]]
         self.sums_of = self.grid_of
-
-    def halfway(self):
-        return tuple(self.half) if self.by_pairs else ()
 
     def scatter(self, sums, meanwhile=()):
         extra = 16
@@ -1117,29 +1103,46 @@
     narrow = jnp.stack(
         [b_query, b_value, b_out, norm1_gain, norm1_shift, b_outer, norm2_gain, norm2_shift]
     )
-    vec_all = plan.all_blocks(jnp.concatenate([narrow, b_inner.reshape(-1, share)], 0)).astype(F32)
-    narrow = vec_all[:, :8].transpose(1, 0, 2).reshape(8, width)
-    bias_inner = vec_all[:, 8:].reshape(1, -1)
-    bias_heads = jnp.concatenate([narrow[0:1], jnp.zeros_like(narrow[0:1]), narrow[1:2]], 1)
-
-    picked = []
-
-    def pick_hidden(near):
-        picked.append(plan.pick(info, hidden_in, near))
-        return picked
-
-    heads = Weights([w_query, w_key, w_value], True, pick_hidden)
-    hidden = plan.gather(hidden_in, picked[0] if picked else plan.pick(info, hidden_in))
-    dense = Weights([w_out, w_inner, w_outer], False, heads.halfway())
-    qkv, *mats = queries_keys_values(info, *hidden, heads, bias_heads)
-    cots = plan.gather(cot_out, plan.pick(info, cot_out, (qkv,)))
-    if per == 1:
-        kv, key_at = qkv, width // PAIR
+    vec_shard = jnp.concatenate([narrow, b_inner.reshape(-1, share)], 0)
+    vec_all = plan.all_blocks(vec_shard)
+    narrow = vec_all[:, :8].transpose(1, 0, 2).reshape(8, width).astype(F32)
+    bias_inner = vec_all[:, 8:].reshape(1, -1).astype(F32)
+
+    def head_bias(query, value):
+        return jnp.concatenate([query, jnp.zeros_like(query), value])[None].astype(F32)
+
+    pairs = HEADS // 2
+    hidden = plan.gather(hidden_in, plan.pick(info, hidden_in))
+    heads = Weights([w_query, w_key, w_value], True)
+    dense = Weights([w_out, w_inner, w_outer], False)
+    if heads.by_pairs:
+        near = jnp.where(plan.me == 0, vec_all[0], vec_all[1])
+        far = jnp.where(plan.me == 0, vec_all[1], vec_all[0])
+        biases = [head_bias(near[0], near[1]), head_bias(far[0], far[1])]
+        packed, grids = heads.packed, heads.grids
     else:
-        kv = lax.all_gather(qkv[:, width:], "blk", axis=0, tiled=True, axis_index_groups=fleets)
-        key_at = 0
-    sources = ((qkv, 0), (kv, key_at), (kv, key_at + width // PAIR))
-    context_low, probs, sums = attend(info, *sources, span)
+        biases = [head_bias(narrow[0], narrow[1])]
+        packed, grids = [heads.packed], [heads.grid_of]
+    groups = len(grids)
+    each = pairs // groups
+    at = lambda kind: lambda j: (j // each) * 3 * each + kind * each + j % each
+    found, result = None, None
+    for group in range(groups):
+        found = queries_keys_values(
+            info, *hidden, packed[group], grids[group], biases[group], group, found
+        )
+        qkv, *mats = found
+        if group == 0:
+            cots = plan.gather(cot_out, plan.pick(info, cot_out, (qkv,)))
+        if per == 1:
+            sources = [(qkv, at(kind)) for kind in range(3)]
+        else:
+            kv = lax.all_gather(
+                qkv[:, width:], "blk", axis=0, tiled=True, axis_index_groups=fleets
+            )
+            sources = [(qkv, at(0)), (kv, at(0)), (kv, at(1))]
+        result = attend(info, sources, span, group * each, each, result)
+    context_low, probs, sums = result
 
     own_cls = lax.dynamic_index_in_dim(cot_cls, plan.passage, 0, keepdims=True).astype(F32)
     layer_kept, layer_other, top, grad_context, grad_resid, dense_sums = middle(
@@ -1153,12 +1156,14 @@
     cls_part = lax.dynamic_slice_in_dim(tops, plan.me * share, share, 1)
 
     back = functools.partial(
-        attend_back, info, *sources, grad_context, context_low, sums, probs, span
+        attend_back, info, sources, grad_context, context_low, sums, probs, span
     )
     give = functools.partial(input_grad, info, resid=grad_resid, mats=mats)
     if per == 1:
         most = back([(1, 1), (1, 0), (0, 1)], None)
-        other = give(most, out_shape=(block_len, width), dtype=BF16, kept=False)
+        other = give(
+            most, out_shape=(block_len, width), dtype=BF16, kept=False, events=(cls_part,)
+        )
         rest = back([(0, 0)], most, (other, layer_rows))
         other = plan.send_back(other)
     else:
@@ -1175,7 +1180,9 @@
     )
     kept = give(rest, out_shape=hidden[0].shape, dtype=F32, kept=True)
     grad_input = plan.join(info, kept, other)
-    part_wq, part_wk, part_wv, head_vecs = heads.scatter(head_sums, (grad_input,))
+    part_wq, part_wk, part_wv, head_vecs = heads.scatter(
+        head_sums, (grad_input, part_wo, dense_vecs)
+    )
     part_bq, part_bv = head_vecs[0], head_vecs[1]
     return (
         layer_rows,

time: 591 us -> 604 us (1.022)
  Pallas kernels: 375 us -> 443 us
  starting transfers between devices: 98 us -> 51.6 us
  waiting for transfers between devices: 73 us -> 65.4 us
    pallas_call x1 -> x2, Pallas kernels: 64.5 us -> 127 us  [attend(): pl.pallas_call(functools.partial(attend_kernel, chunk=min(256, kv), acros...]
    ppermute x18 -> x14, starting transfers between devices: 87.9 us -> 36 us  [exchanged(): return lax.ppermute(block, both, [(i, i ^ mask) for i in places])]
    pallas_call x2, Pallas kernels: 18 us -> 26.3 us  [queries_keys_values(): pl.pallas_call(functools.partial(queries_kernel, split=split, grid_of=gri...]
    ppermute x2, starting transfers between devices: 3.52 us -> 11.1 us  [all_blocks(): other = lax.ppermute(block, 'blk', [(0, 1), (1, 0)])]
    ppermute x18 -> x14, waiting for transfers between devices: 53.2 us -> 45.9 us  [exchanged(): return lax.ppermute(block, both, [(i, i ^ mask) for i in places])]
    unnamed x53 -> x57, local copies, waits for them, and re-layouts: 8.92 us -> 13.3 us
  transfers between devices with their start and end apart: 26 -> 22, of which waited for: 11 -> 8; matrix products, arithmetic and copies ran while one was open for 2% -> 2% of each run, Pallas kernels for 45% -> 56%
where the time goes in v3:
time: 604 us; the launch traced here: 599 us
  Pallas kernels  443 us (73%)
  waiting for transfers between devices  65.4 us (11%)
  starting transfers between devices  51.6 us (9%)
  local copies, waits for them, and re-layouts  21.4 us (4%)
  between operations  14.9 us (2%)
    pallas_call x2, Pallas kernels, attend(): pl.pallas_call(functools.partial(attend_kernel, chunk=min(256, kv), acros...  127 us
    pallas_call x2, Pallas kernels, attend_back(): pl.pallas_call(functools.partial(attend_back_kernel, chunk=min(512, part)...  127 us
    pallas_call x1, Pallas kernels, middle(): pl.pallas_call(functools.partial(middle_kernel, split=split, grid_of=grid...  104 us
    ppermute x14, waiting for transfers between devices, exchanged(): return lax.ppermute(block, both, [(i, i ^ mask) for i in places])  45.9 us
    ppermute x14, starting transfers between devices, exchanged(): return lax.ppermute(block, both, [(i, i ^ mask) for i in places])  36 us
    pallas_call x2, Pallas kernels, queries_keys_values(): pl.pallas_call(functools.partial(queries_kernel, split=split, grid_of=gri...  26.3 us
    ppermute x2, waiting for transfers between devices, all_blocks(): other = lax.ppermute(block, 'blk', [(0, 1), (1, 0)])  19.5 us
    pallas_call x2, Pallas kernels, input_grad(): pl.pallas_call(functools.partial(input_grad_kernel, kept=kept), out_shape...  18.6 us
  transfers between devices with their start and end apart: 22, of which 8 were waited for; matrix products, arithmetic and copies ran while one was open for 2% of the time, Pallas kernels for 56%

profile of v3, /device:TPU:0, one launch (start us, length us, event | category | flops | bytes accessed | tf_op | source)
XLA Modules:
  0.0 599.3 jit_solution(9732762717755362305)
XLA Ops:
  7.2 1.8 pack.3
  10.5 3.0 collective-permute-start.2
  13.6 2.6 collective-permute-start.3
  17.8 1.8 collective-permute-start
  19.6 5.5 collective-permute-done.3
  31.2 5.6 collective-permute-done.5
  41.3 19.5 %collective-permute-done.1 = bf16[12,384]{1,0:T(8,128)(2,1)S(1)} collective-permute-done((bf16[12,384]{1,0:T(8,128)(2,1)S(1)}, bf16[12,384]{1,0:T(8,128)(2,1)S(1)}, u32[]{:S(2)}, u32[]{:S(2)}) %collective-permute-start.1) | collective-permute-done | bytes 9248 | tf_op jit(solution)/shard_map/ppermute | solution.py:901
  64.3 12.9 %queries.2 = (bf16[2048,2304]{1,0:T(8,128)(2,1)}, bf16[768,768]{1,0:T(8,128)(2,1)}, bf16[768,768]{1,0:T(8,128)(2,1)}, bf16[768,768]{1,0:T(8,128)(2,1)}) custom-call(s32[7]{0:T(128)} %stack.74.info, bf16[2,1024,768]{2,1,0:T(8,128)(2,1)} %hid_kept.3, bf16[1024,768]{1,0:T(8,128)(2,1)} %copy-done, f32[1,1152]{1,0:T(1,128)} %get-tuple-element.121.bias_ref, ...), custom_call_target="tpu_custom_call" | custom-call | tf_op jit(solution)/shard_map/queries/pallas_call | solution.py:413
  77.2 4.4 pick_other.1
  82.1 15.2 %collective-permute-done.8.rest_0_ = bf16[8,144,384]{2,1,0:T(8,128)(2,1)} collective-permute-done((bf16[8,144,384]{2,1,0:T(8,128)(2,1)}, bf16[8,144,384]{2,1,0:T(8,128)(2,1)}, u32[]{:S(2)}, u32[]{:S(2)}) %collective-permute-start.8) | collective-permute-done | bytes 884768 | tf_op jit(solution)/shard_map/ppermute | solution.py:937
  99.1 59.9 %attend.2 = (bf16[2048,768]{1,0:T(8,128)(2,1)}, bf16[6,2048,4096]{2,1,0:T(8,128)(2,1)}, f32[6,1,4096]{2,1,0:T(1,128)}) custom-call(s32[7]{0:T(128)} %stack.74.info, bf16[2048,2304]{1,0:T(8,128)(2,1)} %get-tuple-element.62.rest_0_.rest_2_.q_ref.k_ref.v_ref, bf16[2048,2304]{1,0:T(8,128)(2,1)} %get-tuple-element.62.rest_0_.rest_2_.q_ref.k_ref.v_ref, ...), custom_call_target="tpu_custom_call" | custom-call | tf_op jit(solution)/shard_map/attend/pallas_call | solution.py:126
  160.0 13.4 %queries.3 = (bf16[2048,2304]{1,0:T(8,128)(2,1)}, bf16[768,768]{1,0:T(8,128)(2,1)}, bf16[768,768]{1,0:T(8,128)(2,1)}, bf16[768,768]{1,0:T(8,128)(2,1)}) custom-call(s32[7]{0:T(128)} %stack.74.info, bf16[2,1024,768]{2,1,0:T(8,128)(2,1)} %hid_kept.3, ...), custom_call_target="tpu_custom_call", output_to_operand_aliasing={{0}: (6, {}), {1}: (7, {}), {2}: (8, {}), {3}: (9, {})} | custom-call | tf_op jit(solution)/shard_map/queries/pallas_call | solution.py:413
  173.4 67.0 %attend.3 = (bf16[2048,768]{1,0:T(8,128)(2,1)}, bf16[6,2048,4096]{2,1,0:T(8,128)(2,1)}, f32[6,1,4096]{2,1,0:T(1,128)}) custom-call(s32[7]{0:T(128)} %stack.74.info, bf16[2048,2304]{1,0:T(8,128)(2,1)} %get-tuple-element.66.q_ref.k_ref.v_ref, ...), custom_call_target="tpu_custom_call", output_to_operand_aliasing={{0}: (4, {}), {1}: (5, {}), {2}: (6, {})} | custom-call | tf_op jit(solution)/shard_map/attend/pallas_call | solution.py:126
  241.6 103.6 %middle.1 = (bf16[2,1024,768]{2,1,0:T(8,128)(2,1)}, bf16[1024,768]{1,0:T(8,128)(2,1)}, bf16[16,768]{1,0:T(8,128)(2,1)}, bf16[2048,768]{1,0:T(8,128)(2,1)}, f32[2...) custom-call(s32[7]{0:T(128)} %stack.74.info, bf16[2,1024,768]{2,1,0:T(8,128)(2,1)} %hid_kept.3, bf16[1024,768]{1,0:T(8,128)(2,1)} %copy-done, ...), custom_call_target="tpu_custom_call" | custom-call | tf_op jit(solution)/shard_map/middle/pallas_call | solution.py:620
  346.0 9.6 %collective-permute-start.11 = (bf16[16,768]{1,0:T(8,128)(2,1)S(1)}, bf16[16,768]{1,0:T(8,128)(2,1)S(1)}, u32[]{:S(2)}, u32[]{:S(2)}) collective-permute-start(bf16[16,768]{1,0:T(8,128)(2,1)S(1)} %copy-done.14), channel_id=1, source_target_pairs={{0,1},{1,0},{2,3},{3,2},{4,5},{5,4},{6,7},{7,6},{8,9},{9,8},{10,11... | collective-permute-start | bytes 73736 | tf_op jit(solution)/shard_map/ppermute | solution.py:901
  355.6 92.1 %attend_back.1 = (bf16[2048,768]{1,0:T(8,128)(2,1)}, bf16[2048,768]{1,0:T(8,128)(2,1)}, bf16[2048,768]{1,0:T(8,128)(2,1)}) custom-call(s32[7]{0:T(128)} %stack.74.info, s32[2,3]{1,0:T(2,128)} %constant.55.clone.units, bf16[2048,2304]{1,0:T(8,128)(2,1)} %get-tuple-element.66.q_ref.k_ref.v_ref, bf16[2048,2304]{1,0:T(8,128)(2,1)} %get-tuple-element.66.q_ref.k_ref.v_ref, ...), custom_call_target="tpu_custom_call" | custom-call | tf_op jit(solution)/shard_map/attend_back/pallas_call | solution.py:255
  448.4 9.3 %input_grad_other.1.rest_3_ = bf16[1024,768]{1,0:T(8,128)(2,1)} custom-call(s32[7]{0:T(128)} %stack.74.info, bf16[2048,768]{1,0:T(8,128)(2,1)} %get-tuple-element.77.gq_ref.rest_0_.rest_3_, bf16[2048,768]{1,0:T(8,128)(2,1)} %get-tuple-element.78.gk_ref.rest_1_.rest_4_, bf16[2048,768]{1,0:T(8,128)(2,1)} %get-tuple-element.79.gv_ref.rest_2_.rest_5_, ...), custom_call_target="tpu_custom_call" | custom-call | tf_op jit(solution)/shard_map/input_grad_other/pallas_call | solution.py:690
  457.6 2.0 collective-permute-start.12
  460.8 3.0 place_other.2.rest_4_
  464.4 34.4 %attend_back_last.1 = (bf16[1024,768]{1,0:T(8,128)(2,1)}, bf16[1024,768]{1,0:T(8,128)(2,1)}, bf16[1024,768]{1,0:T(8,128)(2,1)}) custom-call(s32[7]{0:T(128)} %stack.74.info, s32[2,1]{1,0:T(2,128)} %call_exported.0.units, bf16[2048,2304]{1,0:T(8,128)(2,1)} %get-tuple-element.66.q_ref.k_ref.v_ref, bf16[2048,2304]{1,0:T(8,128)(2,1)} %get-tuple-element.66.q_ref.k_ref.v_ref, ...), custom_call_target="tpu_custom_call" | custom-call | tf_op jit(solution)/shard_map/attend_back_last/pallas_call | solution.py:255
  500.0 17.4 %head_grads.1 = (bf16[16,160,384]{2,1,0:T(8,128)(2,1)}, bf16[16,160,384]{2,1,0:T(8,128)(2,1)}) custom-call(s32[7]{0:T(128)} %stack.74.info, bf16[2,1024,768]{2,1,0:T(8,128)(2,1)} %hid_kept.3, bf16[1024,768]{1,0:T(8,128)(2,1)} %copy-done, bf16[1024,768]{1,0:T(8,128)(2,1)} %get-tuple-element.84.gq_ref.rest_0_, ...), custom_call_target="tpu_custom_call" | custom-call | tf_op jit(solution)/shard_map/head_grads/pallas_call | solution.py:753
  517.5 4.2 collective-permute-done.13.refs_1_
  523.0 3.6 add_blocks.2
  526.6 3.5 collective-permute-start.16
  530.0 9.3 %input_grad_kept.1.base_ref = f32[2,1024,768]{2,1,0:T(8,128)} custom-call(s32[7]{0:T(128)} %stack.74.info, bf16[1024,768]{1,0:T(8,128)(2,1)} %get-tuple-element.84.gq_ref.rest_0_, bf16[1024,768]{1,0:T(8,128)(2,1)} %get-tuple-element.85.gk_ref.rest_1_, bf16[1024,768]{1,0:T(8,128)(2,1)} %get-tuple-element.86.gv_ref.rest_2_, ...), custom_call_target="tpu_custom_call" | custom-call | tf_op jit(solution)/shard_map/input_grad_kept/pallas_call | solution.py:690
  539.4 3.6 place_other.3.refs_4_
  542.9 1.8 finish_sums.2
  544.8 6.9 %collective-permute-done.16.refs_3_ = bf16[4,160,384]{2,1,0:T(8,128)(2,1)S(1)} collective-permute-done((bf16[4,160,384]{2,1,0:T(8,128)(2,1)}, bf16[4,160,384]{2,1,0:T(8,128)(2,1)S(1)}, u32[]{:S(2)}, u32[]{:S(2)}) %collective-permute-start.16) | collective-permute-done | bytes 491552 | tf_op jit(solution)/shard_map/ppermute | solution.py:937
  552.5 2.4 add_blocks.3
  554.8 20.9 %collective-permute-start.17 = (bf16[1,160,384]{2,1,0:T(8,128)(2,1)}, bf16[1,160,384]{2,1,0:T(8,128)(2,1)S(1)}, u32[]{:S(2)}, u32[]{:S(2)}) collective-permute-start(bf16[1,160,384]{2,1,0:T(8,128)(2,1)} %get-tuple-element.97), channel_id=1, source_target_pairs={{0,8},{1,9},{2,10},{3,11},{4,12},{5,13},{6,14},{7,15},{8,0},{9,1},... | collective-permute-start | bytes 368648 | tf_op jit(solution)/shard_map/ppermute | solution.py:937
  580.4 7.8 %collective-permute-done.18 = bf16[1,160,384]{2,1,0:T(8,128)(2,1)S(1)} collective-permute-done((bf16[1,160,384]{2,1,0:T(8,128)(2,1)}, bf16[1,160,384]{2,1,0:T(8,128)(2,1)S(1)}, u32[]{:S(2)}, u32[]{:S(2)}) %collective-permute-start.18) | collective-permute-done | bytes 122912 | tf_op jit(solution)/shard_map/ppermute | solution.py:937
  588.9 1.8 finish_sums.3
  (123 shorter events, 34.5 us)
Async XLA Ops:
  7.2 233.3 %all-gather.3.cloned.1.call-start = ((), (), s32[]{:S(2)}) async-start(), calls=%async_computation.2 | async-start | bytes 10948608 | tf_op jit(solution)/shard_map/all_gather | solution.py:993
  9.0 533.9 %reduce-scatter.2.cloned.1.call-start = ((), (), s32[]{:S(2)}) async-start(), calls=%async_computation.1 | async-start | bytes 11354112 | tf_op jit(solution)/shard_map/reduce_scatter | solution.py:1027
  10.5 9.1 %collective-permute-start.2 = (bf16[1,144,384]{2,1,0:T(8,128)(2,1)}, bf16[1,144,384]{2,1,0:T(8,128)(2,1)S(1)}, u32[]{:S(2)}, u32[]{:S(2)}) collective-permute-start(bf16[1,144,384]{2,1,0:T(8,128)(2,1)} %bitcast.35), channel_id=1, source_target_pairs={{0,8},{1,9},{2,10},{3,11},{4,12},{5,13},{6,14},{7,15},{8,0},{9,1},... | collective-permute-start | bytes 331784 | tf_op jit(solution)/shard_map/ppermute | solution.py:937
  13.6 11.6 %collective-permute-start.3 = (bf16[1,144,384]{2,1,0:T(8,128)(2,1)}, bf16[1,144,384]{2,1,0:T(8,128)(2,1)S(1)}, u32[]{:S(2)}, u32[]{:S(2)}) collective-permute-start(bf16[1,144,384]{2,1,0:T(8,128)(2,1)} %bitcast.36), channel_id=1, source_target_pairs={{0,16},{1,17},{2,18},{3,19},{4,20},{5,21},{6,22},{7,23},{8,24},{9,... | collective-permute-start | bytes 331784 | tf_op jit(solution)/shard_map/ppermute | solution.py:937
  16.1 9.0 %collective-permute-start.4 = (bf16[1,144,384]{2,1,0:T(8,128)(2,1)}, bf16[1,144,384]{2,1,0:T(8,128)(2,1)}, u32[]{:S(2)}, u32[]{:S(2)}) collective-permute-start(bf16[1,144,384]{2,1,0:T(8,128)(2,1)} %bitcast.37), channel_id=1, source_target_pairs={{0,24},{1,25},{2,26},{3,27},{4,28},{5,29},{6,30},{7,31},{8,16},{9,... | collective-permute-start | bytes 331784 | tf_op jit(solution)/shard_map/ppermute | solution.py:937
  17.7 20.0 %copy-start.18 = (bf16[384]{0:T(512)(128)(2,1)S(1)}, bf16[384]{0:T(512)(128)(2,1)}, u32[]{:S(2)}) copy-start(bf16[384]{0:T(512)(128)(2,1)} %param.32) | copy-start | bytes 2308
  17.7 20.0 %copy-start.19 = (bf16[384]{0:T(512)(128)(2,1)S(1)}, bf16[384]{0:T(512)(128)(2,1)}, u32[]{:S(2)}) copy-start(bf16[384]{0:T(512)(128)(2,1)} %param.33) | copy-start | bytes 2308
  17.7 20.0 %copy-start.20 = (bf16[384]{0:T(512)(128)(2,1)S(1)}, bf16[384]{0:T(512)(128)(2,1)}, u32[]{:S(2)}) copy-start(bf16[384]{0:T(512)(128)(2,1)} %param.34) | copy-start | bytes 2308
  17.7 20.0 %copy-start.21 = (bf16[384]{0:T(512)(128)(2,1)S(1)}, bf16[384]{0:T(512)(128)(2,1)}, u32[]{:S(2)}) copy-start(bf16[384]{0:T(512)(128)(2,1)} %param.35) | copy-start | bytes 2308
  17.7 20.0 %copy-start.22 = (bf16[384]{0:T(512)(128)(2,1)S(1)}, bf16[384]{0:T(512)(128)(2,1)}, u32[]{:S(2)}) copy-start(bf16[384]{0:T(512)(128)(2,1)} %param.37) | copy-start | bytes 2308
  17.7 20.1 %copy-start.23 = (bf16[384]{0:T(512)(128)(2,1)S(1)}, bf16[384]{0:T(512)(128)(2,1)}, u32[]{:S(2)}) copy-start(bf16[384]{0:T(512)(128)(2,1)} %param.38) | copy-start | bytes 2308
  17.8 20.1 %copy-start.24 = (bf16[384]{0:T(512)(128)(2,1)S(1)}, bf16[384]{0:T(512)(128)(2,1)}, u32[]{:S(2)}) copy-start(bf16[384]{0:T(512)(128)(2,1)} %param.39) | copy-start | bytes 2308
  17.8 21.7 %copy-start.25 = (s32[2]{0:T(128)S(1)}, s32[2]{0:T(128)}, u32[]{:S(2)}) copy-start(s32[2]{0:T(128)} %param.22) | copy-start | bytes 28
  17.8 45.3 %collective-permute-start = (bf16[1024,768]{1,0:T(8,128)(2,1)S(1)}, bf16[1024,768]{1,0:T(8,128)(2,1)S(1)}, u32[]{:S(2)}, u32[]{:S(2)}) collective-permute-start(bf16[1024,768]{1,0:T(8,128)(2,1)S(1)} %dynamic-slice_bitcast_fusion), channel_id=1, source_target_pairs={{0,1},{1,0},{2,3},{3,2},{4,5},{5,4},{6,7},{7,6},{8,9},{9,8},{10,11... | collective-permute-start | bytes 4718600 | tf_op jit(solution)/shard_map/ppermute | solution.py:869
  26.1 10.7 %collective-permute-start.5 = (bf16[4,144,384]{2,1,0:T(8,128)(2,1)S(1)}, bf16[4,144,384]{2,1,0:T(8,128)(2,1)S(1)}, u32[]{:S(2)}, u32[]{:S(2)}) collective-permute-start(bf16[4,144,384]{2,1,0:T(8,128)(2,1)S(1)} %pad_maximum_fusion), channel_id=1, source_target_pairs={{0,4},{1,5},{2,6},{3,7},{4,0},{5,1},{6,2},{7,3},{8,12},{9,13},{10,... | collective-permute-start | bytes 1327112 | tf_op jit(solution)/shard_map/ppermute | solution.py:937
  37.7 25.4 %collective-permute-start.6 = (bf16[8,144,384]{2,1,0:T(8,128)(2,1)}, bf16[8,144,384]{2,1,0:T(8,128)(2,1)}, u32[]{:S(2)}, u32[]{:S(2)}) collective-permute-start(bf16[8,144,384]{2,1,0:T(8,128)(2,1)} %constant_dynamic-update-slice_fusion.rest_0_), channel_id=1, source_target_pairs={{0,2},{1,3},{2,0},{3,1},{4,6},{5,7},{6,4},{7,5},{8,10},{9,11},{10,... | collective-permute-start | bytes 2654216 | tf_op jit(solution)/shard_map/ppermute | solution.py:937
  37.9 22.9 %collective-permute-start.1 = (bf16[12,384]{1,0:T(8,128)(2,1)S(1)}, bf16[12,384]{1,0:T(8,128)(2,1)S(1)}, u32[]{:S(2)}, u32[]{:S(2)}) collective-permute-start(bf16[12,384]{1,0:T(8,128)(2,1)S(1)} %concatenate.32), channel_id=1, source_target_pairs={{0,1},{1,0},{2,3},{3,2},{4,5},{5,4},{6,7},{7,6},{8,9},{9,8},{10,11... | collective-permute-start | bytes 27656 | tf_op jit(solution)/shard_map/ppermute | solution.py:901
  60.8 36.5 %collective-permute-start.8 = (bf16[8,144,384]{2,1,0:T(8,128)(2,1)}, bf16[8,144,384]{2,1,0:T(8,128)(2,1)}, u32[]{:S(2)}, u32[]{:S(2)}) collective-permute-start(bf16[8,144,384]{2,1,0:T(8,128)(2,1)} %constant_dynamic-update-slice_fusion.rest_0_), channel_id=1, source_target_pairs={{0,1},{1,0},{2,3},{3,2},{4,5},{5,4},{6,7},{7,6},{8,9},{9,8},{10,11... | collective-permute-start | bytes 2654216 | tf_op jit(solution)/shard_map/ppermute | solution.py:937
  77.2 20.1 %copy-start.16 = (bf16[2,768]{1,0:T(2,128)(2,1)S(1)}, bf16[2,768]{1,0:T(2,128)(2,1)}, u32[]{:S(2)}) copy-start(bf16[2,768]{1,0:T(2,128)(2,1)} %param.24) | copy-start | bytes 9220
  81.6 158.9 %collective-permute-start.7 = (bf16[1024,768]{1,0:T(8,128)(2,1)}, bf16[1024,768]{1,0:T(8,128)(2,1)S(1)}, u32[]{:S(2)}, u32[]{:S(2)}) collective-permute-start(bf16[1024,768]{1,0:T(8,128)(2,1)} %pick_other.1), channel_id=1, source_target_pairs={{0,1},{1,0},{2,3},{3,2},{4,5},{5,4},{6,7},{7,6},{8,9},{9,8},{10,11... | collective-permute-start | bytes 4718600 | tf_op jit(solution)/shard_map/ppermute | solution.py:869
  97.3 61.8 %collective-permute-start.9 = (bf16[8,144,384]{2,1,0:T(8,128)(2,1)}, bf16[8,144,384]{2,1,0:T(8,128)(2,1)S(1)}, u32[]{:S(2)}, u32[]{:S(2)}) collective-permute-start(bf16[8,144,384]{2,1,0:T(8,128)(2,1)} %collective-permute-done.8.rest_0_), channel_id=1, source_target_pairs={{0,2},{1,3},{2,0},{3,1},{4,6},{5,7},{6,4},{7,5},{8,10},{9,11},{10,... | collective-permute-start | bytes 2654216 | tf_op jit(solution)/shard_map/ppermute | solution.py:937
  346.0 101.8 %collective-permute-start.11 = (bf16[16,768]{1,0:T(8,128)(2,1)S(1)}, bf16[16,768]{1,0:T(8,128)(2,1)S(1)}, u32[]{:S(2)}, u32[]{:S(2)}) collective-permute-start(bf16[16,768]{1,0:T(8,128)(2,1)S(1)} %copy-done.14), channel_id=1, source_target_pairs={{0,1},{1,0},{2,3},{3,2},{4,5},{5,4},{6,7},{7,6},{8,9},{9,8},{10,11... | collective-permute-start | bytes 73736 | tf_op jit(solution)/shard_map/ppermute | solution.py:901
  355.6 104.0 %collective-permute-start.10 = (bf16[1024,768]{1,0:T(8,128)(2,1)}, bf16[1024,768]{1,0:T(8,128)(2,1)S(1)}, u32[]{:S(2)}, u32[]{:S(2)}) collective-permute-start(bf16[1024,768]{1,0:T(8,128)(2,1)} %get-tuple-element.72), channel_id=1, source_target_pairs={{1,0},{0,1},{3,2},{2,3},{5,4},{4,5},{7,6},{6,7},{9,8},{8,9},{11,10... | collective-permute-start | bytes 4718600 | tf_op jit(solution)/shard_map/ppermute | solution.py:869
  457.6 41.2 %collective-permute-start.12 = (bf16[1024,768]{1,0:T(8,128)(2,1)}, bf16[1024,768]{1,0:T(8,128)(2,1)S(1)}, u32[]{:S(2)}, u32[]{:S(2)}) collective-permute-start(bf16[1024,768]{1,0:T(8,128)(2,1)} %input_grad_other.1.rest_3_), channel_id=1, source_target_pairs={{1,0},{0,1},{3,2},{2,3},{5,4},{4,5},{7,6},{6,7},{9,8},{8,9},{11,10... | collective-permute-start | bytes 4718600 | tf_op jit(solution)/shard_map/ppermute | solution.py:869
  517.4 4.2 collective-permute-start.13
  526.6 18.2 %collective-permute-start.14 = (bf16[4,160,384]{2,1,0:T(8,128)(2,1)}, bf16[4,160,384]{2,1,0:T(8,128)(2,1)S(1)}, u32[]{:S(2)}, u32[]{:S(2)}) collective-permute-start(bf16[4,160,384]{2,1,0:T(8,128)(2,1)} %get-tuple-element.90), channel_id=1, source_target_pairs={{0,1},{1,0},{2,3},{3,2},{4,5},{5,4},{6,7},{7,6},{8,9},{9,8},{10,11... | collective-permute-start | bytes 1474568 | tf_op jit(solution)/shard_map/ppermute | solution.py:937
  526.6 18.2 %collective-permute-start.15 = (bf16[4,160,384]{2,1,0:T(8,128)(2,1)}, bf16[4,160,384]{2,1,0:T(8,128)(2,1)S(1)}, u32[]{:S(2)}, u32[]{:S(2)}) collective-permute-start(bf16[4,160,384]{2,1,0:T(8,128)(2,1)} %get-tuple-element.91), channel_id=1, source_target_pairs={{0,4},{1,5},{2,6},{3,7},{4,0},{5,1},{6,2},{7,3},{8,12},{9,13},{10,... | collective-permute-start | bytes 1474568 | tf_op jit(solution)/shard_map/ppermute | solution.py:937
  526.6 25.1 %collective-permute-start.16 = (bf16[4,160,384]{2,1,0:T(8,128)(2,1)}, bf16[4,160,384]{2,1,0:T(8,128)(2,1)S(1)}, u32[]{:S(2)}, u32[]{:S(2)}) collective-permute-start(bf16[4,160,384]{2,1,0:T(8,128)(2,1)} %get-tuple-element.92), channel_id=1, source_target_pairs={{0,5},{1,4},{2,7},{3,6},{4,1},{5,0},{6,3},{7,2},{8,13},{9,12},{10,... | collective-permute-start | bytes 1474568 | tf_op jit(solution)/shard_map/ppermute | solution.py:937
  552.5 26.1 %copy-start.13 = (f32[16,384]{1,0:T(8,128)S(1)}, f32[16,384]{1,0:T(8,128)}, u32[]{:S(2)}) copy-start(f32[16,384]{1,0:T(8,128)} %get-tuple-element.95.refs_6_) | copy-start | bytes 73732
  554.8 25.6 %collective-permute-start.17 = (bf16[1,160,384]{2,1,0:T(8,128)(2,1)}, bf16[1,160,384]{2,1,0:T(8,128)(2,1)S(1)}, u32[]{:S(2)}, u32[]{:S(2)}) collective-permute-start(bf16[1,160,384]{2,1,0:T(8,128)(2,1)} %get-tuple-element.97), channel_id=1, source_target_pairs={{0,8},{1,9},{2,10},{3,11},{4,12},{5,13},{6,14},{7,15},{8,0},{9,1},... | collective-permute-start | bytes 368648 | tf_op jit(solution)/shard_map/ppermute | solution.py:937
  575.8 12.4 %collective-permute-start.18 = (bf16[1,160,384]{2,1,0:T(8,128)(2,1)}, bf16[1,160,384]{2,1,0:T(8,128)(2,1)S(1)}, u32[]{:S(2)}, u32[]{:S(2)}) collective-permute-start(bf16[1,160,384]{2,1,0:T(8,128)(2,1)} %get-tuple-element.98), channel_id=1, source_target_pairs={{0,16},{1,17},{2,18},{3,19},{4,20},{5,21},{6,22},{7,23},{8,24},{9,... | collective-permute-start | bytes 368648 | tf_op jit(solution)/shard_map/ppermute | solution.py:937
  577.1 11.1 %collective-permute-start.19 = (bf16[1,160,384]{2,1,0:T(8,128)(2,1)}, bf16[1,160,384]{2,1,0:T(8,128)(2,1)S(1)}, u32[]{:S(2)}, u32[]{:S(2)}) collective-permute-start(bf16[1,160,384]{2,1,0:T(8,128)(2,1)} %get-tuple-element.99), channel_id=1, source_target_pairs={{0,24},{1,25},{2,26},{3,27},{4,28},{5,29},{6,30},{7,31},{8,16},{9,... | collective-permute-start | bytes 368648 | tf_op jit(solution)/shard_map/ppermute | solution.py:937
  (16 other events, 86.1 us)
Sparse Core Ops, SparseCore 0:
  10.9 112.8 all-gather.2
  345.4 183.2 reduce-scatter.1

commit v4 on v3

--- a/solution.py
+++ b/solution.py
@@ -248,6 +248,7 @@
     cut = 2 if more else 1
     rows, kv = rows // cut, kv // cut
     out_rows = [rows, kv, kv]
+    heights = [rows * cut, kv * cut, kv * cut]
     units = jnp.array(list(zip(*units)), jnp.int32)
     col = lambda height, at=lambda j: j: pl.BlockSpec(
         (height, PAIR), lambda j, c, s, u: (0, at(j))
@@ -261,7 +262,7 @@
             more=more,
             extra=len(events),
         ),
-        out_shape=tuple(jax.ShapeDtypeStruct((height, wide), BF16) for height in out_rows),
+        out_shape=tuple(jax.ShapeDtypeStruct((height, wide), BF16) for height in heights),
         grid_spec=pltpu.PrefetchScalarGridSpec(
             num_scalar_prefetch=2,
             grid=(pairs, units.shape[1]),
@@ -289,6 +290,7 @@
                 pltpu.VMEM((kv, PAIR), F32),
             ],
         ),
+        input_output_aliases={9 + t: t for t in range(3)} if more else {},
         compiler_params=pltpu.CompilerParams(vmem_limit_bytes=60 * 2**20),
         name="attend_back_last" if more else "attend_back",
     )(info, units, queries, keys, values, grad, context, sums, probs, *(before or ()), *events)
@@ -370,10 +372,22 @@
     return [pl.BlockSpec(memory_space=pl.ANY)] * len(arrays)
 
 
-def queries_kernel(info, kept_ref, other_ref, bias_ref, *rest, split, grid_of, extra):
+def queries_kernel(info, kept_ref, other_ref, bias_ref, *rest, split, grid_of, extra, carry):
     count = len(grid_of.bundles)
-    packed, (out_ref, mat_q, mat_k, mat_v, sems) = rest[:count], rest[count + extra :]
+    packed, rest = rest[:count], rest[count + extra :]
     step = pl.program_id(0)
+    if carry:
+        carried, (out_ref, mat_q, mat_k, mat_v, picked, sems) = rest[0], rest[1:]
+        if carried.shape == picked.shape:
+
+            @pl.when(step == 0)
+            def copy():
+                picked[...] = carried[...]
+
+        else:
+            picked[...] = carried[0]
+    else:
+        out_ref, mat_q, mat_k, mat_v, sems = rest
     mats = [mat_q, mat_k, mat_v]
 
     @pl.when(step == 0)
@@ -402,32 +416,54 @@
     return pl.BlockSpec(shape, lambda i, s: (0,) * len(shape))
 
 
-def queries_keys_values(info, kept, other, packed, grid_of, bias, group, before):
+def queries_keys_values(info, kept, other, packed, grid_of, bias, group, before, carried=None):
     block_len, width = other.shape
     tile = min(512, block_len)
     split = block_len // tile
     wide = bias.shape[1]
     before = before or ()
+    carried = [] if carried is None else [carried]
+    if not carried:
+        moves = ([], (), ())
+    elif carried[0].shape[1:] == other.shape:
+        part = block_len // (2 * split)
+        moves = (
+            [pl.BlockSpec((1, part, width), lambda i, s: (1 - s[2], i, 0))],
+            (pl.BlockSpec((part, width), lambda i, s: (i, 0)),),
+            (jax.ShapeDtypeStruct(other.shape, BF16),),
+        )
+    else:
+        spec = whole_spec(carried[0].shape)
+        moves = ([spec], (spec,), (jax.ShapeDtypeStruct(carried[0].shape, BF16),))
     mat = jax.ShapeDtypeStruct((width, width), BF16)
     inputs = [kept, other, bias, *packed]
     return pl.pallas_call(
-        functools.partial(queries_kernel, split=split, grid_of=grid_of, extra=len(before)),
-        out_shape=(jax.ShapeDtypeStruct((2 * block_len, 3 * width), BF16), mat, mat, mat),
+        functools.partial(
+            queries_kernel,
+            split=split,
+            grid_of=grid_of,
+            extra=len(before),
+            carry=bool(carried),
+        ),
+        out_shape=(jax.ShapeDtypeStruct((2 * block_len, 3 * width), BF16), mat, mat, mat)
+        + moves[2],
         grid_spec=pltpu.PrefetchScalarGridSpec(
             num_scalar_prefetch=1,
             grid=(2 * split,),
             in_specs=split_specs(2, tile, split, width)
             + [whole_spec(bias.shape)]
             + any_specs(packed)
-            + any_specs(before),
+            + any_specs(before)
+            + moves[0],
             out_specs=(pl.BlockSpec((tile, wide), lambda i, s: (i, group)),)
-            + (pl.BlockSpec((width, wide // 3), lambda i, s: (0, group)),) * 3,
+            + (pl.BlockSpec((width, wide // 3), lambda i, s: (0, group)),) * 3
+            + moves[1],
             scratch_shapes=[pltpu.SemaphoreType.DMA((grid_of.count(),))],
         ),
         input_output_aliases={1 + len(inputs) + t: t for t in range(len(before))},
         compiler_params=pltpu.CompilerParams(vmem_limit_bytes=60 * 2**20),
         name="queries",
-    )(info, *inputs, *before)
+    )(info, *inputs, *before, *carried)
 
 
 def normal(values):
@@ -668,8 +704,12 @@
     )(info, *hidden, *cots, context, cls_row, vectors, inner_bias, *weights.packed)
 
 
-def input_grad_kernel(info, gq_ref, gk_ref, gv_ref, resid_ref, mat_q, mat_k, mat_v, *rest, kept):
-    grad_ref = rest[-1]
+def input_grad_kernel(info, gq_ref, gk_ref, gv_ref, resid_ref, mat_q, mat_k, mat_v, *rest, kept, join):
+    if join:
+        arrived, grad_ref, joined = rest[0], rest[-2], rest[-1]
+        joined[0] = arrived[...].astype(joined.dtype)
+    else:
+        grad_ref = rest[-1]
     total = resid_ref[...]
     for ref, mat in zip((gq_ref, gk_ref, gv_ref), (mat_q, mat_k, mat_v)):
         total += project_back(ref[...], mat[...])
@@ -679,7 +719,7 @@
         grad_ref[...] = total.astype(grad_ref.dtype)
 
 
-def input_grad(info, grads, resid, mats, out_shape, dtype, kept, events=()):
+def input_grad(info, grads, resid, mats, out_shape, dtype, kept, join=(), events=()):
     rows, width = resid.shape
     block_len = rows // 2
     tile = min(512, block_len)
@@ -687,22 +727,32 @@
     off = 0 if kept else split
     spec = pl.BlockSpec((tile, width), lambda i, s: (i + off, 0))
     place = kept_spec(tile, split, width) if kept else other_spec(tile, 0, width)
+    out = (jax.ShapeDtypeStruct(out_shape, dtype),)
+    in_specs = [spec] * 4 + [whole_spec(mat.shape) for mat in mats]
+    out_specs = (place,)
+    aliases = {}
+    if join:
+        in_specs += [pl.BlockSpec((tile, width), lambda i, s: (i, 0))] + any_specs(join[:1])
+        out += (jax.ShapeDtypeStruct(join[0].shape, join[0].dtype),)
+        out_specs += (pl.BlockSpec((1, tile, width), lambda i, s: (1 - s[2], i, 0)),)
+        aliases = {len(in_specs): 1}
     return pl.pallas_call(
-        functools.partial(input_grad_kernel, kept=kept),
-        out_shape=jax.ShapeDtypeStruct(out_shape, dtype),
+        functools.partial(input_grad_kernel, kept=kept, join=bool(join)),
+        out_shape=out,
         grid_spec=pltpu.PrefetchScalarGridSpec(
             num_scalar_prefetch=1,
             grid=(split,),
-            in_specs=[spec] * 4 + [whole_spec(mat.shape) for mat in mats] + any_specs(events),
-            out_specs=place,
+            in_specs=in_specs + any_specs(events),
+            out_specs=out_specs,
         ),
+        input_output_aliases=aliases,
         compiler_params=pltpu.CompilerParams(vmem_limit_bytes=60 * 2**20),
         name="input_grad_kept" if kept else "input_grad_other",
-    )(info, *grads, resid, *mats, *events)
+    )(info, *grads, resid, *mats, *join[::-1], *events)
 
 
 def head_grads_kernel(info, hid_kept, hid_other, *rest, split, grid_of, outs, extra):
-    kept, other, rest = rest[:3], rest[3:6], rest[6 + extra :]
+    found, rest = rest[:3], rest[3 + extra :]
     sums, (acc, mat_q, mat_k, mat_v, totals, vec_low, sems, vec_sems) = rest[:outs], rest[outs:]
     mats = [mat_q, mat_k, mat_v]
     step = pl.program_id(0)
@@ -713,7 +763,7 @@
         totals[...] = jnp.zeros_like(totals)
 
     rows = rows_of(hid_kept, hid_other, step, split)
-    grads = [jnp.where(step < split, a[...], b[...]) for a, b in zip(kept, other)]
+    grads = [ref[...] for ref in found]
     for t, grad in enumerate(grads):
         acc[t] += weight_grad(rows, grad)
     add_rows(totals, 0, grads[0].astype(F32))
@@ -742,13 +792,11 @@
         wait_all(tails)
 
 
-def head_grads(info, hidden, kept, other, grid_of, outs, events=()):
+def head_grads(info, hidden, grads, grid_of, outs, events=()):
     block_len, width = hidden[1].shape
     tile = min(512, block_len)
     split = block_len // tile
-    last = other[0].shape[0] // tile - split
-    kept_rows = pl.BlockSpec((tile, width), lambda i, s: (jnp.minimum(i, split - 1), 0))
-    other_rows = pl.BlockSpec((tile, width), lambda i, s: (jnp.maximum(i, split), 0))
+    rows = pl.BlockSpec((tile, width), lambda i, s: (i, 0))
     block = (grid_of.slots // outs, 3 * grid_of.r + 16, grid_of.c)
     return pl.pallas_call(
         functools.partial(
@@ -758,7 +806,7 @@
         grid_spec=pltpu.PrefetchScalarGridSpec(
             num_scalar_prefetch=1,
             grid=(2 * split,),
-            in_specs=split_specs(2, tile, split, width) + [kept_rows] * 3 + [other_rows] * 3 + any_specs(events),
+            in_specs=split_specs(2, tile, split, width) + [rows] * 3 + any_specs(events),
             out_specs=(pl.BlockSpec(memory_space=pl.ANY),) * outs,
             scratch_shapes=[pltpu.VMEM((3, width, width), F32)]
             + [pltpu.VMEM((width, width), BF16)] * 3
@@ -771,29 +819,7 @@
         ),
         compiler_params=pltpu.CompilerParams(vmem_limit_bytes=60 * 2**20),
         name="head_grads",
-    )(info, *hidden, *kept, *other, *events)
-
-
-def pick_kernel(info, pair_ref, *rest):
-    rest[-1][...] = pair_ref[0]
-
-
-def pick_other(info, pair, events):
-    _, block_len, width = pair.shape
-    tile = min(256, block_len)
-    return pl.pallas_call(
-        pick_kernel,
-        out_shape=jax.ShapeDtypeStruct((block_len, width), pair.dtype),
-        grid_spec=pltpu.PrefetchScalarGridSpec(
-            num_scalar_prefetch=1,
-            grid=(block_len // tile,),
-            in_specs=[pl.BlockSpec((1, tile, width), lambda i, s: (1 - s[2], i, 0))]
-            + any_specs(events),
-            out_specs=pl.BlockSpec((tile, width), lambda i, s: (i, 0)),
-        ),
-        compiler_params=pltpu.CompilerParams(vmem_limit_bytes=60 * 2**20),
-        name="pick_other",
-    )(info, pair, *events)
+    )(info, *hidden, *grads, *events)
 
 
 def pack_kernel(*refs, count):
@@ -880,9 +906,7 @@
         self.second = [(i, (1 - i % 2) * self.per + i // 2) for i in range(self.n)]
         self.stays = all(a == b for a, b in self.first)
 
-    def pick(self, info, pair, events=()):
-        if self.stays and events:
-            return pick_other(info, pair, events)
+    def pick(self, pair):
         return lax.dynamic_index_in_dim(pair, 1 - self.part, 0, keepdims=False)
 
     def gather(self, pair, picked):
@@ -978,14 +1002,9 @@
             z = list(range(4 * n, m * n, 4 * n))
             own = pack_after(shards, ())
             found, masks = xor_gather(own, [z, x])
-            self.packed, self.grids = [], []
-            for far in (0, 1):
-                if far:
-                    found = exchanged(found, y[0])
-                    masks = [mask ^ y[0] for mask in masks]
-                self.packed.append([found, exchanged(found, core[0])])
-                bundles = [(masks, every), ([mask ^ core[0] for mask in masks], every)]
-                self.grids.append(Pieces((r, c), (m, n), bundles))
+            self.found, self.masks, self.far = found, masks, [y[0], y[0] ^ core[0]]
+            self.every, self.shape = every, (r, c)
+            self.near = self.half([found, exchanged(found, core[0])], [0, core[0]])
             self.stages = [core, [a ^ b for a in [0] + x for b in [0] + y][1:], z]
             self.sums_of = Pieces((r, c), (m, n), [(xor_masks(self.stages), every)])
             return
@@ -1004,6 +1023,13 @@
                 whole.append(part.reshape(m * rows, n * cols))
             self.packed = [pack(whole)[None]]
         self.sums_of = self.grid_of
+
+    def half(self, blocks, steps):
+        bundles = [([mask ^ step for mask in self.masks], self.every) for step in steps]
+        return blocks, Pieces(self.shape, (self.m, self.n), bundles)
+
+    def other_half(self, found):
+        return self.half([exchanged(found, step) for step in self.far], self.far)
 
     def scatter(self, sums, meanwhile=()):
         extra = 16
@@ -1112,28 +1138,36 @@
         return jnp.concatenate([query, jnp.zeros_like(query), value])[None].astype(F32)
 
     pairs = HEADS // 2
-    hidden = plan.gather(hidden_in, plan.pick(info, hidden_in))
+    hidden = plan.gather(hidden_in, plan.pick(hidden_in))
     heads = Weights([w_query, w_key, w_value], True)
     dense = Weights([w_out, w_inner, w_outer], False)
     if heads.by_pairs:
-        near = jnp.where(plan.me == 0, vec_all[0], vec_all[1])
         far = jnp.where(plan.me == 0, vec_all[1], vec_all[0])
-        biases = [head_bias(near[0], near[1]), head_bias(far[0], far[1])]
-        packed, grids = heads.packed, heads.grids
+        biases = [head_bias(b_query, b_value), head_bias(far[0], far[1])]
+        packed, grid_of = heads.near
     else:
         biases = [head_bias(narrow[0], narrow[1])]
-        packed, grids = [heads.packed], [heads.grid_of]
-    groups = len(grids)
+        packed, grid_of = heads.packed, heads.grid_of
+    groups = len(biases)
     each = pairs // groups
     at = lambda kind: lambda j: (j // each) * 3 * each + kind * each + j % each
     found, result = None, None
     for group in range(groups):
+        last = group == groups - 1
+        carried = None
+        if not last:
+            carried = heads.found
+        elif plan.stays:
+            carried = cot_out
         found = queries_keys_values(
-            info, *hidden, packed[group], grids[group], biases[group], group, found
+            info, *hidden, packed, grid_of, biases[group], group, found, carried
         )
+        if last:
+            cots = plan.gather(cot_out, found[4] if plan.stays else plan.pick(cot_out))
+        else:
+            packed, grid_of = heads.other_half(found[4])
+        found = found[:4]
         qkv, *mats = found
-        if group == 0:
-            cots = plan.gather(cot_out, plan.pick(info, cot_out, (qkv,)))
         if per == 1:
             sources = [(qkv, at(kind)) for kind in range(3)]
         else:
@@ -1151,7 +1185,7 @@
     part_wo, part_wi, part_wu, dense_vecs = dense.scatter([dense_sums])
     part_bo, part_g1, part_s1, part_bu, part_g2, part_s2 = [dense_vecs[t] for t in range(6)]
     part_bi = dense_vecs[6 : 6 + b_inner.size // share].reshape(-1)
-    layer_rows = plan.join(info, layer_kept, plan.send_back(layer_other))
+    layer_other = plan.send_back(layer_other)
     tops = plan.all_blocks(top)[::per, 0, :]
     cls_part = lax.dynamic_slice_in_dim(tops, plan.me * share, share, 1)
 
@@ -1161,9 +1195,15 @@
     give = functools.partial(input_grad, info, resid=grad_resid, mats=mats)
     if per == 1:
         most = back([(1, 1), (1, 0), (0, 1)], None)
-        other = give(
-            most, out_shape=(block_len, width), dtype=BF16, kept=False, events=(cls_part,)
+        other, *layer_rows = give(
+            most,
+            out_shape=(block_len, width),
+            dtype=BF16,
+            kept=False,
+            join=(layer_kept, layer_other) if plan.stays else (),
+            events=(cls_part,),
         )
+        layer_rows = layer_rows[0] if layer_rows else plan.join(info, layer_kept, layer_other)
         rest = back([(0, 0)], most, (other, layer_rows))
         other = plan.send_back(other)
     else:
@@ -1173,12 +1213,14 @@
             lax.psum_scatter(g, "blk", scatter_dimension=0, tiled=True, axis_index_groups=fleets)
             for g in grad_kv
         ]
-        other = plan.send_back(give(most, out_shape=(block_len, width), dtype=BF16, kept=False))
+        (other,) = give(most, out_shape=(block_len, width), dtype=BF16, kept=False)
+        other = plan.send_back(other)
         rest = most
+        layer_rows = plan.join(info, layer_kept, layer_other)
     head_sums = head_grads(
-        info, hidden, rest, most, heads.sums_of, 2 if heads.by_pairs else 1, (other,)
+        info, hidden, rest, heads.sums_of, 2 if heads.by_pairs else 1, (other,)
     )
-    kept = give(rest, out_shape=hidden[0].shape, dtype=F32, kept=True)
+    (kept,) = give(rest, out_shape=hidden[0].shape, dtype=F32, kept=True)
     grad_input = plan.join(info, kept, other)
     part_wq, part_wk, part_wv, head_vecs = heads.scatter(
         head_sums, (grad_input, part_wo, dense_vecs)

time: 604 us -> 586 us (0.970)
  starting transfers between devices: 51.6 us -> 24.1 us
  Pallas kernels: 443 us -> 458 us
    pallas_call x2, Pallas kernels: 127 us -> 148 us  [attend(): pl.pallas_call(functools.partial(attend_kernel, chunk=min(256, kv), acros...]
    ppermute x14, starting transfers between devices: 36 us -> 16.9 us  [exchanged(): return lax.ppermute(block, both, [(i, i ^ mask) for i in places])]
    ppermute x14, waiting for transfers between devices: 45.9 us -> 33 us  [exchanged(): return lax.ppermute(block, both, [(i, i ^ mask) for i in places])]
    ppermute x2, starting transfers between devices: 11.1 us -> 2.03 us  [all_blocks(): other = lax.ppermute(block, 'blk', [(0, 1), (1, 0)])]
    ppermute x4, waiting for transfers between devices: 0.01 us -> 8.16 us  [swap(): return lax.ppermute(block, axis, route)]
    pallas_call x3 -> x2, Pallas kernels: 23 us -> 19.4 us  [input_grad(): pl.pallas_call(functools.partial(input_grad_kernel, kept=kept, join=bool(...]
    unnamed x57 -> x65, local copies, waits for them, and re-layouts: 13.3 us -> 11 us
  transfers between devices with their start and end apart: 22 -> 22, of which waited for: 8 -> 8; matrix products, arithmetic and copies ran while one was open for 2% -> 2% of each run, Pallas kernels for 56% -> 60%
where the time goes in v4:
time: 586 us; the launch traced here: 581 us
  Pallas kernels  458 us (78%)
  waiting for transfers between devices  62.6 us (11%)
  starting transfers between devices  24.1 us (4%)
  local copies, waits for them, and re-layouts  19.5 us (3%)
  between operations  14.9 us (3%)
    pallas_call x2, Pallas kernels, attend(): pl.pallas_call(functools.partial(attend_kernel, chunk=min(256, kv), acros...  148 us
    pallas_call x2, Pallas kernels, attend_back(): pl.pallas_call(functools.partial(attend_back_kernel, chunk=min(512, part)...  127 us
    pallas_call x1, Pallas kernels, middle(): pl.pallas_call(functools.partial(middle_kernel, split=split, grid_of=grid...  104 us
    ppermute x14, waiting for transfers between devices, exchanged(): return lax.ppermute(block, both, [(i, i ^ mask) for i in places])  33 us
    pallas_call x2, Pallas kernels, queries_keys_values(): pl.pallas_call(functools.partial(queries_kernel, split=split, grid_of=gri...  27.2 us
    ppermute x2, waiting for transfers between devices, all_blocks(): other = lax.ppermute(block, 'blk', [(0, 1), (1, 0)])  21.4 us
    pallas_call x2, Pallas kernels, input_grad(): pl.pallas_call(functools.partial(input_grad_kernel, kept=kept, join=bool(...  19.4 us
    ppermute x14, starting transfers between devices, exchanged(): return lax.ppermute(block, both, [(i, i ^ mask) for i in places])  16.9 us
  transfers between devices with their start and end apart: 22, of which 8 were waited for; matrix products, arithmetic and copies ran while one was open for 2% of the time, Pallas kernels for 60%

profile of v4, /device:TPU:0, one launch (start us, length us, event | category | flops | bytes accessed | tf_op | source)
XLA Modules:
  0.0 581.3 jit_solution(12470996313879529909)
XLA Ops:
  7.2 1.8 pack.3
  10.6 3.0 collective-permute-start.2
  13.7 2.6 collective-permute-start.3
  16.2 2.7 dynamic-slice_bitcast_fusion
  18.9 1.7 collective-permute-start
  20.6 4.6 collective-permute-done.3
  25.3 1.6 collective-permute-start.5
  27.0 9.8 %collective-permute-done.5 = bf16[4,144,384]{2,1,0:T(8,128)(2,1)S(1)} collective-permute-done((bf16[4,144,384]{2,1,0:T(8,128)(2,1)S(1)}, bf16[4,144,384]{2,1,0:T(8,128)(2,1)S(1)}, u32[]{:S(2)}, u32[]{:S(2)}) %collective-permute-start.5) | collective-permute-done | bytes 442400 | tf_op jit(solution)/shard_map/ppermute | solution.py:961
  37.3 1.5 collective-permute-start.1
  40.6 21.4 %collective-permute-done.1 = bf16[12,384]{1,0:T(8,128)(2,1)S(1)} collective-permute-done((bf16[12,384]{1,0:T(8,128)(2,1)S(1)}, bf16[12,384]{1,0:T(8,128)(2,1)S(1)}, u32[]{:S(2)}, u32[]{:S(2)}) %collective-permute-start.1) | collective-permute-done | bytes 9248 | tf_op jit(solution)/shard_map/ppermute | solution.py:925
  64.3 13.2 %queries.2 = (bf16[2048,2304]{1,0:T(8,128)(2,1)}, bf16[768,768]{1,0:T(8,128)(2,1)}, bf16[768,768]{1,0:T(8,128)(2,1)}, bf16[768,768]{1,0:T(8,128)(2,1)}, bf16[8,144,384]{2,1,0:T(8,128)(2,1)}) custom-call(s32[7]{0:T(128)} %stack.74.info, bf16[2,1024,768]{2,1,0:T(8,128)(2,1)} %hid_kept.3, bf16[1024,768]{1,0:T(8,128)(2,1)} %copy-done, ...), custom_call_target="tpu_custom_call" | custom-call | tf_op jit(solution)/shard_map/queries/pallas_call | solution.py:440
  77.5 1.6 collective-permute-start.7
  79.1 74.2 %attend.2 = (bf16[2048,768]{1,0:T(8,128)(2,1)}, bf16[6,2048,4096]{2,1,0:T(8,128)(2,1)}, f32[6,1,4096]{2,1,0:T(1,128)}) custom-call(s32[7]{0:T(128)} %stack.74.info, bf16[2048,2304]{1,0:T(8,128)(2,1)} %get-tuple-element.67.rest_2_.q_ref.k_ref.v_ref, bf16[2048,2304]{1,0:T(8,128)(2,1)} %get-tuple-element.67.rest_2_.q_ref.k_ref.v_ref, ...), custom_call_target="tpu_custom_call" | custom-call | tf_op jit(solution)/shard_map/attend/pallas_call | solution.py:126
  154.5 13.9 %queries.3 = (bf16[2048,2304]{1,0:T(8,128)(2,1)}, bf16[768,768]{1,0:T(8,128)(2,1)}, bf16[768,768]{1,0:T(8,128)(2,1)}, bf16[768,768]{1,0:T(8,128)(2,1)}, bf16[1024,768]{1,0:T(8,128)(2,1)}) custom-call(s32[7]{0:T(128)} %stack.74.info, bf16[2,1024,768]{2,1,0:T(8,128)(2,1)} %hid_kept.3, ...), custom_call_target="tpu_custom_call", output_to_operand_aliasing={{0}: (6, {}), {1}: (7, {}), {2}: (8, {}), {3}: (9, {})} | custom-call | tf_op jit(solution)/shard_map/queries/pallas_call | solution.py:440
  170.8 74.2 %attend.3 = (bf16[2048,768]{1,0:T(8,128)(2,1)}, bf16[6,2048,4096]{2,1,0:T(8,128)(2,1)}, f32[6,1,4096]{2,1,0:T(1,128)}) custom-call(s32[7]{0:T(128)} %stack.74.info, bf16[2048,2304]{1,0:T(8,128)(2,1)} %get-tuple-element.71.q_ref.k_ref.v_ref, ...), custom_call_target="tpu_custom_call", output_to_operand_aliasing={{0}: (4, {}), {1}: (5, {}), {2}: (6, {})} | custom-call | tf_op jit(solution)/shard_map/attend/pallas_call | solution.py:126
  246.2 103.7 %middle.1 = (bf16[2,1024,768]{2,1,0:T(8,128)(2,1)}, bf16[1024,768]{1,0:T(8,128)(2,1)}, bf16[16,768]{1,0:T(8,128)(2,1)}, bf16[2048,768]{1,0:T(8,128)(2,1)}, f32[2...) custom-call(s32[7]{0:T(128)} %stack.74.info, bf16[2,1024,768]{2,1,0:T(8,128)(2,1)} %hid_kept.3, bf16[1024,768]{1,0:T(8,128)(2,1)} %copy-done, ...), custom_call_target="tpu_custom_call" | custom-call | tf_op jit(solution)/shard_map/middle/pallas_call | solution.py:656
  353.4 92.3 %attend_back.1 = (bf16[2048,768]{1,0:T(8,128)(2,1)}, bf16[2048,768]{1,0:T(8,128)(2,1)}, bf16[2048,768]{1,0:T(8,128)(2,1)}) custom-call(s32[7]{0:T(128)} %stack.74.info, s32[2,3]{1,0:T(2,128)} %constant.55.clone.units, bf16[2048,2304]{1,0:T(8,128)(2,1)} %get-tuple-element.71.q_ref.k_ref.v_ref, bf16[2048,2304]{1,0:T(8,128)(2,1)} %get-tuple-element.71.q_ref.k_ref.v_ref, ...), custom_call_target="tpu_custom_call" | custom-call | tf_op jit(solution)/shard_map/attend_back/pallas_call | solution.py:256
  447.4 10.1 %input_grad_other.1 = (bf16[1024,768]{1,0:T(8,128)(2,1)}, bf16[2,1024,768]{2,1,0:T(8,128)(2,1)}) custom-call(s32[7]{0:T(128)} %stack.74.info, bf16[2048,768]{1,0:T(8,128)(2,1)} %get-tuple-element.80.gq_ref.rest_0_, bf16[2048,768]{1,0:T(8,128)(2,1)} %get-tuple-element.81.gk_ref.rest_1_, ...), custom_call_target="tpu_custom_call", output_to_operand_aliasing={{1}: (9, {})} | custom-call | tf_op jit(solution)/shard_map/input_grad_other/pallas_call | solution.py:739
  459.4 34.4 %attend_back_last.1 = (bf16[2048,768]{1,0:T(8,128)(2,1)}, bf16[2048,768]{1,0:T(8,128)(2,1)}, bf16[2048,768]{1,0:T(8,128)(2,1)}) custom-call(s32[7]{0:T(128)} %stack.74.info, s32[2,1]{1,0:T(2,128)} %call_exported.0.units, bf16[2048,2304]{1,0:T(8,128)(2,1)} %get-tuple-element.71.q_ref.k_ref.v_ref, ...), custom_call_target="tpu_custom_call", output_to_operand_aliasing={{0}: (9, {}), {1}: (10, {}), {2}: (11, {})} | custom-call | tf_op jit(solution)/shard_map/attend_back_last/pallas_call | solution.py:256
  493.7 8.2 %collective-permute-done.12.other_ref.rest_3_ = bf16[1024,768]{1,0:T(8,128)(2,1)S(1)} collective-permute-done((bf16[1024,768]{1,0:T(8,128)(2,1)}, bf16[1024,768]{1,0:T(8,128)(2,1)S(1)}, u32[]{:S(2)}, u32[]{:S(2)}) %collective-permute-start.12) | collective-permute-done | bytes 1572896 | tf_op jit(solution)/shard_map/ppermute | solution.py:895
  503.1 16.5 %head_grads.1 = (bf16[16,160,384]{2,1,0:T(8,128)(2,1)}, bf16[16,160,384]{2,1,0:T(8,128)(2,1)}) custom-call(s32[7]{0:T(128)} %stack.74.info, bf16[2,1024,768]{2,1,0:T(8,128)(2,1)} %hid_kept.3, bf16[1024,768]{1,0:T(8,128)(2,1)} %copy-done, bf16[2048,768]{1,0:T(8,128)(2,1)} %get-tuple-element.92.gq_ref.rest_0_, ...), custom_call_target="tpu_custom_call" | custom-call | tf_op jit(solution)/shard_map/head_grads/pallas_call | solution.py:801
  519.8 4.1 collective-permute-done.13.refs_1_
  525.2 3.5 add_blocks.2
  529.0 1.7 collective-permute-start.15
  532.2 9.3 %input_grad_kept.1.base_ref = f32[2,1024,768]{2,1,0:T(8,128)} custom-call(s32[7]{0:T(128)} %stack.74.info, bf16[2048,768]{1,0:T(8,128)(2,1)} %get-tuple-element.92.gq_ref.rest_0_, bf16[2048,768]{1,0:T(8,128)(2,1)} %get-tuple-element.93.gk_ref.rest_1_, bf16[2048,768]{1,0:T(8,128)(2,1)} %get-tuple-element.94.gv_ref.rest_2_, ...), custom_call_target="tpu_custom_call" | custom-call | tf_op jit(solution)/shard_map/input_grad_kept/pallas_call | solution.py:739
  541.5 3.6 place_other.1.refs_4_
  545.1 1.8 finish_sums.2
  547.0 6.9 %collective-permute-done.16.refs_3_ = bf16[4,160,384]{2,1,0:T(8,128)(2,1)S(1)} collective-permute-done((bf16[4,160,384]{2,1,0:T(8,128)(2,1)}, bf16[4,160,384]{2,1,0:T(8,128)(2,1)S(1)}, u32[]{:S(2)}, u32[]{:S(2)}) %collective-permute-start.16) | collective-permute-done | bytes 491552 | tf_op jit(solution)/shard_map/ppermute | solution.py:961
  554.7 2.4 add_blocks.3
  558.3 2.7 collective-permute-start.18
  563.6 6.5 %collective-permute-done.18 = bf16[1,160,384]{2,1,0:T(8,128)(2,1)S(1)} collective-permute-done((bf16[1,160,384]{2,1,0:T(8,128)(2,1)}, bf16[1,160,384]{2,1,0:T(8,128)(2,1)S(1)}, u32[]{:S(2)}, u32[]{:S(2)}) %collective-permute-start.18) | collective-permute-done | bytes 122912 | tf_op jit(solution)/shard_map/ppermute | solution.py:961
  570.9 1.8 finish_sums.3
  (129 shorter events, 28.9 us)
Async XLA Ops:
  7.2 237.8 %all-gather.3.cloned.1.call-start = ((), (), s32[]{:S(2)}) async-start(), calls=%async_computation.2 | async-start | bytes 10948608 | tf_op jit(solution)/shard_map/all_gather | solution.py:1012
  9.0 28.0 %copy-start.20 = (bf16[384]{0:T(512)(128)(2,1)S(1)}, bf16[384]{0:T(512)(128)(2,1)}, u32[]{:S(2)}) copy-start(bf16[384]{0:T(512)(128)(2,1)} %param.31) | copy-start | bytes 2308
  9.0 28.0 %copy-start.21 = (bf16[384]{0:T(512)(128)(2,1)S(1)}, bf16[384]{0:T(512)(128)(2,1)}, u32[]{:S(2)}) copy-start(bf16[384]{0:T(512)(128)(2,1)} %param.32) | copy-start | bytes 2308
  9.0 28.0 %copy-start.18 = (bf16[1536]{0:T(1024)(128)(2,1)S(1)}, bf16[1536]{0:T(1024)(128)(2,1)}, u32[]{:S(2)}) copy-start(bf16[1536]{0:T(1024)(128)(2,1)} %param.36) | copy-start | bytes 9220
  9.0 28.1 %copy-start.22 = (bf16[384]{0:T(512)(128)(2,1)S(1)}, bf16[384]{0:T(512)(128)(2,1)}, u32[]{:S(2)}) copy-start(bf16[384]{0:T(512)(128)(2,1)} %param.33) | copy-start | bytes 2308
  9.0 28.1 %copy-start.23 = (bf16[384]{0:T(512)(128)(2,1)S(1)}, bf16[384]{0:T(512)(128)(2,1)}, u32[]{:S(2)}) copy-start(bf16[384]{0:T(512)(128)(2,1)} %param.34) | copy-start | bytes 2308
  9.0 28.1 %copy-start.24 = (bf16[384]{0:T(512)(128)(2,1)S(1)}, bf16[384]{0:T(512)(128)(2,1)}, u32[]{:S(2)}) copy-start(bf16[384]{0:T(512)(128)(2,1)} %param.35) | copy-start | bytes 2308
  9.0 28.1 %copy-start.25 = (bf16[384]{0:T(512)(128)(2,1)S(1)}, bf16[384]{0:T(512)(128)(2,1)}, u32[]{:S(2)}) copy-start(bf16[384]{0:T(512)(128)(2,1)} %param.37) | copy-start | bytes 2308
  9.1 28.1 %copy-start.26 = (bf16[384]{0:T(512)(128)(2,1)S(1)}, bf16[384]{0:T(512)(128)(2,1)}, u32[]{:S(2)}) copy-start(bf16[384]{0:T(512)(128)(2,1)} %param.38) | copy-start | bytes 2308
  9.1 28.1 %copy-start.27 = (bf16[384]{0:T(512)(128)(2,1)S(1)}, bf16[384]{0:T(512)(128)(2,1)}, u32[]{:S(2)}) copy-start(bf16[384]{0:T(512)(128)(2,1)} %param.39) | copy-start | bytes 2308
  9.1 29.7 %copy-start.29 = (s32[2]{0:T(128)S(1)}, s32[2]{0:T(128)}, u32[]{:S(2)}) copy-start(s32[2]{0:T(128)} %param.22) | copy-start | bytes 28
  9.1 536.0 %reduce-scatter.2.cloned.1.call-start = ((), (), s32[]{:S(2)}) async-start(), calls=%async_computation.1 | async-start | bytes 11354112 | tf_op jit(solution)/shard_map/reduce_scatter | solution.py:1053
  10.6 10.0 %collective-permute-start.2 = (bf16[1,144,384]{2,1,0:T(8,128)(2,1)}, bf16[1,144,384]{2,1,0:T(8,128)(2,1)S(1)}, u32[]{:S(2)}, u32[]{:S(2)}) collective-permute-start(bf16[1,144,384]{2,1,0:T(8,128)(2,1)} %bitcast.31), channel_id=1, source_target_pairs={{0,8},{1,9},{2,10},{3,11},{4,12},{5,13},{6,14},{7,15},{8,0},{9,1},... | collective-permute-start | bytes 331784 | tf_op jit(solution)/shard_map/ppermute | solution.py:961
  13.7 11.6 %collective-permute-start.3 = (bf16[1,144,384]{2,1,0:T(8,128)(2,1)}, bf16[1,144,384]{2,1,0:T(8,128)(2,1)S(1)}, u32[]{:S(2)}, u32[]{:S(2)}) collective-permute-start(bf16[1,144,384]{2,1,0:T(8,128)(2,1)} %bitcast.32), channel_id=1, source_target_pairs={{0,16},{1,17},{2,18},{3,19},{4,20},{5,21},{6,22},{7,23},{8,24},{9,... | collective-permute-start | bytes 331784 | tf_op jit(solution)/shard_map/ppermute | solution.py:961
  16.2 9.0 %collective-permute-start.4 = (bf16[1,144,384]{2,1,0:T(8,128)(2,1)}, bf16[1,144,384]{2,1,0:T(8,128)(2,1)S(1)}, u32[]{:S(2)}, u32[]{:S(2)}) collective-permute-start(bf16[1,144,384]{2,1,0:T(8,128)(2,1)} %bitcast.33), channel_id=1, source_target_pairs={{0,24},{1,25},{2,26},{3,27},{4,28},{5,29},{6,30},{7,31},{8,16},{9,... | collective-permute-start | bytes 331784 | tf_op jit(solution)/shard_map/ppermute | solution.py:961
  18.9 43.8 %collective-permute-start = (bf16[1024,768]{1,0:T(8,128)(2,1)}, bf16[1024,768]{1,0:T(8,128)(2,1)S(1)}, u32[]{:S(2)}, u32[]{:S(2)}) collective-permute-start(bf16[1024,768]{1,0:T(8,128)(2,1)} %dynamic-slice_bitcast_fusion), channel_id=1, source_target_pairs={{0,1},{1,0},{2,3},{3,2},{4,5},{5,4},{6,7},{7,6},{8,9},{9,8},{10,11... | collective-permute-start | bytes 4718600 | tf_op jit(solution)/shard_map/ppermute | solution.py:895
  25.3 11.5 %collective-permute-start.5 = (bf16[4,144,384]{2,1,0:T(8,128)(2,1)S(1)}, bf16[4,144,384]{2,1,0:T(8,128)(2,1)S(1)}, u32[]{:S(2)}, u32[]{:S(2)}) collective-permute-start(bf16[4,144,384]{2,1,0:T(8,128)(2,1)S(1)} %pad_maximum_fusion), channel_id=1, source_target_pairs={{0,4},{1,5},{2,6},{3,7},{4,0},{5,1},{6,2},{7,3},{8,12},{9,13},{10,... | collective-permute-start | bytes 1327112 | tf_op jit(solution)/shard_map/ppermute | solution.py:961
  36.9 25.8 %collective-permute-start.6 = (bf16[8,144,384]{2,1,0:T(8,128)(2,1)S(1)}, bf16[8,144,384]{2,1,0:T(8,128)(2,1)S(1)}, u32[]{:S(2)}, u32[]{:S(2)}) collective-permute-start(bf16[8,144,384]{2,1,0:T(8,128)(2,1)S(1)} %constant_dynamic-update-slice_fusion.rest_0_.rest_2_), channel_id=1, source_target_pairs={{0,2},{1,3},{2,0},{3,1},{4,6},{5,7},{6,4},{7,5},{8,10},{9,11},{10,... | collective-permute-start | bytes 2654216 | tf_op jit(solution)/shard_map/ppermute | solution.py:961
  37.3 24.8 %collective-permute-start.1 = (bf16[12,384]{1,0:T(8,128)(2,1)S(1)}, bf16[12,384]{1,0:T(8,128)(2,1)S(1)}, u32[]{:S(2)}, u32[]{:S(2)}) collective-permute-start(bf16[12,384]{1,0:T(8,128)(2,1)S(1)} %concatenate.32), channel_id=1, source_target_pairs={{0,1},{1,0},{2,3},{3,2},{4,5},{5,4},{6,7},{7,6},{8,9},{9,8},{10,11... | collective-permute-start | bytes 27656 | tf_op jit(solution)/shard_map/ppermute | solution.py:925
  77.5 75.8 %collective-permute-start.7 = (bf16[8,144,384]{2,1,0:T(8,128)(2,1)}, bf16[8,144,384]{2,1,0:T(8,128)(2,1)S(1)}, u32[]{:S(2)}, u32[]{:S(2)}) collective-permute-start(bf16[8,144,384]{2,1,0:T(8,128)(2,1)} %get-tuple-element.66), channel_id=1, source_target_pairs={{0,1},{1,0},{2,3},{3,2},{4,5},{5,4},{6,7},{7,6},{8,9},{9,8},{10,11... | collective-permute-start | bytes 2654216 | tf_op jit(solution)/shard_map/ppermute | solution.py:961
  79.1 74.2 %collective-permute-start.8 = (bf16[8,144,384]{2,1,0:T(8,128)(2,1)}, bf16[8,144,384]{2,1,0:T(8,128)(2,1)S(1)}, u32[]{:S(2)}, u32[]{:S(2)}) collective-permute-start(bf16[8,144,384]{2,1,0:T(8,128)(2,1)} %get-tuple-element.66), channel_id=1, source_target_pairs={{0,3},{1,2},{2,1},{3,0},{4,7},{5,6},{6,5},{7,4},{8,11},{9,10},{10,... | collective-permute-start | bytes 2654216 | tf_op jit(solution)/shard_map/ppermute | solution.py:961
  168.4 76.6 %collective-permute-start.9 = (bf16[1024,768]{1,0:T(8,128)(2,1)}, bf16[1024,768]{1,0:T(8,128)(2,1)S(1)}, u32[]{:S(2)}, u32[]{:S(2)}) collective-permute-start(bf16[1024,768]{1,0:T(8,128)(2,1)} %get-tuple-element.72), channel_id=1, source_target_pairs={{0,1},{1,0},{2,3},{3,2},{4,5},{5,4},{6,7},{7,6},{8,9},{9,8},{10,11... | collective-permute-start | bytes 4718600 | tf_op jit(solution)/shard_map/ppermute | solution.py:895
  351.3 94.9 %collective-permute-start.10 = (bf16[1024,768]{1,0:T(8,128)(2,1)S(1)}, bf16[1024,768]{1,0:T(8,128)(2,1)S(1)}, u32[]{:S(2)}, u32[]{:S(2)}) collective-permute-start(bf16[1024,768]{1,0:T(8,128)(2,1)S(1)} %copy-done.28), channel_id=1, source_target_pairs={{1,0},{0,1},{3,2},{2,3},{5,4},{4,5},{7,6},{6,7},{9,8},{8,9},{11,10... | collective-permute-start | bytes 4718600 | tf_op jit(solution)/shard_map/ppermute | solution.py:895
  352.9 92.8 %collective-permute-start.11 = (bf16[16,768]{1,0:T(8,128)(2,1)S(1)}, bf16[16,768]{1,0:T(8,128)(2,1)S(1)}, u32[]{:S(2)}, u32[]{:S(2)}) collective-permute-start(bf16[16,768]{1,0:T(8,128)(2,1)S(1)} %copy-done.17), channel_id=1, source_target_pairs={{0,1},{1,0},{2,3},{3,2},{4,5},{5,4},{6,7},{7,6},{8,9},{9,8},{10,11... | collective-permute-start | bytes 73736 | tf_op jit(solution)/shard_map/ppermute | solution.py:925
  457.5 44.4 %collective-permute-start.12 = (bf16[1024,768]{1,0:T(8,128)(2,1)}, bf16[1024,768]{1,0:T(8,128)(2,1)S(1)}, u32[]{:S(2)}, u32[]{:S(2)}) collective-permute-start(bf16[1024,768]{1,0:T(8,128)(2,1)} %get-tuple-element.91.rest_3_), channel_id=1, source_target_pairs={{1,0},{0,1},{3,2},{2,3},{5,4},{4,5},{7,6},{6,7},{9,8},{8,9},{11,10... | collective-permute-start | bytes 4718600 | tf_op jit(solution)/shard_map/ppermute | solution.py:895
  519.6 4.2 collective-permute-start.13
  528.7 18.2 %collective-permute-start.14 = (bf16[4,160,384]{2,1,0:T(8,128)(2,1)}, bf16[4,160,384]{2,1,0:T(8,128)(2,1)S(1)}, u32[]{:S(2)}, u32[]{:S(2)}) collective-permute-start(bf16[4,160,384]{2,1,0:T(8,128)(2,1)} %get-tuple-element.98), channel_id=1, source_target_pairs={{0,1},{1,0},{2,3},{3,2},{4,5},{5,4},{6,7},{7,6},{8,9},{9,8},{10,11... | collective-permute-start | bytes 1474568 | tf_op jit(solution)/shard_map/ppermute | solution.py:961
  529.0 17.9 %collective-permute-start.15 = (bf16[4,160,384]{2,1,0:T(8,128)(2,1)}, bf16[4,160,384]{2,1,0:T(8,128)(2,1)S(1)}, u32[]{:S(2)}, u32[]{:S(2)}) collective-permute-start(bf16[4,160,384]{2,1,0:T(8,128)(2,1)} %get-tuple-element.99), channel_id=1, source_target_pairs={{0,4},{1,5},{2,6},{3,7},{4,0},{5,1},{6,2},{7,3},{8,12},{9,13},{10,... | collective-permute-start | bytes 1474568 | tf_op jit(solution)/shard_map/ppermute | solution.py:961
  530.8 23.2 %collective-permute-start.16 = (bf16[4,160,384]{2,1,0:T(8,128)(2,1)}, bf16[4,160,384]{2,1,0:T(8,128)(2,1)S(1)}, u32[]{:S(2)}, u32[]{:S(2)}) collective-permute-start(bf16[4,160,384]{2,1,0:T(8,128)(2,1)} %get-tuple-element.100), channel_id=1, source_target_pairs={{0,5},{1,4},{2,7},{3,6},{4,1},{5,0},{6,3},{7,2},{8,13},{9,12},{10,... | collective-permute-start | bytes 1474568 | tf_op jit(solution)/shard_map/ppermute | solution.py:961
  557.1 6.5 %collective-permute-start.17 = (bf16[1,160,384]{2,1,0:T(8,128)(2,1)}, bf16[1,160,384]{2,1,0:T(8,128)(2,1)S(1)}, u32[]{:S(2)}, u32[]{:S(2)}) collective-permute-start(bf16[1,160,384]{2,1,0:T(8,128)(2,1)} %get-tuple-element.105), channel_id=1, source_target_pairs={{0,8},{1,9},{2,10},{3,11},{4,12},{5,13},{6,14},{7,15},{8,0},{9,1},... | collective-permute-start | bytes 368648 | tf_op jit(solution)/shard_map/ppermute | solution.py:961
  558.3 11.9 %collective-permute-start.18 = (bf16[1,160,384]{2,1,0:T(8,128)(2,1)}, bf16[1,160,384]{2,1,0:T(8,128)(2,1)S(1)}, u32[]{:S(2)}, u32[]{:S(2)}) collective-permute-start(bf16[1,160,384]{2,1,0:T(8,128)(2,1)} %get-tuple-element.106), channel_id=1, source_target_pairs={{0,16},{1,17},{2,18},{3,19},{4,20},{5,21},{6,22},{7,23},{8,24},{9,... | collective-permute-start | bytes 368648 | tf_op jit(solution)/shard_map/ppermute | solution.py:961
  561.0 9.1 %collective-permute-start.19 = (bf16[1,160,384]{2,1,0:T(8,128)(2,1)}, bf16[1,160,384]{2,1,0:T(8,128)(2,1)S(1)}, u32[]{:S(2)}, u32[]{:S(2)}) collective-permute-start(bf16[1,160,384]{2,1,0:T(8,128)(2,1)} %get-tuple-element.107), channel_id=1, source_target_pairs={{0,24},{1,25},{2,26},{3,27},{4,28},{5,29},{6,30},{7,31},{8,16},{9,... | collective-permute-start | bytes 368648 | tf_op jit(solution)/shard_map/ppermute | solution.py:961
  (20 other events, 98.0 us)
Sparse Core Ops, SparseCore 0:
  10.9 103.8 all-gather.2
  350.1 154.7 reduce-scatter.1

commit v5 on v2

--- a/solution.py
+++ b/solution.py
@@ -50,7 +50,22 @@
 
 
 def attend_kernel(
-    info, q_ref, k_ref, v_ref, out_ref, p_ref, sum_ref, keys, vals, ques, bound, turned, *, chunk, across, span
+    info,
+    q_ref,
+    k_ref,
+    v_ref,
+    out_ref,
+    p_ref,
+    sum_ref,
+    keys,
+    vals,
+    ques,
+    bound,
+    turned,
+    *,
+    chunk,
+    across,
+    span,
 ):
     pos = pl.program_id(1)
     kv = k_ref.shape[0]
@@ -116,8 +131,8 @@
     out_ref[...] = turned[...].T.astype(BF16)
 
 
-def attend(info, q_from, k_from, v_from, span):
-    (queries, q_at), (keys, k_at), (values, v_at) = q_from, k_from, v_from
+def attend(info, sources, span):
+    (queries, q_at), (keys, k_at), (values, v_at) = sources
     rows, kv = queries.shape[0], keys.shape[0]
     size = chunk_of(rows)
     pairs = HEADS // 2
@@ -134,9 +149,9 @@
             num_scalar_prefetch=1,
             grid=(pairs, rows // size),
             in_specs=[
-                pl.BlockSpec((rows, PAIR), lambda j, c, s: (0, q_at + j)),
-                pl.BlockSpec((kv, PAIR), lambda j, c, s: (0, k_at + j)),
-                pl.BlockSpec((kv, PAIR), lambda j, c, s: (0, v_at + j)),
+                pl.BlockSpec((rows, PAIR), lambda j, c, s: (0, q_at(j))),
+                pl.BlockSpec((kv, PAIR), lambda j, c, s: (0, k_at(j))),
+                pl.BlockSpec((kv, PAIR), lambda j, c, s: (0, v_at(j))),
             ],
             out_specs=(
                 pl.BlockSpec((size, PAIR), lambda j, c, s: (c, j)),
@@ -230,8 +245,8 @@
         gq_ref[...] = value.astype(BF16)
 
 
-def attend_back(info, q_from, k_from, v_from, grad, context, sums, probs, span, units, before, events=()):
-    (queries, q_at), (keys, k_at), (values, v_at) = q_from, k_from, v_from
+def attend_back(info, sources, grad, context, sums, probs, span, units, before, events=()):
+    (queries, q_at), (keys, k_at), (values, v_at) = sources
     rows, kv = queries.shape[0], keys.shape[0]
     pairs = HEADS // 2
     wide = HEADS * HDIM
@@ -240,8 +255,11 @@
     cut = 2 if more else 1
     rows, kv = rows // cut, kv // cut
     out_rows = [rows, kv, kv]
+    heights = [rows * cut, kv * cut, kv * cut]
     units = jnp.array(list(zip(*units)), jnp.int32)
-    col = lambda height, at=0: pl.BlockSpec((height, PAIR), lambda j, c, s, u: (0, at + j))
+    col = lambda height, at=lambda j: j: pl.BlockSpec(
+        (height, PAIR), lambda j, c, s, u: (0, at(j))
+    )
     return pl.pallas_call(
         functools.partial(
             attend_back_kernel,
@@ -251,7 +269,7 @@
             more=more,
             extra=len(events),
         ),
-        out_shape=tuple(jax.ShapeDtypeStruct((height, wide), BF16) for height in out_rows),
+        out_shape=tuple(jax.ShapeDtypeStruct((height, wide), BF16) for height in heights),
         grid_spec=pltpu.PrefetchScalarGridSpec(
             num_scalar_prefetch=2,
             grid=(pairs, units.shape[1]),
@@ -279,6 +297,7 @@
                 pltpu.VMEM((kv, PAIR), F32),
             ],
         ),
+        input_output_aliases={9 + t: t for t in range(3)} if more else {},
         compiler_params=pltpu.CompilerParams(vmem_limit_bytes=60 * 2**20),
         name="attend_back_last" if more else "attend_back",
     )(info, units, queries, keys, values, grad, context, sums, probs, *(before or ()), *events)
@@ -358,10 +377,15 @@
     return [pl.BlockSpec(memory_space=pl.ANY)] * len(arrays)
 
 
-def queries_kernel(info, kept_ref, other_ref, bias_ref, *rest, split, grid_of):
+def queries_kernel(info, kept_ref, other_ref, bias_ref, *rest, split, grid_of, carry):
     count = len(grid_of.bundles)
-    packed, (out_ref, mat_q, mat_k, mat_v, sems) = rest[:count], rest[count:]
+    packed, rest = rest[:count], rest[count:]
     step = pl.program_id(0)
+    if carry:
+        pair_ref, out_ref, mat_q, mat_k, mat_v, picked, sems = rest
+        picked[...] = pair_ref[0]
+    else:
+        out_ref, mat_q, mat_k, mat_v, sems = rest
     mats = [mat_q, mat_k, mat_v]
 
     @pl.when(step == 0)
@@ -390,27 +414,34 @@
     return pl.BlockSpec(shape, lambda i, s: (0,) * len(shape))
 
 
-def queries_keys_values(info, kept, other, weights, bias):
+def queries_keys_values(info, kept, other, weights, bias, pair):
     block_len, width = other.shape
     tile = min(512, block_len)
     split = block_len // tile
+    part = block_len // (2 * split)
+    carried = [] if pair is None else [pair]
     mat = jax.ShapeDtypeStruct((width, width), BF16)
     return pl.pallas_call(
-        functools.partial(queries_kernel, split=split, grid_of=weights.grid_of),
-        out_shape=(jax.ShapeDtypeStruct((2 * block_len, 3 * width), BF16), mat, mat, mat),
+        functools.partial(
+            queries_kernel, split=split, grid_of=weights.grid_of, carry=bool(carried)
+        ),
+        out_shape=(jax.ShapeDtypeStruct((2 * block_len, 3 * width), BF16), mat, mat, mat)
+        + (jax.ShapeDtypeStruct((block_len, width), BF16),) * len(carried),
         grid_spec=pltpu.PrefetchScalarGridSpec(
             num_scalar_prefetch=1,
             grid=(2 * split,),
             in_specs=split_specs(2, tile, split, width)
             + [whole_spec(bias.shape)]
-            + any_specs(weights.packed),
+            + any_specs(weights.packed)
+            + [pl.BlockSpec((1, part, width), lambda i, s: (1 - s[2], i, 0))] * len(carried),
             out_specs=(pl.BlockSpec((tile, 3 * width), lambda i, s: (i, 0)),)
-            + (whole_spec(mat.shape),) * 3,
+            + (whole_spec(mat.shape),) * 3
+            + (pl.BlockSpec((part, width), lambda i, s: (i, 0)),) * len(carried),
             scratch_shapes=[pltpu.SemaphoreType.DMA((weights.grid_of.count(),))],
         ),
         compiler_params=pltpu.CompilerParams(vmem_limit_bytes=60 * 2**20),
         name="queries",
-    )(info, kept, other, bias, *weights.packed)
+    )(info, kept, other, bias, *weights.packed, *carried)
 
 
 def normal(values):
@@ -651,7 +682,12 @@
     )(info, *hidden, *cots, context, cls_row, vectors, inner_bias, *weights.packed)
 
 
-def input_grad_kernel(info, gq_ref, gk_ref, gv_ref, resid_ref, mat_q, mat_k, mat_v, grad_ref, *, kept):
+def input_grad_kernel(info, gq_ref, gk_ref, gv_ref, resid_ref, mat_q, mat_k, mat_v, *rest, kept, join):
+    if join:
+        arrived, grad_ref, joined = rest[0], rest[-2], rest[-1]
+        joined[0] = arrived[...].astype(joined.dtype)
+    else:
+        grad_ref = rest[-1]
     total = resid_ref[...]
     for ref, mat in zip((gq_ref, gk_ref, gv_ref), (mat_q, mat_k, mat_v)):
         total += project_back(ref[...], mat[...])
@@ -661,7 +697,7 @@
         grad_ref[...] = total.astype(grad_ref.dtype)
 
 
-def input_grad(info, grads, resid, mats, out_shape, dtype, kept):
+def input_grad(info, grads, resid, mats, out_shape, dtype, kept, join=(), events=()):
     rows, width = resid.shape
     block_len = rows // 2
     tile = min(512, block_len)
@@ -669,22 +705,32 @@
     off = 0 if kept else split
     spec = pl.BlockSpec((tile, width), lambda i, s: (i + off, 0))
     place = kept_spec(tile, split, width) if kept else other_spec(tile, 0, width)
+    out = (jax.ShapeDtypeStruct(out_shape, dtype),)
+    in_specs = [spec] * 4 + [whole_spec(mat.shape) for mat in mats]
+    out_specs = (place,)
+    aliases = {}
+    if join:
+        in_specs += [pl.BlockSpec((tile, width), lambda i, s: (i, 0))] + any_specs(join[:1])
+        out += (jax.ShapeDtypeStruct(join[0].shape, join[0].dtype),)
+        out_specs += (pl.BlockSpec((1, tile, width), lambda i, s: (1 - s[2], i, 0)),)
+        aliases = {len(in_specs): 1}
     return pl.pallas_call(
-        functools.partial(input_grad_kernel, kept=kept),
-        out_shape=jax.ShapeDtypeStruct(out_shape, dtype),
+        functools.partial(input_grad_kernel, kept=kept, join=bool(join)),
+        out_shape=out,
         grid_spec=pltpu.PrefetchScalarGridSpec(
             num_scalar_prefetch=1,
             grid=(split,),
-            in_specs=[spec] * 4 + [whole_spec(mat.shape) for mat in mats],
-            out_specs=place,
-        ),
+            in_specs=in_specs + any_specs(events),
+            out_specs=out_specs,
+        ),
+        input_output_aliases=aliases,
         compiler_params=pltpu.CompilerParams(vmem_limit_bytes=60 * 2**20),
         name="input_grad_kept" if kept else "input_grad_other",
-    )(info, *grads, resid, *mats)
+    )(info, *grads, resid, *mats, *join[::-1], *events)
 
 
 def head_grads_kernel(info, hid_kept, hid_other, *rest, split, grid_of, outs, extra):
-    kept, other, rest = rest[:3], rest[3:6], rest[6 + extra :]
+    found, rest = rest[:3], rest[3 + extra :]
     sums, (acc, mat_q, mat_k, mat_v, totals, vec_low, sems, vec_sems) = rest[:outs], rest[outs:]
     mats = [mat_q, mat_k, mat_v]
     step = pl.program_id(0)
@@ -695,7 +741,7 @@
         totals[...] = jnp.zeros_like(totals)
 
     rows = rows_of(hid_kept, hid_other, step, split)
-    grads = [jnp.where(step < split, a[...], b[...]) for a, b in zip(kept, other)]
+    grads = [ref[...] for ref in found]
     for t, grad in enumerate(grads):
         acc[t] += weight_grad(rows, grad)
     add_rows(totals, 0, grads[0].astype(F32))
@@ -724,13 +770,11 @@
         wait_all(tails)
 
 
-def head_grads(info, hidden, kept, other, grid_of, outs, events=()):
+def head_grads(info, hidden, grads, grid_of, outs, events=()):
     block_len, width = hidden[1].shape
     tile = min(512, block_len)
     split = block_len // tile
-    last = other[0].shape[0] // tile - split
-    kept_rows = pl.BlockSpec((tile, width), lambda i, s: (jnp.minimum(i, split - 1), 0))
-    other_rows = pl.BlockSpec((tile, width), lambda i, s: (jnp.maximum(i, split), 0))
+    rows = pl.BlockSpec((tile, width), lambda i, s: (i, 0))
     block = (grid_of.slots // outs, 3 * grid_of.r + 16, grid_of.c)
     return pl.pallas_call(
         functools.partial(
@@ -740,7 +784,7 @@
         grid_spec=pltpu.PrefetchScalarGridSpec(
             num_scalar_prefetch=1,
             grid=(2 * split,),
-            in_specs=split_specs(2, tile, split, width) + [kept_rows] * 3 + [other_rows] * 3 + any_specs(events),
+            in_specs=split_specs(2, tile, split, width) + [rows] * 3 + any_specs(events),
             out_specs=(pl.BlockSpec(memory_space=pl.ANY),) * outs,
             scratch_shapes=[pltpu.VMEM((3, width, width), F32)]
             + [pltpu.VMEM((width, width), BF16)] * 3
@@ -753,7 +797,7 @@
         ),
         compiler_params=pltpu.CompilerParams(vmem_limit_bytes=60 * 2**20),
         name="head_grads",
-    )(info, *hidden, *kept, *other, *events)
+    )(info, *hidden, *grads, *events)
 
 
 def pick_kernel(info, pair_ref, *rest):
@@ -819,6 +863,24 @@
         compiler_params=pltpu.CompilerParams(vmem_limit_bytes=60 * 2**20),
         name="stack_rows",
     )(*blocks, *events)
+
+
+def join_kernel(*refs, count):
+    out = refs[-1]
+    each = refs[0].shape[0]
+    for k, ref in enumerate(refs[:count]):
+        out[k * each : (k + 1) * each] = ref[...]
+
+
+def join_blocks(parts, events):
+    shape = (parts[0].shape[0] * len(parts),) + parts[0].shape[1:]
+    return pl.pallas_call(
+        functools.partial(join_kernel, count=len(parts)),
+        out_shape=jax.ShapeDtypeStruct(shape, BF16),
+        in_specs=[pl.BlockSpec(memory_space=pltpu.VMEM)] * len(parts) + any_specs(events),
+        compiler_params=pltpu.CompilerParams(vmem_limit_bytes=60 * 2**20),
+        name="join_blocks",
+    )(*parts, *events)
 
 
 def add_kernel(*refs, count, extra):
@@ -882,9 +944,7 @@
         self.second = [(i, (1 - i % 2) * self.per + i // 2) for i in range(self.n)]
         self.stays = all(a == b for a, b in self.first)
 
-    def pick(self, info, pair, events=()):
-        if self.stays:
-            return pick_other(info, pair, events)
+    def pick(self, pair):
         return lax.dynamic_index_in_dim(pair, 1 - self.part, 0, keepdims=False)
 
     def gather(self, pair, picked):
@@ -939,13 +999,10 @@
     return lax.ppermute(block, both, [(i, i ^ mask) for i in places])
 
 
-def xor_gather(block, stages):
-    found, masks = block[None], [0]
-    for stage in stages:
-        parts = [found] + [exchanged(found, mask) for mask in stage]
-        masks = masks + [held ^ mask for mask in stage for held in masks]
-        found = jnp.concatenate(parts, 0)
-    return found, masks
+def xor_gather(found, masks, stage, events):
+    parts = [found] + [exchanged(found, mask) for mask in stage]
+    masks = [held ^ mask for mask in [0] + stage for held in masks]
+    return join_blocks(parts, events), masks
 
 
 def xor_masks(stages):
@@ -965,43 +1022,40 @@
 
 
 class Weights:
-    def __init__(self, shards, by_pairs, events=()):
+    def __init__(self, shards, vectors=None, begin=None):
         self.shapes = [s.shape for s in shards]
         self.m, self.n = lax.axis_size("batch"), lax.axis_size("blk")
         m, n = self.m, self.n
         r, c = min(s[0] for s in self.shapes), min(s[1] for s in self.shapes)
         self.fits = r % 16 == 0 and c % 128 == 0
-        powers = m & (m - 1) == 0 and n & (n - 1) == 0 and m >= 8
-        self.by_pairs = by_pairs and self.fits and powers
+        powers = m & (m - 1) == 0 and n == 2 and m >= 8
+        self.by_pairs = begin is not None and self.fits and powers
         every = list(range(len(shards)))
         if self.by_pairs:
             y, core, x = list(range(1, n)), [n], [2 * n]
             z = list(range(4 * n, m * n, 4 * n))
-            near = pack_after(shards, ())
+            near = pack_after([*shards, vectors], ())
             near = [near] + [exchanged(near, mask) for mask in y]
             cut = sum(s.size for s in shards[:-1]) // c
-            cuts = [cut, near[0].shape[0] - cut]
-            near = stack_rows(near, cuts, events(near))
-            self.packed, bundles, self.half = [], [], []
-            for rows, members, order in (
-                (near[0], every[:-1], [z, x]),
-                (near[1], every[-1:], [x, z]),
-            ):
-                part, masks = xor_gather(rows, order[:1])
-                self.half.append(part)
-                part, more = xor_gather(part, order[1:])
-                masks = [a ^ b for a in more for b in masks]
+            cuts = [cut, shards[-1].size // c, vectors.shape[0]]
+            picked, arrival = begin(near[1:])
+            most, least, self.vectors = stack_rows(near, cuts, (picked,))
+            flat = lambda part: part.reshape(-1, *part.shape[-2:])
+            first = [0] + y
+            b, b_masks = xor_gather(flat(least), first, x, ())
+            a, a_masks = xor_gather(flat(most), first, z, (b,))
+            b, b_masks = xor_gather(b, b_masks, z, ())
+            a, a_masks = xor_gather(a, a_masks, x, (arrival, b))
+            self.packed, bundles = [], []
+            for part, masks, members in ((a, a_masks, every[:-1]), (b, b_masks, every[-1:])):
                 for mask in [0] + core:
-                    block = exchanged(part, mask) if mask else part
-                    self.packed.append(block.reshape(-1, *rows.shape[1:]))
-                    bundles.append(([a ^ b ^ mask for a in masks for b in [0] + y], members))
+                    self.packed.append(exchanged(part, mask) if mask else part)
+                    bundles.append(([held ^ mask for held in masks], members))
             self.grid_of = Pieces((r, c), (m, n), bundles)
             self.stages = [core, [a ^ b for a in [0] + x for b in [0] + y][1:], z]
             self.sums_of = Pieces((r, c), (m, n), [(xor_masks(self.stages), every)])
             return
-        if callable(events):
-            events = ()
-        packed = pack_after(shards, events) if self.fits else pack(shards)
+        packed = pack_after(shards, ()) if self.fits else pack(shards)
         packed = lax.all_gather(packed, ("batch", "blk"), axis=0)
         if self.fits:
             self.grid_of = Pieces((r, c), (m, n), [(None, every)])
@@ -1015,9 +1069,6 @@
                 whole.append(part.reshape(m * rows, n * cols))
             self.packed = [pack(whole)[None]]
         self.sums_of = self.grid_of
-
-    def halfway(self):
-        return tuple(self.half) if self.by_pairs else ()
 
     def scatter(self, sums, meanwhile=()):
         extra = 16
@@ -1117,29 +1168,42 @@
     narrow = jnp.stack(
         [b_query, b_value, b_out, norm1_gain, norm1_shift, b_outer, norm2_gain, norm2_shift]
     )
-    vec_all = plan.all_blocks(jnp.concatenate([narrow, b_inner.reshape(-1, share)], 0)).astype(F32)
-    narrow = vec_all[:, :8].transpose(1, 0, 2).reshape(8, width)
-    bias_inner = vec_all[:, 8:].reshape(1, -1)
+    parts = [narrow, b_inner.reshape(-1, share)]
+    used = narrow.shape[0] + parts[1].shape[0]
+    parts.append(jnp.zeros((-used % 16, share), BF16))
+    vec_shard = jnp.concatenate(parts, 0)
+
+    hidden = None
+
+    def begin(near):
+        nonlocal hidden
+        picked = pick_other(info, hidden_in, near)
+        hidden = plan.gather(hidden_in, picked)
+        return picked, hidden[1]
+
+    heads = Weights([w_query, w_key, w_value], vec_shard, begin if plan.stays else None)
+    if hidden is None:
+        hidden = plan.gather(hidden_in, plan.pick(hidden_in))
+    if heads.by_pairs:
+        vec_all = jnp.where(plan.me == 0, heads.vectors, heads.vectors[::-1])
+    else:
+        vec_all = plan.all_blocks(vec_shard)
+    dense = Weights([w_out, w_inner, w_outer])
+    narrow = vec_all[:, :8].transpose(1, 0, 2).reshape(8, width).astype(F32)
+    bias_inner = vec_all[:, 8:used].reshape(1, -1).astype(F32)
     bias_heads = jnp.concatenate([narrow[0:1], jnp.zeros_like(narrow[0:1]), narrow[1:2]], 1)
 
-    picked = []
-
-    def pick_hidden(near):
-        picked.append(plan.pick(info, hidden_in, near))
-        return picked
-
-    heads = Weights([w_query, w_key, w_value], True, pick_hidden)
-    hidden = plan.gather(hidden_in, picked[0] if picked else plan.pick(info, hidden_in))
-    dense = Weights([w_out, w_inner, w_outer], False, heads.halfway())
-    qkv, *mats = queries_keys_values(info, *hidden, heads, bias_heads)
-    cots = plan.gather(cot_out, plan.pick(info, cot_out, (qkv,)))
+    qkv, *mats = queries_keys_values(
+        info, *hidden, heads, bias_heads, cot_out if plan.stays else None
+    )
+    cots = plan.gather(cot_out, mats.pop() if plan.stays else plan.pick(cot_out))
+    at = lambda kind: lambda j: kind * HEADS // 2 + j
     if per == 1:
-        kv, key_at = qkv, width // PAIR
+        sources = [(qkv, at(kind)) for kind in range(3)]
     else:
         kv = lax.all_gather(qkv[:, width:], "blk", axis=0, tiled=True, axis_index_groups=fleets)
-        key_at = 0
-    sources = ((qkv, 0), (kv, key_at), (kv, key_at + width // PAIR))
-    context_low, probs, sums = attend(info, *sources, span)
+        sources = [(qkv, at(0)), (kv, at(0)), (kv, at(1))]
+    context_low, probs, sums = attend(info, sources, span)
 
     own_cls = lax.dynamic_index_in_dim(cot_cls, plan.passage, 0, keepdims=True).astype(F32)
     layer_kept, layer_other, top, grad_context, grad_resid, dense_sums = middle(
@@ -1148,17 +1212,25 @@
     part_wo, part_wi, part_wu, dense_vecs = dense.scatter([dense_sums])
     part_bo, part_g1, part_s1, part_bu, part_g2, part_s2 = [dense_vecs[t] for t in range(6)]
     part_bi = dense_vecs[6 : 6 + b_inner.size // share].reshape(-1)
-    layer_rows = plan.join(info, layer_kept, plan.send_back(layer_other))
+    layer_other = plan.send_back(layer_other)
     tops = plan.all_blocks(top)[::per, 0, :]
     cls_part = lax.dynamic_slice_in_dim(tops, plan.me * share, share, 1)
 
     back = functools.partial(
-        attend_back, info, *sources, grad_context, context_low, sums, probs, span
+        attend_back, info, sources, grad_context, context_low, sums, probs, span
     )
     give = functools.partial(input_grad, info, resid=grad_resid, mats=mats)
     if per == 1:
         most = back([(1, 1), (1, 0), (0, 1)], None)
-        other = give(most, out_shape=(block_len, width), dtype=BF16, kept=False)
+        other, *layer_rows = give(
+            most,
+            out_shape=(block_len, width),
+            dtype=BF16,
+            kept=False,
+            join=(layer_kept, layer_other) if plan.stays else (),
+            events=(cls_part,),
+        )
+        layer_rows = layer_rows[0] if layer_rows else plan.join(info, layer_kept, layer_other)
         rest = back([(0, 0)], most, (other, layer_rows))
         other = plan.send_back(other)
     else:
@@ -1168,14 +1240,18 @@
             lax.psum_scatter(g, "blk", scatter_dimension=0, tiled=True, axis_index_groups=fleets)
             for g in grad_kv
         ]
-        other = plan.send_back(give(most, out_shape=(block_len, width), dtype=BF16, kept=False))
+        (other,) = give(most, out_shape=(block_len, width), dtype=BF16, kept=False)
+        other = plan.send_back(other)
         rest = most
+        layer_rows = plan.join(info, layer_kept, layer_other)
     head_sums = head_grads(
-        info, hidden, rest, most, heads.sums_of, 2 if heads.by_pairs else 1, (other,)
+        info, hidden, rest, heads.sums_of, 2 if heads.by_pairs else 1, (other,)
     )
-    kept = give(rest, out_shape=hidden[0].shape, dtype=F32, kept=True)
+    (kept,) = give(rest, out_shape=hidden[0].shape, dtype=F32, kept=True)
     grad_input = plan.join(info, kept, other)
-    part_wq, part_wk, part_wv, head_vecs = heads.scatter(head_sums, (grad_input,))
+    part_wq, part_wk, part_wv, head_vecs = heads.scatter(
+        head_sums, (grad_input, part_wo, dense_vecs)
+    )
     part_bq, part_bv = head_vecs[0], head_vecs[1]
     return (
         layer_rows,

time: 591 us -> 593 us (level)
  starting transfers between devices: 98 us -> 118 us
  waiting for transfers between devices: 73 us -> 53.4 us
  local copies, waits for them, and re-layouts: 17.6 us -> 30.2 us
  other arithmetic: 8.19 us -> 1.23 us
    ppermute x18, starting transfers between devices: 87.9 us -> 112 us  [exchanged(): return lax.ppermute(block, both, [(i, i ^ mask) for i in places])]
    ppermute x2 -> x1, waiting for transfers between devices: 19.7 us -> 0.01 us  [all_blocks(): other = lax.ppermute(block, 'blk', [(0, 1), (1, 0)])]
    pallas_call x2 -> x6, Pallas kernels: 18.9 us -> 27.9 us  [the longest x2 19.9 us: input_grad(): pl.pallas_call(functools.partial(input_grad_kernel, kept=kept, join=bool(...]
    unnamed x53 -> x57, local copies, waits for them, and re-layouts: 8.92 us -> 15.9 us
    concatenate x4 -> x0, other arithmetic: 6.91 us -> none  [xor_gather(): found = jnp.concatenate(parts, 0)]
    pallas_call x1, Pallas kernels: 64.5 us -> 57.7 us  [attend(): pl.pallas_call(functools.partial(attend_kernel, chunk=min(256, kv), acros...]
  transfers between devices with their start and end apart: 26 -> 25, of which waited for: 11 -> 10; matrix products, arithmetic and copies ran while one was open for 2% -> 3% of each run, Pallas kernels for 45% -> 44%
where the time goes in v5:
time: 593 us; the launch traced here: 587 us
  Pallas kernels  370 us (62%)
  starting transfers between devices  118 us (20%)
  waiting for transfers between devices  53.4 us (9%)
  local copies, waits for them, and re-layouts  30.2 us (5%)
  between operations  14.5 us (2%)
    pallas_call x2, Pallas kernels, attend_back(): pl.pallas_call(functools.partial(attend_back_kernel, chunk=min(512, part)...  126 us
    ppermute x18, starting transfers between devices, exchanged(): return lax.ppermute(block, both, [(i, i ^ mask) for i in places])  112 us
    pallas_call x1, Pallas kernels, middle(): pl.pallas_call(functools.partial(middle_kernel, split=split, grid_of=grid...  104 us
    pallas_call x1, Pallas kernels, attend(): pl.pallas_call(functools.partial(attend_kernel, chunk=min(256, kv), acros...  57.7 us
    ppermute x18, waiting for transfers between devices, exchanged(): return lax.ppermute(block, both, [(i, i ^ mask) for i in places])  47.9 us
    pallas_call x2, Pallas kernels, input_grad(): pl.pallas_call(functools.partial(input_grad_kernel, kept=kept, join=bool(...  19.9 us
    pallas_call x1, Pallas kernels, head_grads(): pl.pallas_call(functools.partial(head_grads_kernel, split=split, grid_of=...  16.6 us
    pallas_call x1, Pallas kernels, queries_keys_values(): pl.pallas_call(functools.partial(queries_kernel, split=split, grid_of=wei...  16.5 us
  transfers between devices with their start and end apart: 25, of which 10 were waited for; matrix products, arithmetic and copies ran while one was open for 3% of the time, Pallas kernels for 44%

profile of v5, /device:TPU:0, one launch (start us, length us, event | category | flops | bytes accessed | tf_op | source)
XLA Modules:
  0.0 587.5 jit_solution(17709555766784962112)
XLA Ops:
  17.9 3.0 collective-permute-start
  23.4 2.2 collective-permute-done.rest_0_.refs_1_
  26.2 3.0 pick_other.1.refs_2_
  29.2 2.4 collective-permute-start.1
  33.3 3.6 collective-permute-start.4
  39.0 3.2 collective-permute-done.5.refs_1_
  44.5 3.6 collective-permute-done.3.refs_2_
  49.4 2.0 join_blocks.5.refs_0_
  52.9 5.1 collective-permute-start.9
  58.6 6.7 %collective-permute-done.9.refs_3_ = bf16[4,48,384]{2,1,0:T(8,128)(2,1)S(1)} collective-permute-done((bf16[4,48,384]{2,1,0:T(8,128)(2,1)}, bf16[4,48,384]{2,1,0:T(8,128)(2,1)S(1)}, u32[]{:S(2)}, u32[]{:S(2)}) %collective-permute-start.9) | collective-permute-done | bytes 147488 | tf_op jit(solution)/shard_map/ppermute | solution.py:999
  65.3 10.1 %collective-permute-done.8.refs_2_ = bf16[4,48,384]{2,1,0:T(8,128)(2,1)S(1)} collective-permute-done((bf16[4,48,384]{2,1,0:T(8,128)(2,1)}, bf16[4,48,384]{2,1,0:T(8,128)(2,1)S(1)}, u32[]{:S(2)}, u32[]{:S(2)}) %collective-permute-start.8) | collective-permute-done | bytes 147488 | tf_op jit(solution)/shard_map/ppermute | solution.py:999
  76.7 2.0 join_blocks.6.refs_3_.rest_2_
  80.8 2.4 join_blocks.7.rest_0_
  84.4 2.6 collective-permute-done.11.rest_3_
  88.8 16.5 %queries.1 = (bf16[2048,2304]{1,0:T(8,128)(2,1)}, bf16[768,768]{1,0:T(8,128)(2,1)}, bf16[768,768]{1,0:T(8,128)(2,1)}, bf16[768,768]{1,0:T(8,128)(2,1)}, bf16[1024,768]{1,0:T(8,128)(2,1)}) custom-call(s32[7]{0:T(128)} %stack.60.info, bf16[2,1024,768]{2,1,0:T(8,128)(2,1)} %hid_kept.3, bf16[1024,768]{1,0:T(8,128)(2,1)} %copy-done, f32[1,2304]{1,0:T(1,128)} %fusion.bias_ref, ...), custom_call_target="tpu_custom_call" | custom-call | tf_op jit(solution)/shard_map/queries/pallas_call | solution.py:424
  108.2 57.7 %attend.1 = (bf16[2048,768]{1,0:T(8,128)(2,1)}, bf16[6,2048,4096]{2,1,0:T(8,128)(2,1)}, f32[6,1,4096]{2,1,0:T(1,128)}) custom-call(s32[7]{0:T(128)} %stack.60.info, bf16[2048,2304]{1,0:T(8,128)(2,1)} %get-tuple-element.64.q_ref.k_ref.v_ref, bf16[2048,2304]{1,0:T(8,128)(2,1)} %get-tuple-element.64.q_ref.k_ref.v_ref, ...), custom_call_target="tpu_custom_call" | custom-call | tf_op jit(solution)/shard_map/attend/pallas_call | solution.py:139
  167.1 103.9 %middle.1 = (bf16[2,1024,768]{2,1,0:T(8,128)(2,1)}, bf16[1024,768]{1,0:T(8,128)(2,1)}, bf16[16,768]{1,0:T(8,128)(2,1)}, bf16[2048,768]{1,0:T(8,128)(2,1)}, f32[2...) custom-call(s32[7]{0:T(128)} %stack.60.info, bf16[2,1024,768]{2,1,0:T(8,128)(2,1)} %hid_kept.3, bf16[1024,768]{1,0:T(8,128)(2,1)} %copy-done, ...), custom_call_target="tpu_custom_call" | custom-call | tf_op jit(solution)/shard_map/middle/pallas_call | solution.py:634
  274.5 91.5 %attend_back.1 = (bf16[2048,768]{1,0:T(8,128)(2,1)}, bf16[2048,768]{1,0:T(8,128)(2,1)}, bf16[2048,768]{1,0:T(8,128)(2,1)}) custom-call(s32[7]{0:T(128)} %stack.60.info, s32[2,3]{1,0:T(2,128)} %constant.51.clone.units, bf16[2048,2304]{1,0:T(8,128)(2,1)} %get-tuple-element.64.q_ref.k_ref.v_ref, bf16[2048,2304]{1,0:T(8,128)(2,1)} %get-tuple-element.64.q_ref.k_ref.v_ref, ...), custom_call_target="tpu_custom_call" | custom-call | tf_op jit(solution)/shard_map/attend_back/pallas_call | solution.py:263
  367.8 10.6 %input_grad_other.1 = (bf16[1024,768]{1,0:T(8,128)(2,1)}, bf16[2,1024,768]{2,1,0:T(8,128)(2,1)}) custom-call(s32[7]{0:T(128)} %stack.60.info, bf16[2048,768]{1,0:T(8,128)(2,1)} %get-tuple-element.70.gq_ref.rest_0_, bf16[2048,768]{1,0:T(8,128)(2,1)} %get-tuple-element.71.gk_ref.rest_1_, ...), custom_call_target="tpu_custom_call", output_to_operand_aliasing={{1}: (9, {})} | custom-call | tf_op jit(solution)/shard_map/input_grad_other/pallas_call | solution.py:717
  379.8 34.5 %attend_back_last.1 = (bf16[2048,768]{1,0:T(8,128)(2,1)}, bf16[2048,768]{1,0:T(8,128)(2,1)}, bf16[2048,768]{1,0:T(8,128)(2,1)}) custom-call(s32[7]{0:T(128)} %stack.60.info, s32[2,1]{1,0:T(2,128)} %call_exported.0.units, bf16[2048,2304]{1,0:T(8,128)(2,1)} %get-tuple-element.64.q_ref.k_ref.v_ref, ...), custom_call_target="tpu_custom_call", output_to_operand_aliasing={{0}: (9, {}), {1}: (10, {}), {2}: (11, {})} | custom-call | tf_op jit(solution)/shard_map/attend_back_last/pallas_call | solution.py:263
  414.3 5.5 collective-permute-done.15.other_ref.rest_3_
  421.0 16.6 %head_grads.1 = (bf16[16,160,384]{2,1,0:T(8,128)(2,1)}, bf16[16,160,384]{2,1,0:T(8,128)(2,1)}) custom-call(s32[7]{0:T(128)} %stack.60.info, bf16[2,1024,768]{2,1,0:T(8,128)(2,1)} %hid_kept.3, bf16[1024,768]{1,0:T(8,128)(2,1)} %copy-done, bf16[2048,768]{1,0:T(8,128)(2,1)} %get-tuple-element.82.gq_ref.rest_0_, ...), custom_call_target="tpu_custom_call" | custom-call | tf_op jit(solution)/shard_map/head_grads/pallas_call | solution.py:779
  437.6 4.2 collective-permute-done.16.refs_1_
  443.1 3.5 add_blocks.2
  448.1 79.4 %collective-permute-start.18 = (bf16[4,160,384]{2,1,0:T(8,128)(2,1)}, bf16[4,160,384]{2,1,0:T(8,128)(2,1)S(1)}, u32[]{:S(2)}, u32[]{:S(2)}) collective-permute-start(bf16[4,160,384]{2,1,0:T(8,128)(2,1)} %get-tuple-element.89), channel_id=1, source_target_pairs={{0,4},{1,5},{2,6},{3,7},{4,0},{5,1},{6,2},{7,3},{8,12},{9,13},{10,... | collective-permute-start | bytes 1474568 | tf_op jit(solution)/shard_map/ppermute | solution.py:999
  527.5 9.3 %input_grad_kept.1.base_ref = f32[2,1024,768]{2,1,0:T(8,128)} custom-call(s32[7]{0:T(128)} %stack.60.info, bf16[2048,768]{1,0:T(8,128)(2,1)} %get-tuple-element.82.gq_ref.rest_0_, bf16[2048,768]{1,0:T(8,128)(2,1)} %get-tuple-element.83.gk_ref.rest_1_, bf16[2048,768]{1,0:T(8,128)(2,1)} %get-tuple-element.84.gv_ref.rest_2_, ...), custom_call_target="tpu_custom_call" | custom-call | tf_op jit(solution)/shard_map/input_grad_kept/pallas_call | solution.py:717
  536.8 3.6 place_other.1.refs_4_
  540.3 1.8 finish_sums.2
  542.2 7.2 %collective-permute-done.19.refs_3_ = bf16[4,160,384]{2,1,0:T(8,128)(2,1)S(1)} collective-permute-done((bf16[4,160,384]{2,1,0:T(8,128)(2,1)}, bf16[4,160,384]{2,1,0:T(8,128)(2,1)S(1)}, u32[]{:S(2)}, u32[]{:S(2)}) %collective-permute-start.19) | collective-permute-done | bytes 491552 | tf_op jit(solution)/shard_map/ppermute | solution.py:999
  550.2 2.4 add_blocks.3
  552.6 14.7 %collective-permute-start.21 = (bf16[1,160,384]{2,1,0:T(8,128)(2,1)}, bf16[1,160,384]{2,1,0:T(8,128)(2,1)S(1)}, u32[]{:S(2)}, u32[]{:S(2)}) collective-permute-start(bf16[1,160,384]{2,1,0:T(8,128)(2,1)} %get-tuple-element.96), channel_id=1, source_target_pairs={{0,16},{1,17},{2,18},{3,19},{4,20},{5,21},{6,22},{7,23},{8,24},{9,... | collective-permute-start | bytes 368648 | tf_op jit(solution)/shard_map/ppermute | solution.py:999
  568.5 8.1 %collective-permute-done.21 = bf16[1,160,384]{2,1,0:T(8,128)(2,1)S(1)} collective-permute-done((bf16[1,160,384]{2,1,0:T(8,128)(2,1)}, bf16[1,160,384]{2,1,0:T(8,128)(2,1)S(1)}, u32[]{:S(2)}, u32[]{:S(2)}) %collective-permute-start.21) | collective-permute-done | bytes 122912 | tf_op jit(solution)/shard_map/ppermute | solution.py:999
  (127 shorter events, 50.1 us)
Async XLA Ops:
  7.2 158.8 %all-gather.3.cloned.1.call-start = ((), (), s32[]{:S(2)}) async-start(), calls=%async_computation.2 | async-start | bytes 10948608 | tf_op jit(solution)/shard_map/all_gather | solution.py:1059
  9.0 531.3 %reduce-scatter.2.cloned.1.call-start = ((), (), s32[]{:S(2)}) async-start(), calls=%async_computation.1 | async-start | bytes 11354112 | tf_op jit(solution)/shard_map/reduce_scatter | solution.py:1092
  17.9 7.7 %collective-permute-start = (bf16[160,384]{1,0:T(8,128)(2,1)}, bf16[160,384]{1,0:T(8,128)(2,1)S(1)}, u32[]{:S(2)}, u32[]{:S(2)}) collective-permute-start(bf16[160,384]{1,0:T(8,128)(2,1)} %pack.2.refs_0_), channel_id=1, source_target_pairs={{0,1},{1,0},{2,3},{3,2},{4,5},{5,4},{6,7},{7,6},{8,9},{9,8},{10,11... | collective-permute-start | bytes 368648 | tf_op jit(solution)/shard_map/ppermute | solution.py:999
  29.2 49.5 %collective-permute-start.1 = (bf16[1024,768]{1,0:T(8,128)(2,1)}, bf16[1024,768]{1,0:T(8,128)(2,1)S(1)}, u32[]{:S(2)}, u32[]{:S(2)}) collective-permute-start(bf16[1024,768]{1,0:T(8,128)(2,1)} %pick_other.1.refs_2_), channel_id=1, source_target_pairs={{0,1},{1,0},{2,3},{3,2},{4,5},{5,4},{6,7},{7,6},{8,9},{9,8},{10,11... | collective-permute-start | bytes 4718600 | tf_op jit(solution)/shard_map/ppermute | solution.py:933
  33.3 11.2 %collective-permute-start.4 = (bf16[2,96,384]{2,1,0:T(8,128)(2,1)}, bf16[2,96,384]{2,1,0:T(8,128)(2,1)S(1)}, u32[]{:S(2)}, u32[]{:S(2)}) collective-permute-start(bf16[2,96,384]{2,1,0:T(8,128)(2,1)} %get-tuple-element.62.refs_0_), channel_id=1, source_target_pairs={{0,24},{1,25},{2,26},{3,27},{4,28},{5,29},{6,30},{7,31},{8,16},{9,... | collective-permute-start | bytes 442376 | tf_op jit(solution)/shard_map/ppermute | solution.py:999
  36.9 11.2 %collective-permute-start.3 = (bf16[2,96,384]{2,1,0:T(8,128)(2,1)}, bf16[2,96,384]{2,1,0:T(8,128)(2,1)S(1)}, u32[]{:S(2)}, u32[]{:S(2)}) collective-permute-start(bf16[2,96,384]{2,1,0:T(8,128)(2,1)} %get-tuple-element.62.refs_0_), channel_id=1, source_target_pairs={{0,16},{1,17},{2,18},{3,19},{4,20},{5,21},{6,22},{7,23},{8,24},{9,... | collective-permute-start | bytes 442376 | tf_op jit(solution)/shard_map/ppermute | solution.py:999
  36.9 11.2 %collective-permute-start.2 = (bf16[2,96,384]{2,1,0:T(8,128)(2,1)}, bf16[2,96,384]{2,1,0:T(8,128)(2,1)S(1)}, u32[]{:S(2)}, u32[]{:S(2)}) collective-permute-start(bf16[2,96,384]{2,1,0:T(8,128)(2,1)} %get-tuple-element.62.refs_0_), channel_id=1, source_target_pairs={{0,8},{1,9},{2,10},{3,11},{4,12},{5,13},{6,14},{7,15},{8,0},{9,1},... | collective-permute-start | bytes 442376 | tf_op jit(solution)/shard_map/ppermute | solution.py:999
  37.7 4.6 collective-permute-start.5
  51.4 31.7 %copy-start.24 = (bf16[2,16,384]{2,1,0:T(8,128)(2,1)S(1)}, bf16[2,16,384]{2,1,0:T(8,128)(2,1)}, u32[]{:S(2)}) copy-start(bf16[2,16,384]{2,1,0:T(8,128)(2,1)} %get-tuple-element.61) | copy-start | bytes 73732
  51.4 27.3 %collective-permute-start.6 = (bf16[8,96,384]{2,1,0:T(8,128)(2,1)}, bf16[8,96,384]{2,1,0:T(8,128)(2,1)S(1)}, u32[]{:S(2)}, u32[]{:S(2)}) collective-permute-start(bf16[8,96,384]{2,1,0:T(8,128)(2,1)} %join_blocks.5.refs_0_), channel_id=1, source_target_pairs={{0,4},{1,5},{2,6},{3,7},{4,0},{5,1},{6,2},{7,3},{8,12},{9,13},{10,... | collective-permute-start | bytes 1769480 | tf_op jit(solution)/shard_map/ppermute | solution.py:999
  52.9 12.4 %collective-permute-start.9 = (bf16[4,48,384]{2,1,0:T(8,128)(2,1)}, bf16[4,48,384]{2,1,0:T(8,128)(2,1)S(1)}, u32[]{:S(2)}, u32[]{:S(2)}) collective-permute-start(bf16[4,48,384]{2,1,0:T(8,128)(2,1)} %join_blocks.4.refs_4_.refs_0_), channel_id=1, source_target_pairs={{0,24},{1,25},{2,26},{3,27},{4,28},{5,29},{6,30},{7,31},{8,16},{9,... | collective-permute-start | bytes 442376 | tf_op jit(solution)/shard_map/ppermute | solution.py:999
  58.0 17.4 %collective-permute-start.8 = (bf16[4,48,384]{2,1,0:T(8,128)(2,1)}, bf16[4,48,384]{2,1,0:T(8,128)(2,1)S(1)}, u32[]{:S(2)}, u32[]{:S(2)}) collective-permute-start(bf16[4,48,384]{2,1,0:T(8,128)(2,1)} %join_blocks.4.refs_4_.refs_0_), channel_id=1, source_target_pairs={{0,16},{1,17},{2,18},{3,19},{4,20},{5,21},{6,22},{7,23},{8,24},{9,... | collective-permute-start | bytes 442376 | tf_op jit(solution)/shard_map/ppermute | solution.py:999
  58.0 17.4 %collective-permute-start.7 = (bf16[4,48,384]{2,1,0:T(8,128)(2,1)}, bf16[4,48,384]{2,1,0:T(8,128)(2,1)S(1)}, u32[]{:S(2)}, u32[]{:S(2)}) collective-permute-start(bf16[4,48,384]{2,1,0:T(8,128)(2,1)} %join_blocks.4.refs_4_.refs_0_), channel_id=1, source_target_pairs={{0,8},{1,9},{2,10},{3,11},{4,12},{5,13},{6,14},{7,15},{8,0},{9,1},... | collective-permute-start | bytes 442376 | tf_op jit(solution)/shard_map/ppermute | solution.py:999
  65.3 10.1 %copy-start.13 = (bf16[4,48,384]{2,1,0:T(8,128)(2,1)}, bf16[4,48,384]{2,1,0:T(8,128)(2,1)S(1)}, u32[]{:S(2)}) copy-start(bf16[4,48,384]{2,1,0:T(8,128)(2,1)S(1)} %collective-permute-done.9.refs_3_) | copy-start | bytes 442372
  83.1 3.9 collective-permute-start.10
  83.2 3.8 collective-permute-start.11
  84.4 22.0 %copy-start.26 = (bf16[2,768]{1,0:T(2,128)(2,1)S(1)}, bf16[2,768]{1,0:T(2,128)(2,1)}, u32[]{:S(2)}) copy-start(bf16[2,768]{1,0:T(2,128)(2,1)} %param.24) | copy-start | bytes 9220
  105.3 60.6 %collective-permute-start.12 = (bf16[1024,768]{1,0:T(8,128)(2,1)}, bf16[1024,768]{1,0:T(8,128)(2,1)S(1)}, u32[]{:S(2)}, u32[]{:S(2)}) collective-permute-start(bf16[1024,768]{1,0:T(8,128)(2,1)} %get-tuple-element.65), channel_id=1, source_target_pairs={{0,1},{1,0},{2,3},{3,2},{4,5},{5,4},{6,7},{7,6},{8,9},{9,8},{10,11... | collective-permute-start | bytes 4718600 | tf_op jit(solution)/shard_map/ppermute | solution.py:933
  272.4 94.2 %collective-permute-start.13 = (bf16[1024,768]{1,0:T(8,128)(2,1)S(1)}, bf16[1024,768]{1,0:T(8,128)(2,1)S(1)}, u32[]{:S(2)}, u32[]{:S(2)}) collective-permute-start(bf16[1024,768]{1,0:T(8,128)(2,1)S(1)} %copy-done.27), channel_id=1, source_target_pairs={{1,0},{0,1},{3,2},{2,3},{5,4},{4,5},{7,6},{6,7},{9,8},{8,9},{11,10... | collective-permute-start | bytes 4718600 | tf_op jit(solution)/shard_map/ppermute | solution.py:933
  273.3 92.8 %collective-permute-start.14 = (bf16[16,768]{1,0:T(8,128)(2,1)S(1)}, bf16[16,768]{1,0:T(8,128)(2,1)S(1)}, u32[]{:S(2)}, u32[]{:S(2)}) collective-permute-start(bf16[16,768]{1,0:T(8,128)(2,1)S(1)} %copy-done.25), channel_id=1, source_target_pairs={{0,1},{1,0},{2,3},{3,2},{4,5},{5,4},{6,7},{7,6},{8,9},{9,8},{10,11... | collective-permute-start | bytes 73736 | tf_op jit(solution)/shard_map/ppermute | solution.py:963
  378.4 41.4 %collective-permute-start.15 = (bf16[1024,768]{1,0:T(8,128)(2,1)}, bf16[1024,768]{1,0:T(8,128)(2,1)S(1)}, u32[]{:S(2)}, u32[]{:S(2)}) collective-permute-start(bf16[1024,768]{1,0:T(8,128)(2,1)} %get-tuple-element.81.rest_3_), channel_id=1, source_target_pairs={{1,0},{0,1},{3,2},{2,3},{5,4},{4,5},{7,6},{6,7},{9,8},{8,9},{11,10... | collective-permute-start | bytes 4718600 | tf_op jit(solution)/shard_map/ppermute | solution.py:933
  437.6 4.2 collective-permute-start.16
  446.6 95.5 %collective-permute-start.17 = (bf16[4,160,384]{2,1,0:T(8,128)(2,1)}, bf16[4,160,384]{2,1,0:T(8,128)(2,1)S(1)}, u32[]{:S(2)}, u32[]{:S(2)}) collective-permute-start(bf16[4,160,384]{2,1,0:T(8,128)(2,1)} %get-tuple-element.88), channel_id=1, source_target_pairs={{0,1},{1,0},{2,3},{3,2},{4,5},{5,4},{6,7},{7,6},{8,9},{9,8},{10,11... | collective-permute-start | bytes 1474568 | tf_op jit(solution)/shard_map/ppermute | solution.py:999
  448.1 94.1 %collective-permute-start.18 = (bf16[4,160,384]{2,1,0:T(8,128)(2,1)}, bf16[4,160,384]{2,1,0:T(8,128)(2,1)S(1)}, u32[]{:S(2)}, u32[]{:S(2)}) collective-permute-start(bf16[4,160,384]{2,1,0:T(8,128)(2,1)} %get-tuple-element.89), channel_id=1, source_target_pairs={{0,4},{1,5},{2,6},{3,7},{4,0},{5,1},{6,2},{7,3},{8,12},{9,13},{10,... | collective-permute-start | bytes 1474568 | tf_op jit(solution)/shard_map/ppermute | solution.py:999
  527.5 21.9 %collective-permute-start.19 = (bf16[4,160,384]{2,1,0:T(8,128)(2,1)}, bf16[4,160,384]{2,1,0:T(8,128)(2,1)S(1)}, u32[]{:S(2)}, u32[]{:S(2)}) collective-permute-start(bf16[4,160,384]{2,1,0:T(8,128)(2,1)} %get-tuple-element.90), channel_id=1, source_target_pairs={{0,5},{1,4},{2,7},{3,6},{4,1},{5,0},{6,3},{7,2},{8,13},{9,12},{10,... | collective-permute-start | bytes 1474568 | tf_op jit(solution)/shard_map/ppermute | solution.py:999
  542.2 7.2 %copy-start.9 = (bf16[4,160,384]{2,1,0:T(8,128)(2,1)}, bf16[4,160,384]{2,1,0:T(8,128)(2,1)S(1)}, u32[]{:S(2)}) copy-start(bf16[4,160,384]{2,1,0:T(8,128)(2,1)S(1)} %collective-permute-done.17.refs_1_) | copy-start | bytes 1474564
  542.2 7.2 %copy-start.10 = (bf16[4,160,384]{2,1,0:T(8,128)(2,1)}, bf16[4,160,384]{2,1,0:T(8,128)(2,1)S(1)}, u32[]{:S(2)}) copy-start(bf16[4,160,384]{2,1,0:T(8,128)(2,1)S(1)} %collective-permute-done.18.refs_2_) | copy-start | bytes 1474564
  550.2 17.1 %copy-start.23 = (f32[16,384]{1,0:T(8,128)S(1)}, f32[16,384]{1,0:T(8,128)}, u32[]{:S(2)}) copy-start(f32[16,384]{1,0:T(8,128)} %get-tuple-element.93.refs_6_) | copy-start | bytes 73732
  552.5 16.0 %collective-permute-start.20 = (bf16[1,160,384]{2,1,0:T(8,128)(2,1)}, bf16[1,160,384]{2,1,0:T(8,128)(2,1)S(1)}, u32[]{:S(2)}, u32[]{:S(2)}) collective-permute-start(bf16[1,160,384]{2,1,0:T(8,128)(2,1)} %get-tuple-element.95), channel_id=1, source_target_pairs={{0,8},{1,9},{2,10},{3,11},{4,12},{5,13},{6,14},{7,15},{8,0},{9,1},... | collective-permute-start | bytes 368648 | tf_op jit(solution)/shard_map/ppermute | solution.py:999
  552.6 24.0 %collective-permute-start.21 = (bf16[1,160,384]{2,1,0:T(8,128)(2,1)}, bf16[1,160,384]{2,1,0:T(8,128)(2,1)S(1)}, u32[]{:S(2)}, u32[]{:S(2)}) collective-permute-start(bf16[1,160,384]{2,1,0:T(8,128)(2,1)} %get-tuple-element.96), channel_id=1, source_target_pairs={{0,16},{1,17},{2,18},{3,19},{4,20},{5,21},{6,22},{7,23},{8,24},{9,... | collective-permute-start | bytes 368648 | tf_op jit(solution)/shard_map/ppermute | solution.py:999
  567.3 9.3 %collective-permute-start.22 = (bf16[1,160,384]{2,1,0:T(8,128)(2,1)}, bf16[1,160,384]{2,1,0:T(8,128)(2,1)S(1)}, u32[]{:S(2)}, u32[]{:S(2)}) collective-permute-start(bf16[1,160,384]{2,1,0:T(8,128)(2,1)} %get-tuple-element.97), channel_id=1, source_target_pairs={{0,24},{1,25},{2,26},{3,27},{4,28},{5,29},{6,30},{7,31},{8,16},{9,... | collective-permute-start | bytes 368648 | tf_op jit(solution)/shard_map/ppermute | solution.py:999
  568.5 8.1 %copy-start.19 = (bf16[1,160,384]{2,1,0:T(8,128)(2,1)}, bf16[1,160,384]{2,1,0:T(8,128)(2,1)S(1)}, u32[]{:S(2)}) copy-start(bf16[1,160,384]{2,1,0:T(8,128)(2,1)S(1)} %collective-permute-done.20) | copy-start | bytes 368644
  (21 other events, 26.4 us)
Sparse Core Ops, SparseCore 0:
  10.9 103.6 all-gather.2
  271.2 238.8 reduce-scatter.1

commit v6 on v5

--- a/solution.py
+++ b/solution.py
@@ -1022,7 +1022,7 @@
 
 
 class Weights:
-    def __init__(self, shards, vectors=None, begin=None):
+    def __init__(self, shards, begin=None):
         self.shapes = [s.shape for s in shards]
         self.m, self.n = lax.axis_size("batch"), lax.axis_size("blk")
         m, n = self.m, self.n
@@ -1034,12 +1034,12 @@
         if self.by_pairs:
             y, core, x = list(range(1, n)), [n], [2 * n]
             z = list(range(4 * n, m * n, 4 * n))
-            near = pack_after([*shards, vectors], ())
+            near = pack_after(shards, ())
             near = [near] + [exchanged(near, mask) for mask in y]
             cut = sum(s.size for s in shards[:-1]) // c
-            cuts = [cut, shards[-1].size // c, vectors.shape[0]]
+            cuts = [cut, shards[-1].size // c]
             picked, arrival = begin(near[1:])
-            most, least, self.vectors = stack_rows(near, cuts, (picked,))
+            most, least = stack_rows(near, cuts, (picked,))
             flat = lambda part: part.reshape(-1, *part.shape[-2:])
             first = [0] + y
             b, b_masks = xor_gather(flat(least), first, x, ())
@@ -1181,13 +1181,12 @@
         hidden = plan.gather(hidden_in, picked)
         return picked, hidden[1]
 
-    heads = Weights([w_query, w_key, w_value], vec_shard, begin if plan.stays else None)
+    heads = Weights([w_query, w_key, w_value], begin if plan.stays else None)
     if hidden is None:
         hidden = plan.gather(hidden_in, plan.pick(hidden_in))
     if heads.by_pairs:
-        vec_all = jnp.where(plan.me == 0, heads.vectors, heads.vectors[::-1])
-    else:
-        vec_all = plan.all_blocks(vec_shard)
+        vec_shard = pack_after([vec_shard], hidden[1:])
+    vec_all = plan.all_blocks(vec_shard)
     dense = Weights([w_out, w_inner, w_outer])
     narrow = vec_all[:, :8].transpose(1, 0, 2).reshape(8, width).astype(F32)
     bias_inner = vec_all[:, 8:used].reshape(1, -1).astype(F32)

time: 593 us -> 597 us (level)
  Pallas kernels: 370 us -> 413 us
  starting transfers between devices: 118 us -> 81.6 us
  local copies, waits for them, and re-layouts: 30.2 us -> 24.2 us
    ppermute x18, starting transfers between devices: 112 us -> 51.7 us  [exchanged(): return lax.ppermute(block, both, [(i, i ^ mask) for i in places])]
    pallas_call x1, Pallas kernels: 57.7 us -> 100 us  [attend(): pl.pallas_call(functools.partial(attend_kernel, chunk=min(256, kv), acros...]
    ppermute x4, starting transfers between devices: 5.11 us -> 27.4 us  [swap(): return lax.ppermute(block, axis, route)]
    reduce_scatter x1, waiting for transfers between devices: 0.01 us -> 7.1 us  [scatter(): lax.psum_scatter(sums.reshape(-1, c), ('batch', 'blk'), scatter_dimension...]
    unnamed x57 -> x73, local copies, waits for them, and re-layouts: 15.9 us -> 16 us
  transfers between devices with their start and end apart: 25 -> 26, of which waited for: 10 -> 11; matrix products, arithmetic and copies ran while one was open for 3% -> 2% of each run, Pallas kernels for 44% -> 51%
where the time goes in v6:
time: 597 us; the launch traced here: 592 us
  Pallas kernels  413 us (69%)
  starting transfers between devices  81.6 us (14%)
  waiting for transfers between devices  56.1 us (9%)
  local copies, waits for them, and re-layouts  24.2 us (4%)
  between operations  14.6 us (2%)
    pallas_call x2, Pallas kernels, attend_back(): pl.pallas_call(functools.partial(attend_back_kernel, chunk=min(512, part)...  126 us
    pallas_call x1, Pallas kernels, middle(): pl.pallas_call(functools.partial(middle_kernel, split=split, grid_of=grid...  104 us
    pallas_call x1, Pallas kernels, attend(): pl.pallas_call(functools.partial(attend_kernel, chunk=min(256, kv), acros...  100 us
    ppermute x18, starting transfers between devices, exchanged(): return lax.ppermute(block, both, [(i, i ^ mask) for i in places])  51.7 us
    ppermute x18, waiting for transfers between devices, exchanged(): return lax.ppermute(block, both, [(i, i ^ mask) for i in places])  47 us
    ppermute x4, starting transfers between devices, swap(): return lax.ppermute(block, axis, route)  27.4 us
    pallas_call x2, Pallas kernels, input_grad(): pl.pallas_call(functools.partial(input_grad_kernel, kept=kept, join=bool(...  19.8 us
    pallas_call x1, Pallas kernels, head_grads(): pl.pallas_call(functools.partial(head_grads_kernel, split=split, grid_of=...  16.6 us
  transfers between devices with their start and end apart: 26, of which 11 were waited for; matrix products, arithmetic and copies ran while one was open for 2% of the time, Pallas kernels for 51%

profile of v6, /device:TPU:0, one launch (start us, length us, event | category | flops | bytes accessed | tf_op | source)
XLA Modules:
  0.0 591.6 jit_solution(13361639653232915585)
XLA Ops:
  10.5 3.0 collective-permute-start
  17.4 3.0 pick_other.1.refs_2_
  23.8 3.6 collective-permute-start.5
  29.7 3.1 collective-permute-done.6.refs_1_
  35.5 10.4 %collective-permute-done.4.refs_2_ = bf16[2,96,384]{2,1,0:T(8,128)(2,1)S(1)} collective-permute-done((bf16[2,96,384]{2,1,0:T(8,128)(2,1)}, bf16[2,96,384]{2,1,0:T(8,128)(2,1)S(1)}, u32[]{:S(2)}, u32[]{:S(2)}) %collective-permute-start.4) | collective-permute-done | bytes 147488 | tf_op jit(solution)/shard_map/ppermute | solution.py:999
  52.2 3.1 collective-permute-start.8
  55.2 7.5 %collective-permute-done.10.refs_3_ = bf16[4,48,384]{2,1,0:T(8,128)(2,1)S(1)} collective-permute-done((bf16[4,48,384]{2,1,0:T(8,128)(2,1)}, bf16[4,48,384]{2,1,0:T(8,128)(2,1)S(1)}, u32[]{:S(2)}, u32[]{:S(2)}) %collective-permute-start.10) | collective-permute-done | bytes 147488 | tf_op jit(solution)/shard_map/ppermute | solution.py:999
  62.7 10.5 %collective-permute-done.9.refs_2_ = bf16[4,48,384]{2,1,0:T(8,128)(2,1)S(1)} collective-permute-done((bf16[4,48,384]{2,1,0:T(8,128)(2,1)}, bf16[4,48,384]{2,1,0:T(8,128)(2,1)S(1)}, u32[]{:S(2)}, u32[]{:S(2)}) %collective-permute-start.9) | collective-permute-done | bytes 147488 | tf_op jit(solution)/shard_map/ppermute | solution.py:999
  74.5 2.0 join_blocks.6.refs_3_.rest_2_
  78.5 2.4 join_blocks.7.rest_0_
  83.7 2.4 collective-permute-start.2
  91.5 16.4 %queries.1 = (bf16[2048,2304]{1,0:T(8,128)(2,1)}, bf16[768,768]{1,0:T(8,128)(2,1)}, bf16[768,768]{1,0:T(8,128)(2,1)}, bf16[768,768]{1,0:T(8,128)(2,1)}, bf16[1024,768]{1,0:T(8,128)(2,1)}) custom-call(s32[7]{0:T(128)} %stack.74.info, bf16[2,1024,768]{2,1,0:T(8,128)(2,1)} %hid_kept.3, bf16[1024,768]{1,0:T(8,128)(2,1)} %copy-done, f32[1,2304]{1,0:T(1,128)} %fusion.bias_ref, ...), custom_call_target="tpu_custom_call" | custom-call | tf_op jit(solution)/shard_map/queries/pallas_call | solution.py:424
  108.0 2.0 collective-permute-start.13
  111.8 100.2 %attend.1 = (bf16[2048,768]{1,0:T(8,128)(2,1)}, bf16[6,2048,4096]{2,1,0:T(8,128)(2,1)}, f32[6,1,4096]{2,1,0:T(1,128)}) custom-call(s32[7]{0:T(128)} %stack.74.info, bf16[2048,2304]{1,0:T(8,128)(2,1)} %get-tuple-element.62.q_ref.k_ref.v_ref, bf16[2048,2304]{1,0:T(8,128)(2,1)} %get-tuple-element.62.q_ref.k_ref.v_ref, ...), custom_call_target="tpu_custom_call" | custom-call | tf_op jit(solution)/shard_map/attend/pallas_call | solution.py:139
  213.3 103.9 %middle.1 = (bf16[2,1024,768]{2,1,0:T(8,128)(2,1)}, bf16[1024,768]{1,0:T(8,128)(2,1)}, bf16[16,768]{1,0:T(8,128)(2,1)}, bf16[2048,768]{1,0:T(8,128)(2,1)}, f32[2...) custom-call(s32[7]{0:T(128)} %stack.74.info, bf16[2,1024,768]{2,1,0:T(8,128)(2,1)} %hid_kept.3, bf16[1024,768]{1,0:T(8,128)(2,1)} %copy-done, ...), custom_call_target="tpu_custom_call" | custom-call | tf_op jit(solution)/shard_map/middle/pallas_call | solution.py:634
  318.6 21.6 %collective-permute-start.14 = (bf16[1024,768]{1,0:T(8,128)(2,1)S(1)}, bf16[1024,768]{1,0:T(8,128)(2,1)S(1)}, u32[]{:S(2)}, u32[]{:S(2)}) collective-permute-start(bf16[1024,768]{1,0:T(8,128)(2,1)S(1)} %copy-done.35), channel_id=1, source_target_pairs={{1,0},{0,1},{3,2},{2,3},{5,4},{4,5},{7,6},{6,7},{9,8},{8,9},{11,10... | collective-permute-start | bytes 4718600 | tf_op jit(solution)/shard_map/ppermute | solution.py:933
  340.2 91.6 %attend_back.1 = (bf16[2048,768]{1,0:T(8,128)(2,1)}, bf16[2048,768]{1,0:T(8,128)(2,1)}, bf16[2048,768]{1,0:T(8,128)(2,1)}) custom-call(s32[7]{0:T(128)} %stack.74.info, s32[2,3]{1,0:T(2,128)} %constant.51.clone.units, bf16[2048,2304]{1,0:T(8,128)(2,1)} %get-tuple-element.62.q_ref.k_ref.v_ref, bf16[2048,2304]{1,0:T(8,128)(2,1)} %get-tuple-element.62.q_ref.k_ref.v_ref, ...), custom_call_target="tpu_custom_call" | custom-call | tf_op jit(solution)/shard_map/attend_back/pallas_call | solution.py:263
  433.5 10.2 %input_grad_other.1 = (bf16[1024,768]{1,0:T(8,128)(2,1)}, bf16[2,1024,768]{2,1,0:T(8,128)(2,1)}) custom-call(s32[7]{0:T(128)} %stack.74.info, bf16[2048,768]{1,0:T(8,128)(2,1)} %get-tuple-element.68.gq_ref.rest_0_, bf16[2048,768]{1,0:T(8,128)(2,1)} %get-tuple-element.69.gk_ref.rest_1_, ...), custom_call_target="tpu_custom_call", output_to_operand_aliasing={{1}: (9, {})} | custom-call | tf_op jit(solution)/shard_map/input_grad_other/pallas_call | solution.py:717
  443.7 2.0 collective-permute-start.16
  446.3 34.4 %attend_back_last.1 = (bf16[2048,768]{1,0:T(8,128)(2,1)}, bf16[2048,768]{1,0:T(8,128)(2,1)}, bf16[2048,768]{1,0:T(8,128)(2,1)}) custom-call(s32[7]{0:T(128)} %stack.74.info, s32[2,1]{1,0:T(2,128)} %call_exported.0.units, bf16[2048,2304]{1,0:T(8,128)(2,1)} %get-tuple-element.62.q_ref.k_ref.v_ref, ...), custom_call_target="tpu_custom_call", output_to_operand_aliasing={{0}: (9, {}), {1}: (10, {}), {2}: (11, {})} | custom-call | tf_op jit(solution)/shard_map/attend_back_last/pallas_call | solution.py:263
  481.9 16.6 %head_grads.1 = (bf16[16,160,384]{2,1,0:T(8,128)(2,1)}, bf16[16,160,384]{2,1,0:T(8,128)(2,1)}) custom-call(s32[7]{0:T(128)} %stack.74.info, bf16[2,1024,768]{2,1,0:T(8,128)(2,1)} %hid_kept.3, bf16[1024,768]{1,0:T(8,128)(2,1)} %copy-done, bf16[2048,768]{1,0:T(8,128)(2,1)} %get-tuple-element.80.gq_ref.rest_0_, ...), custom_call_target="tpu_custom_call" | custom-call | tf_op jit(solution)/shard_map/head_grads/pallas_call | solution.py:779
  498.5 4.2 collective-permute-done.17.refs_1_
  504.0 3.5 add_blocks.2
  507.5 3.5 collective-permute-start.20
  511.0 9.5 %input_grad_kept.1.base_ref = f32[2,1024,768]{2,1,0:T(8,128)} custom-call(s32[7]{0:T(128)} %stack.74.info, bf16[2048,768]{1,0:T(8,128)(2,1)} %get-tuple-element.80.gq_ref.rest_0_, bf16[2048,768]{1,0:T(8,128)(2,1)} %get-tuple-element.81.gk_ref.rest_1_, bf16[2048,768]{1,0:T(8,128)(2,1)} %get-tuple-element.82.gv_ref.rest_2_, ...), custom_call_target="tpu_custom_call" | custom-call | tf_op jit(solution)/shard_map/input_grad_kept/pallas_call | solution.py:717
  520.5 3.6 place_other.1.refs_4_
  524.1 7.1 %reduce-scatter.2.cloned.1.call-done.refs_0_ = bf16[448,384]{1,0:T(8,128)(2,1)} async-done(((bf16[14336,384]{1,0:T(8,128)(2,1)}), bf16[448,384]{1,0:T(8,128)(2,1)}) %reduce-scatter.2.cloned.1.call-update) | async-done | bytes 344080 | tf_op jit(solution)/shard_map/reduce_scatter | solution.py:1092
  533.1 2.1 collective-permute-done.20.refs_3_
  536.0 2.4 add_blocks.3
  538.4 21.1 %collective-permute-start.21 = (bf16[1,160,384]{2,1,0:T(8,128)(2,1)}, bf16[1,160,384]{2,1,0:T(8,128)(2,1)S(1)}, u32[]{:S(2)}, u32[]{:S(2)}) collective-permute-start(bf16[1,160,384]{2,1,0:T(8,128)(2,1)} %get-tuple-element.93), channel_id=1, source_target_pairs={{0,8},{1,9},{2,10},{3,11},{4,12},{5,13},{6,14},{7,15},{8,0},{9,1},... | collective-permute-start | bytes 368648 | tf_op jit(solution)/shard_map/ppermute | solution.py:999
  559.5 11.9 %collective-permute-start.22 = (bf16[1,160,384]{2,1,0:T(8,128)(2,1)}, bf16[1,160,384]{2,1,0:T(8,128)(2,1)S(1)}, u32[]{:S(2)}, u32[]{:S(2)}) collective-permute-start(bf16[1,160,384]{2,1,0:T(8,128)(2,1)} %get-tuple-element.94), channel_id=1, source_target_pairs={{0,16},{1,17},{2,18},{3,19},{4,20},{5,21},{6,22},{7,23},{8,24},{9,... | collective-permute-start | bytes 368648 | tf_op jit(solution)/shard_map/ppermute | solution.py:999
  572.6 8.1 %collective-permute-done.22 = bf16[1,160,384]{2,1,0:T(8,128)(2,1)S(1)} collective-permute-done((bf16[1,160,384]{2,1,0:T(8,128)(2,1)}, bf16[1,160,384]{2,1,0:T(8,128)(2,1)S(1)}, u32[]{:S(2)}, u32[]{:S(2)}) %collective-permute-start.22) | collective-permute-done | bytes 122912 | tf_op jit(solution)/shard_map/ppermute | solution.py:999
  (146 shorter events, 50.2 us)
Async XLA Ops:
  7.2 204.9 %all-gather.3.cloned.1.call-start = ((), (), s32[]{:S(2)}) async-start(), calls=%async_computation.2 | async-start | bytes 10948608 | tf_op jit(solution)/shard_map/all_gather | solution.py:1059
  9.0 522.2 %reduce-scatter.2.cloned.1.call-start = ((), (), s32[]{:S(2)}) async-start(), calls=%async_computation.1 | async-start | bytes 11354112 | tf_op jit(solution)/shard_map/reduce_scatter | solution.py:1092
  10.5 6.2 %collective-permute-start = (bf16[144,384]{1,0:T(8,128)(2,1)}, bf16[144,384]{1,0:T(8,128)(2,1)S(1)}, u32[]{:S(2)}, u32[]{:S(2)}) collective-permute-start(bf16[144,384]{1,0:T(8,128)(2,1)} %pack.3.refs_0_), channel_id=1, source_target_pairs={{0,1},{1,0},{2,3},{3,2},{4,5},{5,4},{6,7},{7,6},{8,9},{9,8},{10,11... | collective-permute-start | bytes 331784 | tf_op jit(solution)/shard_map/ppermute | solution.py:999
  20.4 56.1 %collective-permute-start.1 = (bf16[1024,768]{1,0:T(8,128)(2,1)}, bf16[1024,768]{1,0:T(8,128)(2,1)S(1)}, u32[]{:S(2)}, u32[]{:S(2)}) collective-permute-start(bf16[1024,768]{1,0:T(8,128)(2,1)} %pick_other.1.refs_2_), channel_id=1, source_target_pairs={{0,1},{1,0},{2,3},{3,2},{4,5},{5,4},{6,7},{7,6},{8,9},{9,8},{10,11... | collective-permute-start | bytes 4718600 | tf_op jit(solution)/shard_map/ppermute | solution.py:933
  23.8 11.7 %collective-permute-start.5 = (bf16[2,96,384]{2,1,0:T(8,128)(2,1)}, bf16[2,96,384]{2,1,0:T(8,128)(2,1)S(1)}, u32[]{:S(2)}, u32[]{:S(2)}) collective-permute-start(bf16[2,96,384]{2,1,0:T(8,128)(2,1)} %get-tuple-element.60.refs_0_), channel_id=1, source_target_pairs={{0,24},{1,25},{2,26},{3,27},{4,28},{5,29},{6,30},{7,31},{8,16},{9,... | collective-permute-start | bytes 442376 | tf_op jit(solution)/shard_map/ppermute | solution.py:999
  27.4 18.5 %collective-permute-start.4 = (bf16[2,96,384]{2,1,0:T(8,128)(2,1)}, bf16[2,96,384]{2,1,0:T(8,128)(2,1)S(1)}, u32[]{:S(2)}, u32[]{:S(2)}) collective-permute-start(bf16[2,96,384]{2,1,0:T(8,128)(2,1)} %get-tuple-element.60.refs_0_), channel_id=1, source_target_pairs={{0,16},{1,17},{2,18},{3,19},{4,20},{5,21},{6,22},{7,23},{8,24},{9,... | collective-permute-start | bytes 442376 | tf_op jit(solution)/shard_map/ppermute | solution.py:999
  27.4 18.5 %collective-permute-start.3 = (bf16[2,96,384]{2,1,0:T(8,128)(2,1)}, bf16[2,96,384]{2,1,0:T(8,128)(2,1)S(1)}, u32[]{:S(2)}, u32[]{:S(2)}) collective-permute-start(bf16[2,96,384]{2,1,0:T(8,128)(2,1)} %get-tuple-element.60.refs_0_), channel_id=1, source_target_pairs={{0,8},{1,9},{2,10},{3,11},{4,12},{5,13},{6,14},{7,15},{8,0},{9,1},... | collective-permute-start | bytes 442376 | tf_op jit(solution)/shard_map/ppermute | solution.py:999
  28.2 4.6 collective-permute-start.6
  49.2 31.8 %copy-start.31 = (bf16[384]{0:T(512)(128)(2,1)S(1)}, bf16[384]{0:T(512)(128)(2,1)}, u32[]{:S(2)}) copy-start(bf16[384]{0:T(512)(128)(2,1)} %param.35) | copy-start | bytes 2308
  49.2 31.8 %copy-start.32 = (bf16[384]{0:T(512)(128)(2,1)S(1)}, bf16[384]{0:T(512)(128)(2,1)}, u32[]{:S(2)}) copy-start(bf16[384]{0:T(512)(128)(2,1)} %param.37) | copy-start | bytes 2308
  49.3 31.8 %copy-start.33 = (bf16[384]{0:T(512)(128)(2,1)S(1)}, bf16[384]{0:T(512)(128)(2,1)}, u32[]{:S(2)}) copy-start(bf16[384]{0:T(512)(128)(2,1)} %param.38) | copy-start | bytes 2308
  49.3 31.8 %copy-start.34 = (bf16[384]{0:T(512)(128)(2,1)S(1)}, bf16[384]{0:T(512)(128)(2,1)}, u32[]{:S(2)}) copy-start(bf16[384]{0:T(512)(128)(2,1)} %param.39) | copy-start | bytes 2308
  49.3 31.8 %copy-start.25 = (bf16[1536]{0:T(1024)(128)(2,1)S(1)}, bf16[1536]{0:T(1024)(128)(2,1)}, u32[]{:S(2)}) copy-start(bf16[1536]{0:T(1024)(128)(2,1)} %param.36) | copy-start | bytes 9220
  49.3 27.2 %collective-permute-start.7 = (bf16[8,96,384]{2,1,0:T(8,128)(2,1)}, bf16[8,96,384]{2,1,0:T(8,128)(2,1)S(1)}, u32[]{:S(2)}, u32[]{:S(2)}) collective-permute-start(bf16[8,96,384]{2,1,0:T(8,128)(2,1)} %join_blocks.5.refs_0_), channel_id=1, source_target_pairs={{0,4},{1,5},{2,6},{3,7},{4,0},{5,1},{6,2},{7,3},{8,12},{9,13},{10,... | collective-permute-start | bytes 1769480 | tf_op jit(solution)/shard_map/ppermute | solution.py:999
  50.8 11.9 %collective-permute-start.10 = (bf16[4,48,384]{2,1,0:T(8,128)(2,1)}, bf16[4,48,384]{2,1,0:T(8,128)(2,1)S(1)}, u32[]{:S(2)}, u32[]{:S(2)}) collective-permute-start(bf16[4,48,384]{2,1,0:T(8,128)(2,1)} %join_blocks.4.refs_4_.refs_0_), channel_id=1, source_target_pairs={{0,24},{1,25},{2,26},{3,27},{4,28},{5,29},{6,30},{7,31},{8,16},{9,... | collective-permute-start | bytes 442376 | tf_op jit(solution)/shard_map/ppermute | solution.py:999
  52.2 21.0 %collective-permute-start.9 = (bf16[4,48,384]{2,1,0:T(8,128)(2,1)}, bf16[4,48,384]{2,1,0:T(8,128)(2,1)S(1)}, u32[]{:S(2)}, u32[]{:S(2)}) collective-permute-start(bf16[4,48,384]{2,1,0:T(8,128)(2,1)} %join_blocks.4.refs_4_.refs_0_), channel_id=1, source_target_pairs={{0,16},{1,17},{2,18},{3,19},{4,20},{5,21},{6,22},{7,23},{8,24},{9,... | collective-permute-start | bytes 442376 | tf_op jit(solution)/shard_map/ppermute | solution.py:999
  52.2 21.0 %collective-permute-start.8 = (bf16[4,48,384]{2,1,0:T(8,128)(2,1)}, bf16[4,48,384]{2,1,0:T(8,128)(2,1)S(1)}, u32[]{:S(2)}, u32[]{:S(2)}) collective-permute-start(bf16[4,48,384]{2,1,0:T(8,128)(2,1)} %join_blocks.4.refs_4_.refs_0_), channel_id=1, source_target_pairs={{0,8},{1,9},{2,10},{3,11},{4,12},{5,13},{6,14},{7,15},{8,0},{9,1},... | collective-permute-start | bytes 442376 | tf_op jit(solution)/shard_map/ppermute | solution.py:999
  80.9 8.8 %collective-permute-start.11 = (bf16[16,96,384]{2,1,0:T(8,128)(2,1)}, bf16[16,96,384]{2,1,0:T(8,128)(2,1)S(1)}, u32[]{:S(2)}, u32[]{:S(2)}) collective-permute-start(bf16[16,96,384]{2,1,0:T(8,128)(2,1)} %join_blocks.7.rest_0_), channel_id=1, source_target_pairs={{0,2},{1,3},{2,0},{3,1},{4,6},{5,7},{6,4},{7,5},{8,10},{9,11},{10,... | collective-permute-start | bytes 3538952 | tf_op jit(solution)/shard_map/ppermute | solution.py:999
  83.7 4.6 collective-permute-start.2
  86.1 3.6 collective-permute-start.12
  108.0 104.1 %collective-permute-start.13 = (bf16[1024,768]{1,0:T(8,128)(2,1)}, bf16[1024,768]{1,0:T(8,128)(2,1)S(1)}, u32[]{:S(2)}, u32[]{:S(2)}) collective-permute-start(bf16[1024,768]{1,0:T(8,128)(2,1)} %get-tuple-element.63), channel_id=1, source_target_pairs={{0,1},{1,0},{2,3},{3,2},{4,5},{5,4},{6,7},{7,6},{8,9},{9,8},{10,11... | collective-permute-start | bytes 4718600 | tf_op jit(solution)/shard_map/ppermute | solution.py:933
  318.6 113.8 %collective-permute-start.14 = (bf16[1024,768]{1,0:T(8,128)(2,1)S(1)}, bf16[1024,768]{1,0:T(8,128)(2,1)S(1)}, u32[]{:S(2)}, u32[]{:S(2)}) collective-permute-start(bf16[1024,768]{1,0:T(8,128)(2,1)S(1)} %copy-done.35), channel_id=1, source_target_pairs={{1,0},{0,1},{3,2},{2,3},{5,4},{4,5},{7,6},{6,7},{9,8},{8,9},{11,10... | collective-permute-start | bytes 4718600 | tf_op jit(solution)/shard_map/ppermute | solution.py:933
  340.1 91.6 %collective-permute-start.15 = (bf16[16,768]{1,0:T(8,128)(2,1)S(1)}, bf16[16,768]{1,0:T(8,128)(2,1)S(1)}, u32[]{:S(2)}, u32[]{:S(2)}) collective-permute-start(bf16[16,768]{1,0:T(8,128)(2,1)S(1)} %copy-done.24), channel_id=1, source_target_pairs={{0,1},{1,0},{2,3},{3,2},{4,5},{5,4},{6,7},{7,6},{8,9},{9,8},{10,11... | collective-permute-start | bytes 73736 | tf_op jit(solution)/shard_map/ppermute | solution.py:963
  443.7 37.0 %collective-permute-start.16 = (bf16[1024,768]{1,0:T(8,128)(2,1)}, bf16[1024,768]{1,0:T(8,128)(2,1)S(1)}, u32[]{:S(2)}, u32[]{:S(2)}) collective-permute-start(bf16[1024,768]{1,0:T(8,128)(2,1)} %get-tuple-element.79.rest_3_), channel_id=1, source_target_pairs={{1,0},{0,1},{3,2},{2,3},{5,4},{4,5},{7,6},{6,7},{9,8},{8,9},{11,10... | collective-permute-start | bytes 4718600 | tf_op jit(solution)/shard_map/ppermute | solution.py:933
  498.5 4.2 collective-permute-start.17
  507.5 25.5 %collective-permute-start.18 = (bf16[4,160,384]{2,1,0:T(8,128)(2,1)}, bf16[4,160,384]{2,1,0:T(8,128)(2,1)S(1)}, u32[]{:S(2)}, u32[]{:S(2)}) collective-permute-start(bf16[4,160,384]{2,1,0:T(8,128)(2,1)} %get-tuple-element.86), channel_id=1, source_target_pairs={{0,1},{1,0},{2,3},{3,2},{4,5},{5,4},{6,7},{7,6},{8,9},{9,8},{10,11... | collective-permute-start | bytes 1474568 | tf_op jit(solution)/shard_map/ppermute | solution.py:999
  507.5 25.5 %collective-permute-start.19 = (bf16[4,160,384]{2,1,0:T(8,128)(2,1)}, bf16[4,160,384]{2,1,0:T(8,128)(2,1)S(1)}, u32[]{:S(2)}, u32[]{:S(2)}) collective-permute-start(bf16[4,160,384]{2,1,0:T(8,128)(2,1)} %get-tuple-element.87), channel_id=1, source_target_pairs={{0,4},{1,5},{2,6},{3,7},{4,0},{5,1},{6,2},{7,3},{8,12},{9,13},{10,... | collective-permute-start | bytes 1474568 | tf_op jit(solution)/shard_map/ppermute | solution.py:999
  507.5 27.6 %collective-permute-start.20 = (bf16[4,160,384]{2,1,0:T(8,128)(2,1)}, bf16[4,160,384]{2,1,0:T(8,128)(2,1)S(1)}, u32[]{:S(2)}, u32[]{:S(2)}) collective-permute-start(bf16[4,160,384]{2,1,0:T(8,128)(2,1)} %get-tuple-element.88), channel_id=1, source_target_pairs={{0,5},{1,4},{2,7},{3,6},{4,1},{5,0},{6,3},{7,2},{8,13},{9,12},{10,... | collective-permute-start | bytes 1474568 | tf_op jit(solution)/shard_map/ppermute | solution.py:999
  536.0 35.4 %copy-start.23 = (f32[16,384]{1,0:T(8,128)S(1)}, f32[16,384]{1,0:T(8,128)}, u32[]{:S(2)}) copy-start(f32[16,384]{1,0:T(8,128)} %get-tuple-element.91.refs_6_) | copy-start | bytes 73732
  538.4 34.3 %collective-permute-start.21 = (bf16[1,160,384]{2,1,0:T(8,128)(2,1)}, bf16[1,160,384]{2,1,0:T(8,128)(2,1)S(1)}, u32[]{:S(2)}, u32[]{:S(2)}) collective-permute-start(bf16[1,160,384]{2,1,0:T(8,128)(2,1)} %get-tuple-element.93), channel_id=1, source_target_pairs={{0,8},{1,9},{2,10},{3,11},{4,12},{5,13},{6,14},{7,15},{8,0},{9,1},... | collective-permute-start | bytes 368648 | tf_op jit(solution)/shard_map/ppermute | solution.py:999
  559.5 21.2 %collective-permute-start.22 = (bf16[1,160,384]{2,1,0:T(8,128)(2,1)}, bf16[1,160,384]{2,1,0:T(8,128)(2,1)S(1)}, u32[]{:S(2)}, u32[]{:S(2)}) collective-permute-start(bf16[1,160,384]{2,1,0:T(8,128)(2,1)} %get-tuple-element.94), channel_id=1, source_target_pairs={{0,16},{1,17},{2,18},{3,19},{4,20},{5,21},{6,22},{7,23},{8,24},{9,... | collective-permute-start | bytes 368648 | tf_op jit(solution)/shard_map/ppermute | solution.py:999
  571.4 9.3 %collective-permute-start.23 = (bf16[1,160,384]{2,1,0:T(8,128)(2,1)}, bf16[1,160,384]{2,1,0:T(8,128)(2,1)S(1)}, u32[]{:S(2)}, u32[]{:S(2)}) collective-permute-start(bf16[1,160,384]{2,1,0:T(8,128)(2,1)} %get-tuple-element.95), channel_id=1, source_target_pairs={{0,24},{1,25},{2,26},{3,27},{4,28},{5,29},{6,30},{7,31},{8,16},{9,... | collective-permute-start | bytes 368648 | tf_op jit(solution)/shard_map/ppermute | solution.py:999
  (30 other events, 229.0 us)
Sparse Core Ops, SparseCore 0:
  10.9 108.0 all-gather.2
  317.3 213.8 reduce-scatter.1
